TPU v7x, 32 devices: a whole 2x2x4 slice. The times are simulated.
32 devices in a mesh: dp: 4 (over z), cp: 8 (over y, x, core).
Axes of the slice: x: 2, y: 2, z: 4, core: 2. Of those that a mesh axis runs over, the one named last changes fastest.
Arguments:
- tokens: bfloat16 [4, 1024, 2048], P('dp', 'cp')
- cotangent: bfloat16 [4, 1024, 2048], P('dp', 'cp'), may hold values from -6 to 6
- lengths: int32 [4, 8], P('dp'), may hold values from 1 to 896, 1024 in all within a row
- big_weight: float32 [2048, 24576], P(('dp', 'cp'))
- big_first: float32 [2048, 24576], P(('dp', 'cp')), may hold values from -0.0005636108 to 0.0005636108
- big_second: float32 [2048, 24576], P(('dp', 'cp')), may hold values from 1.9853573e-08 to 7.941429e-08
- small_weight: float32 [2048, 18], P(('dp', 'cp'))
- small_first: float32 [2048, 18], P(('dp', 'cp')), may hold values from -0.0033816649 to 0.0033816649
- small_second: float32 [2048, 18], P(('dp', 'cp')), may hold values from 4.7648575e-07 to 7.623772e-06
- qk_gain: float32 [2, 128], replicated, may hold values from -0.06 to 0.06
- qk_first: float32 [2, 128], replicated, may hold values from -0.002818054 to 0.002818054
- qk_second: float32 [2, 128], replicated, may hold values from 1.5882858e-07 to 2.5412573e-06
Outputs:
- mixed: bfloat16 [4, 1024, 2048], P('dp', 'cp')
- grad_input: bfloat16 [4, 1024, 2048], P('dp', 'cp')
- big_first_new: float32 [2048, 24576], P(('dp', 'cp'))
- big_second_new: float32 [2048, 24576], P(('dp', 'cp'))
- big_new: float32 [2048, 24576], P(('dp', 'cp'))
- big_copy: bfloat16 [2048, 24576], P(('dp', 'cp'))
- small_first_new: float32 [2048, 18], P(('dp', 'cp'))
- small_second_new: float32 [2048, 18], P(('dp', 'cp'))
- small_new: float32 [2048, 18], P(('dp', 'cp'))
- small_copy: bfloat16 [2048, 18], P(('dp', 'cp'))
- qk_first_new: float32 [2, 128], replicated
- qk_second_new: float32 [2, 128], replicated
- qk_new: float32 [2, 128], replicated
- qk_copy: bfloat16 [2, 128], replicated
- gain_grads: float32 [2048, 2], P(('dp', 'cp'))
- grad_norm: float32 [], replicated
Inputs may be any that keep to these rules, and one draw needn't show every extreme that they name: Each row's 8 lengths are positive and sum to 1024.
All inputs are finite; a program needn't handle non-finite values.
Results may differ from a plain program's by a relative error of at most 0.025.
Values may be sent and summed in bfloat16 or wider, within the bound.
No kernel may reach another device: no remote copies, remote signals or barrier semaphores. Data moves between devices by JAX's collectives and lax.ppermute only.
A program may use at most 320 MiB of HBM per device.

v0:
```python
import math

import jax
import jax.numpy as jnp
from jax import lax
from jax.sharding import PartitionSpec as P

HEADS = 16
KV_HEADS = 8
HEAD_DIM = 128
FF = 6144
TOK_DEV = 128
STEP = 5


eps = 1e-06
theta = 1000000.0
beta_one = 0.5
beta_two = 0.5
rate = 0.02
decay = 0.1
adam_eps = 1e-08
contract_cols = (((1,), (1,)), ((), ()))
contract_rows = (((0,), (0,)), ((), ()))


def token_info(stored, doc_lengths, groups):
    half = TOK_DEV // 2
    device = stored // TOK_DEV
    within = stored % TOK_DEV
    section = jnp.where(within < half, device, 2 * groups - 1 - device)
    place = section * half + within % half
    ends = jnp.cumsum(doc_lengths)
    segment = jnp.sum((place[:, None] >= ends[None, :]).astype(jnp.int32), axis=1)
    starts = ends - doc_lengths
    picked = segment[:, None] == jnp.arange(doc_lengths.shape[0], dtype=jnp.int32)[None, :]
    begin = jnp.sum(jnp.where(picked, starts[None, :], 0), axis=1)
    return (place, segment, place - begin)


def rms(values):
    return values * lax.rsqrt(jnp.mean(values * values, axis=-1, keepdims=True) + eps)


def norm_back(values, grads):
    factor = lax.rsqrt(jnp.mean(values * values, axis=-1, keepdims=True) + eps)
    normed = values * factor
    return factor * (grads - normed * jnp.mean(grads * normed, axis=-1, keepdims=True))


def rotary(position):
    half = HEAD_DIM // 2
    freq = theta ** (-jnp.arange(half, dtype=jnp.float32) * 2.0 / HEAD_DIM)
    angle = position.astype(jnp.float32)[:, None] * freq[None, :]
    return (jnp.cos(angle), jnp.sin(angle))


def turn(values, cosine, sine):
    half = HEAD_DIM // 2
    first = values[..., :half]
    second = values[..., half:]
    cos_b = cosine[:, None, :]
    sin_b = sine[:, None, :]
    return jnp.concatenate(
        [first * cos_b - second * sin_b, second * cos_b + first * sin_b], axis=-1
    )


def turn_back(grads, cosine, sine):
    half = HEAD_DIM // 2
    first = grads[..., :half]
    second = grads[..., half:]
    cos_b = cosine[:, None, :]
    sin_b = sine[:, None, :]
    return jnp.concatenate(
        [first * cos_b + second * sin_b, second * cos_b - first * sin_b], axis=-1
    )


def adam(weight, first, second, grad):
    first_new = beta_one * first + (1.0 - beta_one) * grad
    second_new = beta_two * second + (1.0 - beta_two) * grad * grad
    fix_one = 1.0 - beta_one**STEP
    fix_two = 1.0 - beta_two**STEP
    weight_new = weight - rate * (
        first_new / fix_one / (jnp.sqrt(second_new / fix_two) + adam_eps) + decay * weight
    )
    return (first_new, second_new, weight_new, weight_new.astype(jnp.bfloat16))


def local(
    tokens,
    cotangent,
    lengths,
    big_weight,
    big_first,
    big_second,
    small_weight,
    small_first,
    small_second,
    qk_gain,
    qk_first,
    qk_second,
):
    groups = lax.axis_size("cp")
    owners = lax.axis_size("dp") * lax.axis_size("cp")
    width_attn = HEADS * HEAD_DIM
    width_kv = KV_HEADS * HEAD_DIM
    width_qkv = width_attn + 2 * width_kv
    width_in = width_qkv + HEADS
    start_mlp = width_qkv + width_attn
    start_down = start_mlp + 2 * FF
    share = HEADS // KV_HEADS
    factor_scale = HEAD_DIM ** (-0.5)
    rows = tokens.shape[1]
    weight_rows = big_weight.shape[0]
    row_group = math.gcd(weight_rows, 4)
    group_steps = weight_rows // row_group
    doc_lengths = lengths[0]
    own = lax.axis_index("cp") * rows + jnp.arange(rows, dtype=jnp.int32)
    place, segment, position = token_info(own, doc_lengths, groups)
    cosine, sine = rotary(position)
    query_gain = 1.0 + qk_gain[0]
    key_gain = 1.0 + qk_gain[1]
    attn_pack = jnp.concatenate(
        [big_weight[:, :width_qkv], small_weight[:, : HEADS + 1]], axis=1
    ).astype(jnp.bfloat16)
    mlp_pack = jnp.concatenate(
        [big_weight[:, start_mlp:start_down], small_weight[:, HEADS + 1 :]], axis=1
    ).astype(jnp.bfloat16)
    out_rows = big_weight[:, width_qkv:start_mlp].astype(jnp.bfloat16)
    down_rows = big_weight[:, start_down:].astype(jnp.bfloat16)
    inputs = tokens[0].astype(jnp.float32)
    normed_one = rms(inputs)
    attn_full, out_full = (
        lax.all_gather(attn_pack, ("dp", "cp"), axis=0, tiled=True),
        lax.all_gather(out_rows, ("dp", "cp"), axis=0, tiled=True),
    )
    gain_one = 1.0 + attn_full[:, width_in].astype(jnp.float32)
    kept_one = (normed_one * gain_one[None, :]).astype(jnp.bfloat16)
    proj = jnp.dot(kept_one, attn_full[:, :width_in], preferred_element_type=jnp.float32)
    q_part = proj[:, :width_attn].reshape(rows, HEADS, HEAD_DIM)
    k_part = proj[:, width_attn : width_attn + width_kv].reshape(rows, KV_HEADS, HEAD_DIM)
    v_part = proj[:, width_attn + width_kv : width_qkv]
    logits = proj[:, width_qkv:]
    q_hat = rms(q_part)
    k_hat = rms(k_part)
    queries = turn(q_hat * query_gain, cosine, sine).astype(jnp.bfloat16)
    keys = turn(k_hat * key_gain, cosine, sine).astype(jnp.bfloat16).reshape(rows, width_kv)
    values = v_part.astype(jnp.bfloat16)
    grouped = queries.reshape(rows, KV_HEADS, share, HEAD_DIM)
    attend_start = (
        jnp.full((KV_HEADS, share, rows), -1e30, jnp.float32),
        jnp.zeros((KV_HEADS, share, rows), jnp.float32),
        jnp.zeros((KV_HEADS, share, rows, HEAD_DIM), jnp.float32),
    )
    carry = attend_start
    key_piece = lax.all_gather(keys, "cp", axis=0, tiled=True)
    value_piece = lax.all_gather(values, "cp", axis=0, tiled=True)
    count = key_piece.shape[0]
    attend_block = math.gcd(count, 512)
    stored = jnp.arange(count, dtype=jnp.int32)
    key_place, key_segment, key_position = token_info(stored, doc_lengths, groups)
    items = (
        key_piece.reshape(count // attend_block, attend_block, KV_HEADS, HEAD_DIM),
        value_piece.reshape(count // attend_block, attend_block, KV_HEADS, HEAD_DIM),
        key_place.reshape(count // attend_block, attend_block),
        key_segment.reshape(count // attend_block, attend_block),
    )

    def step(state, item):
        top, total, accum = state
        key_block, value_block, place_block, segment_block = item
        scores = (
            jnp.einsum("qgrd,kgd->grqk", grouped, key_block, preferred_element_type=jnp.float32)
            * factor_scale
        )
        allowed = (segment_block[None, :] == segment[:, None]) & (
            place_block[None, :] <= place[:, None]
        )
        scores = jnp.where(allowed, scores, -1e30)
        new_top = jnp.maximum(top, jnp.max(scores, axis=-1))
        weights = jnp.where(allowed, jnp.exp(scores - new_top[..., None]), 0.0)
        shrink = jnp.exp(top - new_top)
        total = total * shrink + jnp.sum(weights, axis=-1)
        accum = accum * shrink[..., None] + jnp.einsum(
            "grqk,kgd->grqd",
            weights.astype(jnp.bfloat16),
            value_block,
            preferred_element_type=jnp.float32,
        )
        return ((new_top, total, accum), None)

    carry, unused = lax.scan(step, carry, items)
    top, total, accum = carry
    lse = top + jnp.log(total)
    heads = (accum / total[..., None]).transpose(2, 0, 1, 3).reshape(rows, HEADS, HEAD_DIM)
    sig = jax.nn.sigmoid(logits)
    gated = (heads * sig[:, :, None]).astype(jnp.bfloat16).reshape(rows, width_attn)
    middle = inputs + lax.dot_general(
        gated, out_full, contract_cols, preferred_element_type=jnp.float32
    )
    normed_two = rms(middle)
    mlp_full, down_full = (
        lax.all_gather(mlp_pack, ("dp", "cp"), axis=0, tiled=True),
        lax.all_gather(down_rows, ("dp", "cp"), axis=0, tiled=True),
    )
    gain_two = 1.0 + mlp_full[:, 2 * FF].astype(jnp.float32)
    kept_two = (normed_two * gain_two[None, :]).astype(jnp.bfloat16)
    gate_up = jnp.dot(kept_two, mlp_full[:, : 2 * FF], preferred_element_type=jnp.float32)
    gate = gate_up[:, :FF]
    upper = gate_up[:, FF:]
    sig_gate = jax.nn.sigmoid(gate)
    hidden = (gate * sig_gate * upper).astype(jnp.bfloat16)
    result = middle + lax.dot_general(
        hidden, down_full, contract_cols, preferred_element_type=jnp.float32
    )
    grad_out = cotangent[0].astype(jnp.float32)
    grad_branch = grad_out.astype(jnp.bfloat16)
    mlp_back, down_back = (
        lax.all_gather(mlp_pack, ("dp", "cp"), axis=0, tiled=True),
        lax.all_gather(down_rows, ("dp", "cp"), axis=0, tiled=True),
    )
    grad_hidden = jnp.dot(grad_branch, down_back, preferred_element_type=jnp.float32)
    grad_gate = grad_hidden * upper * sig_gate * (1.0 + gate * (1.0 - sig_gate))
    grad_upper = grad_hidden * gate * sig_gate
    grad_gu = jnp.concatenate([grad_gate, grad_upper], axis=1).astype(jnp.bfloat16)
    grad_two = lax.dot_general(
        grad_gu, mlp_back[:, : 2 * FF], contract_cols, preferred_element_type=jnp.float32
    )
    gain_two_term = jnp.sum(grad_two * normed_two, axis=0)

    def pick_cols(matrix, index):
        shaped = matrix.reshape(matrix.shape[0], owners, weight_rows)
        picked = lax.dynamic_slice_in_dim(shaped, index * row_group, row_group, 2)
        return picked.reshape(matrix.shape[0], owners * row_group)

    def pick_gain(vector, index):
        shaped = vector.reshape(owners, weight_rows)
        picked = lax.dynamic_slice_in_dim(shaped, index * row_group, row_group, 1)
        return picked.reshape(owners * row_group, 1)

    row_steps = jnp.arange(group_steps, dtype=jnp.int32)

    def mlp_term(index):
        part_in = lax.dot_general(
            pick_cols(kept_two, index), grad_gu, contract_rows, preferred_element_type=jnp.float32
        )
        part_down = lax.dot_general(
            pick_cols(grad_branch, index), hidden, contract_rows, preferred_element_type=jnp.float32
        )
        return jnp.concatenate([part_in, part_down, pick_gain(gain_two_term, index)], axis=1)

    grad_middle = grad_out + norm_back(middle, grad_two * gain_two[None, :])
    grad_attn_branch = grad_middle.astype(jnp.bfloat16)
    attn_back, out_back = (
        lax.all_gather(attn_pack, ("dp", "cp"), axis=0, tiled=True),
        lax.all_gather(out_rows, ("dp", "cp"), axis=0, tiled=True),
    )
    grad_gated = jnp.dot(grad_attn_branch, out_back, preferred_element_type=jnp.float32).reshape(
        rows, HEADS, HEAD_DIM
    )
    grad_sig = jnp.sum(grad_gated * heads, axis=-1)
    grad_logits = (grad_sig * sig * (1.0 - sig)).astype(jnp.bfloat16)
    grad_heads = (grad_gated * sig[:, :, None]).astype(jnp.bfloat16)
    delta = (
        jnp.sum(grad_heads.astype(jnp.float32) * heads, axis=-1)
        .reshape(rows, KV_HEADS, share)
        .transpose(1, 2, 0)
    )
    grouped_grad = grad_heads.reshape(rows, KV_HEADS, share, HEAD_DIM)
    all_keys, all_values = (
        lax.all_gather(keys, "cp", axis=0, tiled=True),
        lax.all_gather(values, "cp", axis=0, tiled=True),
    )
    length = all_keys.shape[0]
    block = math.gcd(length, 512)
    all_place, all_segment, all_position = token_info(
        jnp.arange(length, dtype=jnp.int32), doc_lengths, groups
    )
    back_items = (
        all_keys.reshape(length // block, block, KV_HEADS, HEAD_DIM),
        all_values.reshape(length // block, block, KV_HEADS, HEAD_DIM),
        all_place.reshape(length // block, block),
        all_segment.reshape(length // block, block),
    )

    def back_step(grad_query, item):
        key_block, value_block, place_block, segment_block = item
        scores = (
            jnp.einsum("qgrd,kgd->grqk", grouped, key_block, preferred_element_type=jnp.float32)
            * factor_scale
        )
        allowed = (segment_block[None, :] == segment[:, None]) & (
            place_block[None, :] <= place[:, None]
        )
        probs = jnp.where(allowed, jnp.exp(jnp.where(allowed, scores, -1e30) - lse[..., None]), 0.0)
        grad_probs = jnp.einsum(
            "qgrd,kgd->grqk", grouped_grad, value_block, preferred_element_type=jnp.float32
        )
        grad_scores = (probs * (grad_probs - delta[..., None])).astype(jnp.bfloat16)
        grad_query = grad_query + jnp.einsum(
            "grqk,kgd->qgrd", grad_scores, key_block, preferred_element_type=jnp.float32
        )
        grad_key = (
            jnp.einsum("grqk,qgrd->kgd", grad_scores, grouped, preferred_element_type=jnp.float32)
            * factor_scale
        )
        grad_value = jnp.einsum(
            "grqk,qgrd->kgd",
            probs.astype(jnp.bfloat16),
            grouped_grad,
            preferred_element_type=jnp.float32,
        )
        return (
            grad_query,
            jnp.concatenate(
                [grad_key.reshape(block, width_kv), grad_value.reshape(block, width_kv)], axis=1
            ),
        )

    grad_query, kv_terms = lax.scan(
        back_step, jnp.zeros((rows, KV_HEADS, share, HEAD_DIM), jnp.float32), back_items
    )
    kv_mine = lax.psum_scatter(
        kv_terms.reshape(length, 2 * width_kv).astype(jnp.bfloat16),
        "cp",
        scatter_dimension=0,
        tiled=True,
    ).astype(jnp.float32)
    grad_qn = turn_back((grad_query * factor_scale).reshape(rows, HEADS, HEAD_DIM), cosine, sine)
    grad_kn = turn_back(kv_mine[:, :width_kv].reshape(rows, KV_HEADS, HEAD_DIM), cosine, sine)
    q_gain_term = jnp.sum(grad_qn * q_hat, axis=(0, 1))
    k_gain_term = jnp.sum(grad_kn * k_hat, axis=(0, 1))
    grad_q_part = norm_back(q_part, grad_qn * query_gain).reshape(rows, width_attn)
    grad_k_part = norm_back(k_part, grad_kn * key_gain).reshape(rows, width_kv)
    grad_proj = jnp.concatenate(
        [grad_q_part, grad_k_part, kv_mine[:, width_kv:], grad_logits.astype(jnp.float32)], axis=1
    ).astype(jnp.bfloat16)
    grad_one = lax.dot_general(
        grad_proj, attn_back[:, :width_in], contract_cols, preferred_element_type=jnp.float32
    )
    gain_one_term = jnp.sum(grad_one * normed_one, axis=0)
    grad_input = grad_middle + norm_back(inputs, grad_one * gain_one[None, :])

    def attn_term(index):
        part_in = lax.dot_general(
            pick_cols(kept_one, index), grad_proj, contract_rows, preferred_element_type=jnp.float32
        )
        part_out = lax.dot_general(
            pick_cols(grad_attn_branch, index),
            gated,
            contract_rows,
            preferred_element_type=jnp.float32,
        )
        return jnp.concatenate([part_in, part_out, pick_gain(gain_one_term, index)], axis=1)

    attn_columns = width_in + width_attn + 1

    def both_step(carry, index):
        joined_term = jnp.concatenate([attn_term(index), mlp_term(index)], axis=1)
        return (carry, lax.psum_scatter(joined_term, ("dp", "cp"), scatter_dimension=0, tiled=True))

    unused, joined_stack = lax.scan(both_step, jnp.zeros((), jnp.int32), row_steps)
    joined = joined_stack.reshape(weight_rows, attn_columns + 3 * FF + 1)
    attn_grads = joined[:, :attn_columns]
    mlp_grads = joined[:, attn_columns:]
    big_grad = jnp.concatenate(
        [
            attn_grads[:, :width_qkv],
            attn_grads[:, width_in : width_in + width_attn],
            mlp_grads[:, : 3 * FF],
        ],
        axis=1,
    )
    small_grad = jnp.concatenate(
        [
            attn_grads[:, width_qkv:width_in],
            attn_grads[:, attn_columns - 1 :],
            mlp_grads[:, 3 * FF :],
        ],
        axis=1,
    )
    qk_term = jnp.stack([q_gain_term, k_gain_term])
    local_squares = jnp.sum(big_grad * big_grad) + jnp.sum(small_grad * small_grad)
    qk_grad, squares = lax.psum((qk_term, local_squares), ("dp", "cp"))
    norm_value = jnp.sqrt(squares + jnp.sum(qk_grad * qk_grad))
    factor = jnp.minimum(1.0, 1.0 / (norm_value + 1e-06))
    big_out = adam(big_weight, big_first, big_second, big_grad * factor)
    small_out = adam(small_weight, small_first, small_second, small_grad * factor)
    qk_out = adam(qk_gain, qk_first, qk_second, qk_grad * factor)
    gain_grads = small_grad[:, HEADS:] * factor
    return (
        result.astype(jnp.bfloat16)[None],
        grad_input.astype(jnp.bfloat16)[None],
        big_out[0],
        big_out[1],
        big_out[2],
        big_out[3],
        small_out[0],
        small_out[1],
        small_out[2],
        small_out[3],
        qk_out[0],
        qk_out[1],
        qk_out[2],
        qk_out[3],
        gain_grads,
        norm_value,
    )


def solution(mesh):
    placed = (
        P("dp", "cp", None),
        P("dp", "cp", None),
        P("dp", None),
        P(("dp", "cp"), None),
        P(("dp", "cp"), None),
        P(("dp", "cp"), None),
        P(("dp", "cp"), None),
        P(("dp", "cp"), None),
        P(("dp", "cp"), None),
        P(),
        P(),
        P(),
    )
    return jax.shard_map(
        local,
        mesh=mesh,
        in_specs=placed,
        out_specs=(
            P("dp", "cp", None),
            P("dp", "cp", None),
            P(("dp", "cp"), None),
            P(("dp", "cp"), None),
            P(("dp", "cp"), None),
            P(("dp", "cp"), None),
            P(("dp", "cp"), None),
            P(("dp", "cp"), None),
            P(("dp", "cp"), None),
            P(("dp", "cp"), None),
            P(),
            P(),
            P(),
            P(),
            P(("dp", "cp"), None),
            P(),
        ),
        check_vma=False,
    )
```

profile of v0, /device:TPU:0, one launch (start us, length us, event | category | flops | bytes accessed | tf_op | source)
XLA Modules:
  0.0 5145.1 jit_solution(10351089662373754595)
XLA Ops:
  14.1 119.4 %all-gather.7.cloned.1.call-done = bf16[2048,4113]{1,0:T(8,128)(2,1)} async-done(((bf16[64,4113]{1,0:T(8,128)(2,1)}), bf16[2048,4113]{1,0:T(8,128)(2,1)}) %all-gather.7.cloned.1.call-update) | async-done | bytes 16846864 | tf_op jit(solution)/shard_map/all_gather | solution.py:136
  178.7 26.2 all-gather.11.cloned.1.call-done
  215.6 21.3 while.39
  243.1 42.1 all-gather.13.cloned.1.call-done
  291.5 273.0 %all-gather.15.cloned.1.call-done = bf16[2048,12289]{1,0:T(8,128)(2,1)} async-done(((bf16[64,12289]{1,0:T(8,128)(2,1)}), bf16[2048,12289]{1,0:T(8,128)(2,1)}) %all-gather.15.cloned.1.call-update) | async-done | bytes 50335760 | tf_op jit(solution)/shard_map/all_gather | solution.py:205
  566.1 21.2 fusion.60
  587.3 132.8 %all-gather.17.cloned.1.call-done = bf16[2048,6144]{1,0:T(8,128)(2,1)} async-done(((bf16[64,6144]{1,0:T(8,128)(2,1)}), bf16[2048,6144]{1,0:T(8,128)(2,1)}) %all-gather.17.cloned.1.call-update) | async-done | bytes 25165840 | tf_op jit(solution)/shard_map/all_gather | solution.py:206
  735.1 24.0 multiply_reduce_fusion.1
  769.1 20.9 while.40
  809.7 36.1 reduce-scatter.4.cloned.1.call-done
  871.9 4167.7 %while.38 = (s32[]{:T(128)}, f32[16,4,24594]{2,1,0:T(4,128)}, bf16[128,2048]{0,1:T(8,128)(2,1)}, s32[16]{0:T(128)S(1)}, bf16[128,4112]{1,0:T(8,128)(2,1)}, /*ind...) while((s32[]{:T(128)}, f32[16,4,24594]{2,1,0:T(4,128)}, ...), condition=%wide.region_25.26_spmd, body=%wide.region_23.25_spmd.sunk | while | flops 808978688 | bytes 158722544 | solution.py:364
  882.8 15.9 concatenate.71
  898.8 232.2 %all-reduce.6.cloned.1.call-done = f32[128,24594]{1,0:T(8,128)} async-done(((f32[128,24594]{1,0:T(8,128)}), f32[128,24594]{1,0:T(8,128)}) %all-reduce.6.cloned.1.call-update) | async-done | bytes 12592144 | tf_op jit(solution)/shard_map/while
  1143.9 15.9 concatenate.71
  1159.8 231.7 %all-reduce.6.cloned.1.call-done = f32[128,24594]{1,0:T(8,128)} async-done(((f32[128,24594]{1,0:T(8,128)}), f32[128,24594]{1,0:T(8,128)}) %all-reduce.6.cloned.1.call-update) | async-done | bytes 12592144 | tf_op jit(solution)/shard_map/while
  1420.3 231.6 %all-reduce.6.cloned.1.call-done = f32[128,24594]{1,0:T(8,128)} async-done(((f32[128,24594]{1,0:T(8,128)}), f32[128,24594]{1,0:T(8,128)}) %all-reduce.6.cloned.1.call-update) | async-done | bytes 12592144 | tf_op jit(solution)/shard_map/while
  1664.8 15.9 concatenate.71
  1680.7 231.6 %all-reduce.6.cloned.1.call-done = f32[128,24594]{1,0:T(8,128)} async-done(((f32[128,24594]{1,0:T(8,128)}), f32[128,24594]{1,0:T(8,128)}) %all-reduce.6.cloned.1.call-update) | async-done | bytes 12592144 | tf_op jit(solution)/shard_map/while
  1941.2 231.6 %all-reduce.6.cloned.1.call-done = f32[128,24594]{1,0:T(8,128)} async-done(((f32[128,24594]{1,0:T(8,128)}), f32[128,24594]{1,0:T(8,128)}) %all-reduce.6.cloned.1.call-update) | async-done | bytes 12592144 | tf_op jit(solution)/shard_map/while
  2201.6 231.7 %all-reduce.6.cloned.1.call-done = f32[128,24594]{1,0:T(8,128)} async-done(((f32[128,24594]{1,0:T(8,128)}), f32[128,24594]{1,0:T(8,128)}) %all-reduce.6.cloned.1.call-update) | async-done | bytes 12592144 | tf_op jit(solution)/shard_map/while
  2462.1 231.6 %all-reduce.6.cloned.1.call-done = f32[128,24594]{1,0:T(8,128)} async-done(((f32[128,24594]{1,0:T(8,128)}), f32[128,24594]{1,0:T(8,128)}) %all-reduce.6.cloned.1.call-update) | async-done | bytes 12592144 | tf_op jit(solution)/shard_map/while
  2722.5 231.7 %all-reduce.6.cloned.1.call-done = f32[128,24594]{1,0:T(8,128)} async-done(((f32[128,24594]{1,0:T(8,128)}), f32[128,24594]{1,0:T(8,128)}) %all-reduce.6.cloned.1.call-update) | async-done | bytes 12592144 | tf_op jit(solution)/shard_map/while
  2983.0 231.6 %all-reduce.6.cloned.1.call-done = f32[128,24594]{1,0:T(8,128)} async-done(((f32[128,24594]{1,0:T(8,128)}), f32[128,24594]{1,0:T(8,128)}) %all-reduce.6.cloned.1.call-update) | async-done | bytes 12592144 | tf_op jit(solution)/shard_map/while
  3243.4 231.6 %all-reduce.6.cloned.1.call-done = f32[128,24594]{1,0:T(8,128)} async-done(((f32[128,24594]{1,0:T(8,128)}), f32[128,24594]{1,0:T(8,128)}) %all-reduce.6.cloned.1.call-update) | async-done | bytes 12592144 | tf_op jit(solution)/shard_map/while
  3503.8 231.7 %all-reduce.6.cloned.1.call-done = f32[128,24594]{1,0:T(8,128)} async-done(((f32[128,24594]{1,0:T(8,128)}), f32[128,24594]{1,0:T(8,128)}) %all-reduce.6.cloned.1.call-update) | async-done | bytes 12592144 | tf_op jit(solution)/shard_map/while
  3764.3 231.6 %all-reduce.6.cloned.1.call-done = f32[128,24594]{1,0:T(8,128)} async-done(((f32[128,24594]{1,0:T(8,128)}), f32[128,24594]{1,0:T(8,128)}) %all-reduce.6.cloned.1.call-update) | async-done | bytes 12592144 | tf_op jit(solution)/shard_map/while
  4024.7 231.6 %all-reduce.6.cloned.1.call-done = f32[128,24594]{1,0:T(8,128)} async-done(((f32[128,24594]{1,0:T(8,128)}), f32[128,24594]{1,0:T(8,128)}) %all-reduce.6.cloned.1.call-update) | async-done | bytes 12592144 | tf_op jit(solution)/shard_map/while
  4285.0 231.7 %all-reduce.6.cloned.1.call-done = f32[128,24594]{1,0:T(8,128)} async-done(((f32[128,24594]{1,0:T(8,128)}), f32[128,24594]{1,0:T(8,128)}) %all-reduce.6.cloned.1.call-update) | async-done | bytes 12592144 | tf_op jit(solution)/shard_map/while
  4545.5 231.7 %all-reduce.6.cloned.1.call-done = f32[128,24594]{1,0:T(8,128)} async-done(((f32[128,24594]{1,0:T(8,128)}), f32[128,24594]{1,0:T(8,128)}) %all-reduce.6.cloned.1.call-update) | async-done | bytes 12592144 | tf_op jit(solution)/shard_map/while
  4806.0 231.6 %all-reduce.6.cloned.1.call-done = f32[128,24594]{1,0:T(8,128)} async-done(((f32[128,24594]{1,0:T(8,128)}), f32[128,24594]{1,0:T(8,128)}) %all-reduce.6.cloned.1.call-update) | async-done | bytes 12592144 | tf_op jit(solution)/shard_map/while
  5074.9 39.5 all-reduce.1
  5118.3 17.4 fusion.119
  (716 shorter events, 627.7 us)
Async XLA Ops:
  7.2 126.2 %all-gather.7.cloned.1.call-start = ((), (), s32[]{:S(2)}) async-start(), calls=%async_computation.1 | async-start | bytes 17842176 | tf_op jit(solution)/shard_map/all_gather | solution.py:136
  13.1 161.7 %all-gather.9.cloned.1.call-start = ((), (), s32[]{:S(2)}) async-start(), calls=%async_computation.2 | async-start | bytes 2359296 | tf_op jit(solution)/shard_map/all_gather | solution.py:158
  148.6 56.3 %all-gather.11.cloned.1.call-start = ((), (), s32[]{:S(2)}) async-start(), calls=%async_computation.3 | async-start | bytes 2359296 | tf_op jit(solution)/shard_map/all_gather | solution.py:159
  149.4 135.7 %all-gather.13.cloned.1.call-start = ((), (), s32[]{:S(2)}) async-start(), calls=%async_computation.4 | async-start | bytes 8650752 | tf_op jit(solution)/shard_map/all_gather | solution.py:137
  151.1 413.4 %all-gather.15.cloned.1.call-start = ((), (), s32[]{:S(2)}) async-start(), calls=%async_computation.5 | async-start | bytes 52445184 | tf_op jit(solution)/shard_map/all_gather | solution.py:205
  156.7 563.4 %all-gather.17.cloned.1.call-start = ((), (), s32[]{:S(2)}) async-start(), calls=%async_computation.6 | async-start | bytes 25952256 | tf_op jit(solution)/shard_map/all_gather | solution.py:206
  158.9 687.0 %reduce-scatter.4.cloned.1.call-start = ((), (), s32[]{:S(2)}) async-start(), calls=%async_computation.7 | async-start | bytes 4718592
  291.5 467.7 %copy-start.7 = (f32[128,2048]{1,0:T(8,128)}, f32[128,2048]{1,0:T(8,128)S(1)}, u32[]{:S(2)}) copy-start(f32[128,2048]{1,0:T(8,128)S(1)} %get-tuple-element.616) | copy-start | bytes 3145732
  291.5 467.6 %copy-start.56 = (f32[128]{0:T(128)}, f32[128]{0:T(128)S(1)}, u32[]{:S(2)}) copy-start(f32[128]{0:T(128)S(1)} %add_rsqrt_fusion.2) | copy-start | bytes 1540
  871.9 259.1 %all-reduce.6.cloned.1.call-start = ((), (), s32[]{:S(2)}) async-start(), calls=%async_computation.8 | async-start | bytes 25296896 | tf_op jit(solution)/shard_map/while
  898.7 234.2 %copy-start.2 = (bf16[128,12288]{1,0:T(8,128)(2,1)S(1)}, bf16[128,12288]{1,0:T(8,128)(2,1)}, u32[]{:S(2)}) copy-start(bf16[128,12288]{1,0:T(8,128)(2,1)} %copy-done.1) | copy-start | bytes 9437188 | tf_op jit(solution)/shard_map/while
  1133.0 258.5 %all-reduce.6.cloned.1.call-start = ((), (), s32[]{:S(2)}) async-start(), calls=%async_computation.8 | async-start | bytes 25296896 | tf_op jit(solution)/shard_map/while
  1159.8 233.6 %copy-start.2 = (bf16[128,12288]{1,0:T(8,128)(2,1)S(1)}, bf16[128,12288]{1,0:T(8,128)(2,1)}, u32[]{:S(2)}) copy-start(bf16[128,12288]{1,0:T(8,128)(2,1)} %copy-done.1) | copy-start | bytes 9437188 | tf_op jit(solution)/shard_map/while
  1393.4 258.5 %all-reduce.6.cloned.1.call-start = ((), (), s32[]{:S(2)}) async-start(), calls=%async_computation.8 | async-start | bytes 25296896 | tf_op jit(solution)/shard_map/while
  1653.9 258.5 %all-reduce.6.cloned.1.call-start = ((), (), s32[]{:S(2)}) async-start(), calls=%async_computation.8 | async-start | bytes 25296896 | tf_op jit(solution)/shard_map/while
  1914.3 258.4 %all-reduce.6.cloned.1.call-start = ((), (), s32[]{:S(2)}) async-start(), calls=%async_computation.8 | async-start | bytes 25296896 | tf_op jit(solution)/shard_map/while
  2174.7 258.5 %all-reduce.6.cloned.1.call-start = ((), (), s32[]{:S(2)}) async-start(), calls=%async_computation.8 | async-start | bytes 25296896 | tf_op jit(solution)/shard_map/while
  2201.6 233.7 %copy-start.2 = (bf16[128,12288]{1,0:T(8,128)(2,1)S(1)}, bf16[128,12288]{1,0:T(8,128)(2,1)}, u32[]{:S(2)}) copy-start(bf16[128,12288]{1,0:T(8,128)(2,1)} %copy-done.1) | copy-start | bytes 9437188 | tf_op jit(solution)/shard_map/while
  2435.2 258.5 %all-reduce.6.cloned.1.call-start = ((), (), s32[]{:S(2)}) async-start(), calls=%async_computation.8 | async-start | bytes 25296896 | tf_op jit(solution)/shard_map/while
  2695.6 258.5 %all-reduce.6.cloned.1.call-start = ((), (), s32[]{:S(2)}) async-start(), calls=%async_computation.8 | async-start | bytes 25296896 | tf_op jit(solution)/shard_map/while
  2722.4 233.7 %copy-start.2 = (bf16[128,12288]{1,0:T(8,128)(2,1)S(1)}, bf16[128,12288]{1,0:T(8,128)(2,1)}, u32[]{:S(2)}) copy-start(bf16[128,12288]{1,0:T(8,128)(2,1)} %copy-done.1) | copy-start | bytes 9437188 | tf_op jit(solution)/shard_map/while
  2956.1 258.4 %all-reduce.6.cloned.1.call-start = ((), (), s32[]{:S(2)}) async-start(), calls=%async_computation.8 | async-start | bytes 25296896 | tf_op jit(solution)/shard_map/while
  3216.5 258.4 %all-reduce.6.cloned.1.call-start = ((), (), s32[]{:S(2)}) async-start(), calls=%async_computation.8 | async-start | bytes 25296896 | tf_op jit(solution)/shard_map/while
  3476.9 258.5 %all-reduce.6.cloned.1.call-start = ((), (), s32[]{:S(2)}) async-start(), calls=%async_computation.8 | async-start | bytes 25296896 | tf_op jit(solution)/shard_map/while
  3503.7 233.7 %copy-start.2 = (bf16[128,12288]{1,0:T(8,128)(2,1)S(1)}, bf16[128,12288]{1,0:T(8,128)(2,1)}, u32[]{:S(2)}) copy-start(bf16[128,12288]{1,0:T(8,128)(2,1)} %copy-done.1) | copy-start | bytes 9437188 | tf_op jit(solution)/shard_map/while
  3737.5 258.4 %all-reduce.6.cloned.1.call-start = ((), (), s32[]{:S(2)}) async-start(), calls=%async_computation.8 | async-start | bytes 25296896 | tf_op jit(solution)/shard_map/while
  3997.8 258.4 %all-reduce.6.cloned.1.call-start = ((), (), s32[]{:S(2)}) async-start(), calls=%async_computation.8 | async-start | bytes 25296896 | tf_op jit(solution)/shard_map/while
  4258.2 258.5 %all-reduce.6.cloned.1.call-start = ((), (), s32[]{:S(2)}) async-start(), calls=%async_computation.8 | async-start | bytes 25296896 | tf_op jit(solution)/shard_map/while
  4285.0 233.7 %copy-start.2 = (bf16[128,12288]{1,0:T(8,128)(2,1)S(1)}, bf16[128,12288]{1,0:T(8,128)(2,1)}, u32[]{:S(2)}) copy-start(bf16[128,12288]{1,0:T(8,128)(2,1)} %copy-done.1) | copy-start | bytes 9437188 | tf_op jit(solution)/shard_map/while
  4518.7 258.5 %all-reduce.6.cloned.1.call-start = ((), (), s32[]{:S(2)}) async-start(), calls=%async_computation.8 | async-start | bytes 25296896 | tf_op jit(solution)/shard_map/while
  4545.5 233.7 %copy-start.2 = (bf16[128,12288]{1,0:T(8,128)(2,1)S(1)}, bf16[128,12288]{1,0:T(8,128)(2,1)}, u32[]{:S(2)}) copy-start(bf16[128,12288]{1,0:T(8,128)(2,1)} %copy-done.1) | copy-start | bytes 9437188 | tf_op jit(solution)/shard_map/while
  4779.1 258.5 %all-reduce.6.cloned.1.call-start = ((), (), s32[]{:S(2)}) async-start(), calls=%async_computation.8 | async-start | bytes 25296896 | tf_op jit(solution)/shard_map/while
  (137 other events, 4178.1 us)
Sparse Core Ops, SparseCore 0:
  13.2 120.1 all-gather.6
  148.7 26.0 all-gather.8
  176.7 28.1 all-gather.10
  207.6 77.4 all-gather.12
  287.8 276.6 all-gather.14
  567.2 152.7 all-gather.16
  796.3 49.5 reduce-scatter.3
  898.9 232.0 all-reduce.5
  1159.9 231.5 all-reduce.5
  1420.4 231.4 all-reduce.5
  1680.8 231.4 all-reduce.5
  1941.3 231.4 all-reduce.5
  2201.7 231.5 all-reduce.5
  2462.2 231.4 all-reduce.5
  2722.6 231.5 all-reduce.5
  2983.1 231.4 all-reduce.5
  3243.5 231.4 all-reduce.5
  3503.9 231.5 all-reduce.5
  3764.4 231.3 all-reduce.5
  4024.8 231.3 all-reduce.5
  4285.2 231.5 all-reduce.5
  4545.6 231.5 all-reduce.5
  4806.1 231.4 all-reduce.5
where the time goes:
time: 5160 us; the launch traced here: 5150 us
  waiting for transfers between devices  4350 us (84%)
  local copies, waits for them, and re-layouts  402 us (8%)
  matrix products  256 us (5%)
  other arithmetic  64.5 us (1%)
    while x32, waiting for transfers between devices  3710 us
    all_gather x1, waiting for transfers between devices, local(): lax.all_gather(mlp_pack, ('dp', 'cp'), axis=0, tiled=True)  273 us
    concatenate x16, local copies, waits for them, and re-layouts, both_step(): joined_term = jnp.concatenate([attn_term(index), mlp_term(index)], axis=1)  255 us
    all_gather x1, waiting for transfers between devices, local(): lax.all_gather(down_rows, ('dp', 'cp'), axis=0, tiled=True)  133 us
    all_gather x1, waiting for transfers between devices, local(): lax.all_gather(attn_pack, ('dp', 'cp'), axis=0, tiled=True)  119 us
  transfers between devices with their start and end apart: 23, of which 23 were waited for; matrix products, arithmetic and copies ran while one was open for 2% of the time, Pallas kernels for 0%

commit v1 on v0

v1 whole, which is shorter than its diff:
```python
import jax
import jax.numpy as jnp
from jax import lax
from jax.sharding import PartitionSpec as P

HEADS = 16
KV_HEADS = 8
HEAD_DIM = 128
FF = 6144
TOK_DEV = 128
STEP = 5

eps = 1e-06
theta = 1000000.0
beta_one = 0.5
beta_two = 0.5
rate = 0.02
decay = 0.1
adam_eps = 1e-08
contract_cols = (((1,), (1,)), ((), ()))
contract_rows = (((0,), (0,)), ((), ()))
f32 = jnp.float32
bf16 = jnp.bfloat16


def dot(a, b):
    return jnp.dot(a, b, preferred_element_type=f32)


def dot_nt(a, b):
    return lax.dot_general(a, b, contract_cols, preferred_element_type=f32)


def dot_tn(a, b):
    return lax.dot_general(a, b, contract_rows, preferred_element_type=f32)


def token_info(stored, doc_lengths, groups):
    half = TOK_DEV // 2
    device = stored // TOK_DEV
    within = stored % TOK_DEV
    section = jnp.where(within < half, device, 2 * groups - 1 - device)
    place = section * half + within % half
    ends = jnp.cumsum(doc_lengths)
    segment = jnp.sum((place[:, None] >= ends[None, :]).astype(jnp.int32), axis=1)
    starts = ends - doc_lengths
    picked = segment[:, None] == jnp.arange(doc_lengths.shape[0], dtype=jnp.int32)[None, :]
    begin = jnp.sum(jnp.where(picked, starts[None, :], 0), axis=1)
    return (place, segment, place - begin)


def rms_factor(values):
    return lax.rsqrt(jnp.mean(values * values, axis=-1, keepdims=True) + eps)


def rms(values):
    return values * rms_factor(values)


def norm_back(values, grads):
    factor = rms_factor(values)
    normed = values * factor
    return factor * (grads - normed * jnp.mean(grads * normed, axis=-1, keepdims=True))


def rotary(position):
    half = HEAD_DIM // 2
    freq = theta ** (-jnp.arange(half, dtype=f32) * 2.0 / HEAD_DIM)
    angle = position.astype(f32)[:, None] * freq[None, :]
    cosine, sine = jnp.cos(angle), jnp.sin(angle)
    return (
        jnp.concatenate([cosine, cosine], axis=1),
        jnp.concatenate([-sine, sine], axis=1),
    )


def swap_halves(values):
    half = HEAD_DIM // 2
    return jnp.concatenate([values[:, half:], values[:, :half]], axis=1)


def turn(values, cosine, sine):
    return values * cosine + swap_halves(values) * sine


def turn_back(grads, cosine, sine):
    return grads * cosine - swap_halves(grads) * sine


def adam(weight, first, second, grad):
    first_new = beta_one * first + (1.0 - beta_one) * grad
    second_new = beta_two * second + (1.0 - beta_two) * grad * grad
    fix_one = 1.0 - beta_one**STEP
    fix_two = 1.0 - beta_two**STEP
    weight_new = weight - rate * (
        first_new / fix_one / (jnp.sqrt(second_new / fix_two) + adam_eps) + decay * weight
    )
    return (first_new, second_new, weight_new, weight_new.astype(bf16))


def swap(value, axes, size, bit):
    return lax.ppermute(value, axes, [(i, i ^ (1 << bit)) for i in range(size)])


def cp_offsets(groups):
    bits = groups.bit_length() - 1
    order = [0] + list(range(bits - 1, 0, -1))
    offsets = [0]
    for bit in reversed(order):
        offsets = offsets + [o | (1 << bit) for o in offsets]
    return offsets


def gather_cp(value, groups):
    bits = groups.bit_length() - 1
    rows, columns = value.shape
    longs = list(range(1, bits))
    parts = []
    for reverse in (False, True):
        part = value[:, columns // 2 :] if reverse else value[:, : columns // 2]
        part = part.reshape((1,) * len(longs) + part.shape)
        for bit in reversed(longs) if reverse else longs:
            axis = len(longs) - bit
            part = jnp.concatenate([part, swap(part, "cp", groups, bit)], axis=axis)
        parts.append(part.reshape(-1, columns // 2))
    joined = jnp.concatenate(parts, axis=1)
    return jnp.concatenate([joined, swap(joined, "cp", groups, 0)], axis=0)


def scatter_cp(value, groups):
    bits = groups.bit_length() - 1
    total, columns = value.shape
    half = total // 2
    kept = value[:half] + swap(value[half:].astype(bf16), "cp", groups, 0).astype(f32)
    longs = list(range(1, bits))
    parts = []
    for reverse in (False, True):
        part = kept[:, columns // 2 :] if reverse else kept[:, : columns // 2]
        part = part.reshape((2,) * len(longs) + (total // groups, columns // 2))
        for bit in reversed(longs) if reverse else longs:
            axis = len(longs) - bit
            stays = lax.slice_in_dim(part, 0, 1, axis=axis)
            leaves = lax.slice_in_dim(part, 1, 2, axis=axis).astype(bf16)
            part = stays + swap(leaves, "cp", groups, bit).astype(f32)
        parts.append(part.reshape(-1, columns // 2))
    return jnp.concatenate(parts, axis=1)


def sum_all(value, count):
    axes = ("dp", "cp")
    for bit in range(count.bit_length() - 1):
        value = value + swap(value, axes, count, bit)
    return value


def local(
    tokens,
    cotangent,
    lengths,
    big_weight,
    big_first,
    big_second,
    small_weight,
    small_first,
    small_second,
    qk_gain,
    qk_first,
    qk_second,
):
    groups = lax.axis_size("cp")
    planes = lax.axis_size("dp")
    me = lax.axis_index("cp")
    owner = lax.axis_index("dp") * groups + me
    wr = big_weight.shape[0]
    features = tokens.shape[2]
    rows = tokens.shape[1]
    width_attn = HEADS * HEAD_DIM
    width_kv = KV_HEADS * HEAD_DIM
    width_qkv = width_attn + 2 * width_kv
    start_mlp = width_qkv + width_attn
    start_down = start_mlp + 2 * FF
    own_q = HEADS // groups
    own_kv = max(1, KV_HEADS // groups)
    copies = max(1, groups // KV_HEADS)
    share = own_q // own_kv
    wq = own_q * HEAD_DIM
    wkv = own_kv * HEAD_DIM
    wff = FF // groups
    scale = HEAD_DIM ** (-0.5)

    def blocks(start, width, repeat=1):
        part = big_weight[:, start : start + width].astype(bf16)
        part = part.reshape(wr, groups // repeat, -1).transpose(1, 0, 2)
        return jnp.repeat(part, repeat, axis=0) if repeat > 1 else part

    def to_columns(part):
        part = lax.all_to_all(part, "cp", 0, 0, tiled=True).reshape(groups * wr, -1)
        return lax.all_gather(part, "dp", axis=0, tiled=True)

    small_parts = lax.all_gather(small_weight.astype(bf16).T, ("dp", "cp"), axis=0)
    small_full = small_parts.transpose(1, 0, 2).reshape(HEADS + 2, features)
    attn_w = to_columns(
        jnp.concatenate(
            [
                blocks(0, width_attn),
                blocks(width_attn, width_kv, copies),
                blocks(width_attn + width_kv, width_kv, copies),
                blocks(width_qkv, width_attn),
            ],
            axis=2,
        )
    )
    gu_w = to_columns(
        jnp.concatenate([blocks(start_mlp, FF), blocks(start_mlp + FF, FF)], axis=2)
    )
    down_w = to_columns(blocks(start_down, FF))
    win = wq + 2 * wkv
    out_w = attn_w[:, win:]
    gate_w = lax.dynamic_slice_in_dim(small_full, me * own_q, own_q, 0).T
    in_w = jnp.concatenate([attn_w[:, :win], gate_w], axis=1)
    gain_one = 1.0 + small_full[HEADS].astype(f32)
    gain_two = 1.0 + small_full[HEADS + 1].astype(f32)

    doc_lengths = lengths[0]
    offsets = jnp.array(cp_offsets(groups), jnp.int32)
    stored = ((me ^ offsets)[:, None] * rows + jnp.arange(rows, dtype=jnp.int32)).reshape(-1)
    place, segment, position = token_info(stored, doc_lengths, groups)
    cosine, sine = rotary(position)
    allowed = (segment[:, None] == segment[None, :]) & (place[None, :] <= place[:, None])
    query_gain = 1.0 + qk_gain[0]
    key_gain = 1.0 + qk_gain[1]

    tokens_all = gather_cp(tokens[0], groups).astype(f32)
    kept_one = (rms(tokens_all) * gain_one).astype(bf16)
    grad_branch = gather_cp(cotangent[0], groups)

    proj = dot(kept_one, in_w)
    sig = jax.nn.sigmoid(proj[:, win:])

    def head(matrix, index):
        return matrix[:, index * HEAD_DIM : (index + 1) * HEAD_DIM]

    q_part = [head(proj, h) for h in range(own_q)]
    k_part = [head(proj, own_q + g) for g in range(own_kv)]
    values = [head(proj, own_q + own_kv + g).astype(bf16) for g in range(own_kv)]
    queries = [turn(rms(q) * query_gain, cosine, sine).astype(bf16) for q in q_part]
    keys = [turn(rms(k) * key_gain, cosine, sine).astype(bf16) for k in k_part]
    probs, heads = [], []
    for h in range(own_q):
        g = h // share
        scores = jnp.where(allowed, dot_nt(queries[h], keys[g]) * scale, -1e30)
        weights = jnp.where(allowed, jnp.exp(scores - jnp.max(scores, axis=-1, keepdims=True)), 0.0)
        prob = (weights / jnp.sum(weights, axis=-1, keepdims=True)).astype(bf16)
        probs.append(prob)
        heads.append(dot(prob, values[g]))
    gated = jnp.concatenate(
        [(heads[h] * sig[:, h : h + 1]).astype(bf16) for h in range(own_q)], axis=1
    )
    inputs = tokens[0].astype(f32)
    middle = inputs + scatter_cp(dot_nt(gated, out_w), groups)

    normed_two = rms(middle)
    kept_two = gather_cp((normed_two * gain_two).astype(bf16), groups)
    gate = dot(kept_two, gu_w[:, :wff])
    upper = dot(kept_two, gu_w[:, wff:])
    sig_gate = jax.nn.sigmoid(gate)
    hidden = (gate * sig_gate * upper).astype(bf16)

    def to_rows(part):
        part = lax.psum_scatter(part.astype(bf16), "dp", scatter_dimension=0, tiled=True)
        return part

    down_term = to_rows(dot_tn(grad_branch, hidden))
    grad_hidden = dot(grad_branch, down_w)
    grad_gate = grad_hidden * upper * sig_gate * (1.0 + gate * (1.0 - sig_gate))
    grad_upper = grad_hidden * gate * sig_gate
    grad_gu = jnp.concatenate([grad_gate, grad_upper], axis=1).astype(bf16)
    grad_two = scatter_cp(dot_nt(grad_gu, gu_w), groups)
    gu_term = to_rows(dot_tn(kept_two, grad_gu))
    gain_two_term = jnp.sum(grad_two * normed_two, axis=0)
    grad_out = cotangent[0].astype(f32)
    grad_middle = grad_out + norm_back(middle, grad_two * gain_two)
    result = middle + scatter_cp(dot_nt(hidden, down_w), groups)

    grad_attn_branch = gather_cp(grad_middle.astype(bf16), groups)
    grad_gated = dot(grad_attn_branch, out_w)
    grad_q, grad_logits = [], []
    grad_k = [0.0] * own_kv
    grad_v = [0.0] * own_kv
    q_gain_term = jnp.zeros((HEAD_DIM,), f32)
    k_gain_term = jnp.zeros((HEAD_DIM,), f32)
    for h in range(own_q):
        g = h // share
        sig_h = sig[:, h : h + 1]
        back = head(grad_gated, h)
        grad_sig = jnp.sum(back * heads[h], axis=-1, keepdims=True)
        grad_logits.append((grad_sig * sig_h * (1.0 - sig_h)).astype(bf16))
        grad_head = (back * sig_h).astype(bf16)
        delta = jnp.sum(grad_head.astype(f32) * heads[h], axis=-1, keepdims=True)
        grad_probs = dot_nt(grad_head, values[g])
        grad_scores = (probs[h].astype(f32) * (grad_probs - delta)).astype(bf16)
        grad_qn = turn_back(dot(grad_scores, keys[g]) * scale, cosine, sine)
        q_gain_term = q_gain_term + jnp.sum(grad_qn * rms(q_part[h]), axis=0)
        grad_q.append(norm_back(q_part[h], grad_qn * query_gain).astype(bf16))
        grad_k[g] = grad_k[g] + dot_tn(grad_scores, queries[h])
        grad_v[g] = grad_v[g] + dot_tn(probs[h], grad_head)
    grad_keys = []
    for g in range(own_kv):
        grad_kn = turn_back(grad_k[g] * scale, cosine, sine)
        k_gain_term = k_gain_term + jnp.sum(grad_kn * rms(k_part[g]), axis=0)
        grad_keys.append(norm_back(k_part[g], grad_kn * key_gain).astype(bf16))
    grad_proj = jnp.concatenate(
        grad_q + grad_keys + [v.astype(bf16) for v in grad_v] + grad_logits, axis=1
    )
    in_grad = dot_tn(kept_one, grad_proj)
    attn_term = to_rows(
        jnp.concatenate([in_grad[:, :win], dot_tn(grad_attn_branch, gated)], axis=1)
    )
    grad_one = scatter_cp(dot_nt(grad_proj, in_w), groups)
    gain_one_term = jnp.sum(grad_one * rms(inputs), axis=0)
    grad_input = grad_middle + norm_back(inputs, grad_one * gain_one)

    gate_term = lax.dynamic_update_slice_in_dim(
        jnp.zeros((HEADS, features), f32), in_grad[:, win:].T, me * own_q, 0
    )
    first_small = sum_all(
        jnp.concatenate([gate_term, gain_two_term[None]], axis=0).reshape(-1, 128),
        planes * groups,
    ).reshape(HEADS + 1, features)
    def squares_of(value):
        value = value.astype(f32)
        return jnp.sum(value * value)

    unit = win + wq

    def kv_sum(part):
        if copies == 1:
            return part
        return part.astype(f32).reshape(groups // copies, copies, wr, -1).sum(axis=1)

    def to_owner(part):
        return lax.all_to_all(part.reshape(groups, wr, -1), "cp", 0, 0, tiled=True)

    def wide(part):
        return part.transpose(1, 0, 2).reshape(wr, -1).astype(f32)

    down_own = to_owner(down_term)
    gu_own = to_owner(gu_term)
    attn_own = to_owner(attn_term)
    k_own = kv_sum(attn_own[:, :, wq : wq + wkv])
    v_own = kv_sum(attn_own[:, :, wq + wkv : win])
    if copies == 1:
        attn_squares = squares_of(attn_term)
    else:
        attn_squares = (
            squares_of(attn_term[:, :wq]) + squares_of(attn_term[:, win:])
            + squares_of(k_own) + squares_of(v_own)
        )
    local_squares = squares_of(down_term) + squares_of(gu_term) + attn_squares
    last_small = sum_all(
        jnp.concatenate(
            [
                gain_one_term.reshape(-1, 128),
                q_gain_term[None],
                k_gain_term[None],
                jnp.full((1, 128), local_squares, f32),
            ],
            axis=0,
        ),
        planes * groups,
    )
    tall = features // 128
    gain_one_grad = last_small[:tall].reshape(1, features)
    qk_grad = last_small[tall : tall + 2]
    small_all = jnp.concatenate([first_small[:HEADS], gain_one_grad, first_small[HEADS:]], axis=0)
    total = (
        last_small[tall + 2, 0] + jnp.sum(small_all * small_all) + jnp.sum(qk_grad * qk_grad)
    )
    norm_value = jnp.sqrt(total)
    factor = jnp.minimum(1.0, 1.0 / (norm_value + 1e-06))
    small_grad = lax.dynamic_slice_in_dim(small_all, owner * wr, wr, 1).T
    big_grad = jnp.concatenate(
        [
            wide(attn_own[:, :, :wq]),
            wide(k_own),
            wide(v_own),
            wide(attn_own[:, :, win:unit]),
            wide(gu_own[:, :, :wff]),
            wide(gu_own[:, :, wff:]),
            wide(down_own),
        ],
        axis=1,
    )
    big_out = adam(big_weight, big_first, big_second, big_grad * factor)
    small_out = adam(small_weight, small_first, small_second, small_grad * factor)
    qk_out = adam(qk_gain, qk_first, qk_second, qk_grad * factor)
    gain_grads = small_grad[:, HEADS:] * factor
    return (
        result.astype(bf16)[None],
        grad_input.astype(bf16)[None],
        *big_out,
        *small_out,
        *qk_out,
        gain_grads,
        norm_value,
    )


def solution(mesh):
    rows = P(("dp", "cp"), None)
    row_tokens = P("dp", "cp", None)
    return jax.shard_map(
        local,
        mesh=mesh,
        in_specs=(row_tokens, row_tokens, P("dp", None)) + (rows,) * 6 + (P(),) * 3,
        out_specs=(row_tokens, row_tokens) + (rows,) * 8 + (P(),) * 4 + (rows, P()),
        check_vma=False,
    )
```

time: 5160 us -> 730 us (0.14)
  waiting for transfers between devices: 4350 us -> 301 us
  local copies, waits for them, and re-layouts: 402 us -> 65.2 us
  matrix products: 256 us -> 99.3 us
  starting transfers between devices: 0.58 us -> 77.6 us
    while x32 -> x0, waiting for transfers between devices: 3710 us -> none
    all_gather x6 -> x3, waiting for transfers between devices: 607 us -> 52.4 us  [to_columns(): return lax.all_gather(part, 'dp', axis=0, tiled=True)]
    concatenate x16 -> x5, local copies, waits for them, and re-layouts: 255 us -> 8.11 us  [the longest x1 4.49 us: local(): jnp.concatenate(grad_q + grad_keys + [v.astype(bf16) for v in grad_v] + g...]
    dot_general x86 -> x25, matrix products: 256 us -> 99.3 us  [the longest x9 43.3 us: dot(): return jnp.dot(a, b, preferred_element_type=f32)]
    ppermute x0 -> x50, waiting for transfers between devices: none -> 108 us  [swap(): return lax.ppermute(value, axes, [(i, i ^ 1 << bit) for i in range(size)])]
    reduce_scatter x0 -> x3, waiting for transfers between devices: none -> 108 us  [to_rows(): lax.psum_scatter(part.astype(bf16), 'dp', scatter_dimension=0, tiled=True)]
    ppermute x0 -> x50, starting transfers between devices: none -> 52.4 us  [swap(): return lax.ppermute(value, axes, [(i, i ^ 1 << bit) for i in range(size)])]
  transfers between devices with their start and end apart: 23 -> 62, of which waited for: 23 -> 28; matrix products, arithmetic and copies ran while one was open for 2% -> 27% of each run, Pallas kernels for 0% -> 0%
where the time goes in v1:
time: 730 us; the launch traced here: 723 us
  waiting for transfers between devices  301 us (41%)
  other arithmetic  111 us (15%)
  matrix products  99.3 us (14%)
  starting transfers between devices  77.6 us (11%)
  local copies, waits for them, and re-layouts  65.2 us (9%)
  blocking collectives  47.8 us (7%)
  between operations  21.5 us (3%)
    ppermute x50, waiting for transfers between devices, swap(): return lax.ppermute(value, axes, [(i, i ^ 1 << bit) for i in range(size)])  108 us
    reduce_scatter x3, waiting for transfers between devices, to_rows(): lax.psum_scatter(part.astype(bf16), 'dp', scatter_dimension=0, tiled=True)  108 us
    all_gather x3, waiting for transfers between devices, to_columns(): return lax.all_gather(part, 'dp', axis=0, tiled=True)  52.4 us
    ppermute x50, starting transfers between devices, swap(): return lax.ppermute(value, axes, [(i, i ^ 1 << bit) for i in range(size)])  52.4 us
    all_gather x1, blocking collectives, local(): lax.all_gather(small_weight.astype(bf16).T, ('dp', 'cp'), axis=0)  47.8 us
    dot_general x9, matrix products, dot(): return jnp.dot(a, b, preferred_element_type=f32)  43.3 us
    dot_general x8, matrix products, dot_tn(): return lax.dot_general(a, b, contract_rows, preferred_element_type=f32)  30.2 us
    unnamed x179, local copies, waits for them, and re-layouts  26.4 us
  transfers between devices with their start and end apart: 62, of which 28 were waited for; matrix products, arithmetic and copies ran while one was open for 27% of the time, Pallas kernels for 0%

profile of v1, /device:TPU:0, one launch (start us, length us, event | category | flops | bytes accessed | tf_op | source)
XLA Modules:
  0.0 723.1 jit_solution(5091429047745839522)
XLA Ops:
  13.3 5.2 all-to-all-start
  22.0 9.5 %all-to-all-done = bf16[8,64,768]{2,1,0:T(8,128)(2,1)S(1)} async-done(((bf16[8,64,768]{2,1,0:T(8,128)(2,1)}), bf16[8,64,768]{2,1,0:T(8,128)(2,1)S(1)}, u32[]{:S(2)}, u32[]{:S(2)}) %all-to-all-start) | async-done | bytes 786464 | tf_op jit(solution)/shard_map/all_to_all | solution.py:197
  42.6 4.2 all-to-all-start.2
  47.0 47.8 %all-gather.1 = bf16[32,18,64]{2,1,0:T(8,128)(2,1)S(1)} all-gather(bf16[1,18,64]{2,1,0:T(8,128)(2,1)S(1)} %convert_bitcast_fusion), channel_id=2, replica_groups=mesh['dp'=4,'cp'=8] {'dp','cp'}, dimensions={0}, use_global_device_ids=true | all-gather | bytes 76032 | tf_op jit(solution)/shard_map/all_gather | solution.py:200
  104.6 4.3 all-to-all-start.1
  110.1 9.2 %fusion = f32[1024]{0:T(1024)S(1)} fusion(bf16[512,2048]{1,0:T(8,128)(2,1)} %collective-permute-done.4, bf16[512,1024]{1,0:T(8,128)(2,1)S(1)} %bitcast.257, bf16[512,1024]{1,0:T(8,128)(2,1)S(1)} %bitcast.253), kind=kLoop, calls=%fused_computation.4 | loop fusion | flops 16776192 | bytes 4198400 | tf_op jit(solution)/shard_map/reduce_sum | solution.py:53
  121.3 5.0 fusion.16
  130.7 14.0 %divide_convert_fusion.1 = (bf16[1024,1024]{0,1:T(8,128)(2,1)S(1)}, f32[1024]{0:T(1024)S(1)}) fusion(f32[1024,1024]{0,1:T(8,128)S(1)} %get-tuple-element.132, f32[1024]{0:T(1024)S(1)} %get-tuple-element.40, f32[1024]{0:T(1024)S(1)} %get-tuple-element.131, s32[1024]{0:T(1024)S(1)} %fusion.79, s32[1024]{0:T(1024)S(1)} %convert_reduce_fusion, ...), kind=kLoop, calls=%fused_computation.29 | loop fusion | flops 14679040 | bytes 10510336 | tf_op jit(solution)/shard_map/convert_element_type | solution.py:253
  173.5 4.5 collective-permute-done.20
  184.2 5.1 collective-permute-done.6
  195.1 7.6 %collective-permute-done.7 = bf16[1,1,128,1024]{3,2,1,0:T(8,128)(2,1)S(1)} collective-permute-done((bf16[1,1,128,1024]{3,2,1,0:T(8,128)(2,1)S(1)}, bf16[1,1,128,1024]{3,2,1,0:T(8,128)(2,1)S(1)}, u32[]{:S(2)}, u32[]{:S(2)}) %collective-permute-start.7) | collective-permute-done | bytes 262176 | tf_op jit(solution)/shard_map/ppermute | solution.py:102
  215.5 10.1 %collective-permute-done.11 = bf16[1,2,128,1024]{3,2,1,0:T(8,128)(2,1)S(1)} collective-permute-done((bf16[1,2,128,1024]{3,2,1,0:T(8,128)(2,1)S(1)}, bf16[1,2,128,1024]{3,2,1,0:T(8,128)(2,1)S(1)}, u32[]{:S(2)}, u32[]{:S(2)}) %collective-permute-start.11) | collective-permute-done | bytes 524320 | tf_op jit(solution)/shard_map/ppermute | solution.py:102
  228.4 8.3 %fusion.13 = f32[1024,768]{0,1:T(8,128)} fusion(bf16[2048,768]{1,0:T(8,128)(2,1)} %all-gather.10.cloned.1.call-done, bf16[512,2048]{1,0:T(8,128)(2,1)} %collective-permute-done.24, bf16[512,1024]{1,0:T(8,128)(2,1)} %bitcast.285, bf16[512,1024]{1,0:T(8,128)(2,1)} %bitcast.282), kind=kOutput, calls=%fused_computation.56 | convolution fusion | flops 3233808384 | bytes 10485760 | tf_op jit(solution)/shard_map/dot_general | solution.py:27
  236.7 52.4 %all-gather.8.cloned.1.call-done = bf16[2048,1536]{1,0:T(8,128)(2,1)} async-done(((bf16[512,1536]{1,0:T(8,128)(2,1)}), bf16[2048,1536]{1,0:T(8,128)(2,1)}) %all-gather.8.cloned.1.call-update) | async-done | bytes 6291472 | tf_op jit(solution)/shard_map/all_gather | solution.py:198
  289.1 8.4 %fusion.6 = f32[1024,768]{0,1:T(8,128)} fusion(bf16[2048,1536]{1,0:T(8,128)(2,1)} %all-gather.8.cloned.1.call-done, bf16[512,2048]{1,0:T(8,128)(2,1)} %collective-permute-done.14, bf16[512,1024]{1,0:T(8,128)(2,1)} %bitcast.278, bf16[512,1024]{1,0:T(8,128)(2,1)} %bitcast.274), kind=kOutput, calls=%fused_computation.36 | convolution fusion | flops 3233808384 | bytes 10485760 | tf_op jit(solution)/shard_map/dot_general | solution.py:27
  297.6 14.1 %multiply_convert_fusion.3 = (bf16[1024,768]{0,1:T(8,128)(2,1)}, bf16[1024,768]{0,1:T(8,128)(2,1)S(1)}, bf16[1024,768]{0,1:T(8,128)(2,1)}) fusion(f32[1024,768]{0,1:T(8,128)S(1)} %copy-done.80, f32[1024,768]{0,1:T(8,128)} %fusion.6, bf16[2048,1536]{1,0:T(8,128)(2,1)S(1)} %copy-done.75, bf16[512,2048]{1,0:T(8,128)(2,1)} %collective-permute-done.14, ...), kind=kOutput, calls=%fused_computation.44 | convolution fusion | flops 3246391296 | bytes 18350080 | tf_op jit(solution)/shard_map/dot_general | solution.py:27
  311.6 9.4 %fusion.12 = f32[1024,2048]{1,0:T(8,128)S(1)} fusion(bf16[2048,1536]{1,0:T(8,128)(2,1)S(1)} %copy-done.75, bf16[1024,768]{0,1:T(8,128)(2,1)} %get-tuple-element.62, bf16[1024,768]{0,1:T(8,128)(2,1)} %get-tuple-element.60), kind=kOutput, calls=%fused_computation.55 | convolution fusion | flops 6448742400 | bytes 17825792 | tf_op jit(solution)/shard_map/dot_general | solution.py:31
  321.5 4.1 collective-permute-done.25
  329.8 10.5 %collective-permute-done.28 = bf16[1,2,128,1024]{3,2,1,0:T(8,128)(2,1)S(1)} collective-permute-done((bf16[1,2,128,1024]{3,2,1,0:T(8,128)(2,1)S(1)}, bf16[1,2,128,1024]{3,2,1,0:T(8,128)(2,1)S(1)}, u32[]{:S(2)}, u32[]{:S(2)}) %collective-permute-start.28) | collective-permute-done | bytes 524320 | tf_op jit(solution)/shard_map/ppermute | solution.py:102
  343.9 4.3 collective-permute-done.29
  361.0 9.4 %collective-permute-done.31 = bf16[1,2,128,1024]{3,2,1,0:T(8,128)(2,1)S(1)} collective-permute-done((bf16[1,2,128,1024]{3,2,1,0:T(8,128)(2,1)S(1)}, bf16[1,2,128,1024]{3,2,1,0:T(8,128)(2,1)S(1)}, u32[]{:S(2)}, u32[]{:S(2)}) %collective-permute-start.31) | collective-permute-done | bytes 524320 | tf_op jit(solution)/shard_map/ppermute | solution.py:102
  373.0 6.8 convolution_convert_fusion.1
  392.6 4.5 concatenate.233
  397.1 4.6 fusion.98
  410.4 11.8 %convolution_convert_fusion = bf16[2048,1536]{1,0:T(8,128)(2,1)} fusion(bf16[1024,768]{0,1:T(8,128)(2,1)} %get-tuple-element.62, bf16[1024,768]{0,1:T(8,128)(2,1)} %get-tuple-element.60, bf16[512,2048]{1,0:T(8,128)(2,1)} %collective-permute-done.14, bf16[512,1024]{1,0:T(8,128)(2,1)} %bitcast.279, bf16[512,1024]{1,0:T(8,128)(2,1)} %bitcast.275), kind=kOutput, calls=%fused_computation.7 | convolution fusion | flops 6464471040 | bytes 13631488 | tf_op jit(solution)/shard_map/dot_general | solution.py:35
  423.7 5.4 fusion.123
  448.5 8.3 %collective-permute-done.18 = bf16[1,2,128,1024]{3,2,1,0:T(8,128)(2,1)} collective-permute-done((bf16[1,2,128,1024]{3,2,1,0:T(8,128)(2,1)}, bf16[1,2,128,1024]{3,2,1,0:T(8,128)(2,1)}, u32[]{:S(2)}, u32[]{:S(2)}) %collective-permute-start.18) | collective-permute-done | bytes 524320 | tf_op jit(solution)/shard_map/ppermute | solution.py:102
  471.5 15.2 %collective-permute-done.46 = f32[272,128]{1,0:T(8,128)S(1)} collective-permute-done((f32[272,128]{1,0:T(8,128)S(1)}, f32[272,128]{1,0:T(8,128)S(1)}, u32[]{:S(2)}, u32[]{:S(2)}) %collective-permute-start.46) | collective-permute-done | bytes 139296 | tf_op jit(solution)/shard_map/ppermute | solution.py:102
  506.1 107.9 %reduce-scatter.6.cloned.1.call-done = bf16[512,1536]{1,0:T(8,128)(2,1)} async-done(((bf16[2048,1536]{1,0:T(8,128)(2,1)}), bf16[512,1536]{1,0:T(8,128)(2,1)}) %reduce-scatter.6.cloned.1.call-update) | async-done | bytes 1572880 | tf_op jit(solution)/shard_map/reduce_scatter | solution.py:270
  633.0 5.9 collective-permute-done.41
  678.3 18.0 %all-to-all-done.4 = bf16[8,64,1536]{2,1,0:T(8,128)(2,1)S(1)} async-done(((bf16[8,64,1536]{2,1,0:T(8,128)(2,1)}), bf16[8,64,1536]{2,1,0:T(8,128)(2,1)S(1)}, u32[]{:S(2)}, u32[]{:S(2)}) %all-to-all-start.4) | async-done | bytes 1572896 | tf_op jit(solution)/shard_map/all_to_all | solution.py:342
  699.4 15.3 %fusion.105 = (bf16[64,24576]{1,0:T(8,128)(2,1)}, f32[64,24576]{1,0:T(8,128)}, f32[64,24576]{1,0:T(8,128)}, f32[64,24576]{1,0:T(8,128)}) fusion(f32[64,24576]{1,0:T(8,128)} %param.16, f32[]{:T(128)S(6)} %min.3, bf16[64,24576]{1,0:T(8,128)(2,1)} %constant_dynamic-update-slice_fusion, f32[64,24576]{1,0:T(8,128)} %param.18, f32[64,24576]{1,0:T(8,128)} %param.17), kind=kLoop, calls=%fused_computation.328 | loop fusion | flops 26738688 | bytes 44040196 | tf_op jit(solution)/shard_map/convert_element_type | solution.py:98
  (476 shorter events, 250.3 us)
Async XLA Ops:
  13.3 18.3 %all-to-all-start = ((bf16[8,64,768]{2,1,0:T(8,128)(2,1)}), bf16[8,64,768]{2,1,0:T(8,128)(2,1)S(1)}, u32[]{:S(2)}, u32[]{:S(2)}) async-start(bf16[8,64,768]{2,1,0:T(8,128)(2,1)} %copy.76), calls=%async_computation | async-start | bytes 1572864 | tf_op jit(solution)/shard_map/all_to_all | solution.py:197
  18.4 101.0 %all-gather.6.cloned.1.call-start = ((), (), s32[]{:S(2)}) async-start(), calls=%async_computation.9 | async-start | bytes 3932160 | tf_op jit(solution)/shard_map/all_gather | solution.py:198
  18.5 17.3 %collective-permute-start = (bf16[1,1,128,1024]{3,2,1,0:T(8,128)(2,1)S(1)}, bf16[1,1,128,1024]{3,2,1,0:T(8,128)(2,1)S(1)}, u32[]{:S(2)}, u32[]{:S(2)}) collective-permute-start(bf16[1,1,128,1024]{3,2,1,0:T(8,128)(2,1)S(1)} %get-tuple-element.116), channel_id=1, source_target_pairs={{0,2},{1,3},{2,0},{3,1},{4,6},{5,7},{6,4},{7,5},{8,10},{9,11},{10,... | collective-permute-start | bytes 786440 | tf_op jit(solution)/shard_map/ppermute | solution.py:102
  20.6 17.6 %collective-permute-start.2 = (bf16[1,1,128,1024]{3,2,1,0:T(8,128)(2,1)S(1)}, bf16[1,1,128,1024]{3,2,1,0:T(8,128)(2,1)S(1)}, u32[]{:S(2)}, u32[]{:S(2)}) collective-permute-start(bf16[1,1,128,1024]{3,2,1,0:T(8,128)(2,1)S(1)} %get-tuple-element.117), channel_id=1, source_target_pairs={{0,4},{1,5},{2,6},{3,7},{4,0},{5,1},{6,2},{7,3},{8,12},{9,13},{10,... | collective-permute-start | bytes 786440 | tf_op jit(solution)/shard_map/ppermute | solution.py:102
  36.7 59.0 %collective-permute-start.1 = (bf16[1,2,128,1024]{3,2,1,0:T(8,128)(2,1)}, bf16[1,2,128,1024]{3,2,1,0:T(8,128)(2,1)}, u32[]{:S(2)}, u32[]{:S(2)}) collective-permute-start(bf16[1,2,128,1024]{3,2,1,0:T(8,128)(2,1)} %pad_maximum_fusion.31), channel_id=1, source_target_pairs={{0,4},{1,5},{2,6},{3,7},{4,0},{5,1},{6,2},{7,3},{8,12},{9,13},{10,... | collective-permute-start | bytes 1572872 | tf_op jit(solution)/shard_map/ppermute | solution.py:102
  39.0 57.9 %collective-permute-start.3 = (bf16[2,1,128,1024]{3,2,1,0:T(8,128)(2,1)}, bf16[2,1,128,1024]{3,2,1,0:T(8,128)(2,1)}, u32[]{:S(2)}, u32[]{:S(2)}) collective-permute-start(bf16[2,1,128,1024]{3,2,1,0:T(8,128)(2,1)} %pad_maximum_fusion.32), channel_id=1, source_target_pairs={{0,2},{1,3},{2,0},{3,1},{4,6},{5,7},{6,4},{7,5},{8,10},{9,11},{10,... | collective-permute-start | bytes 1572872 | tf_op jit(solution)/shard_map/ppermute | solution.py:102
  42.6 62.0 %all-to-all-start.2 = ((bf16[8,64,768]{2,1,0:T(8,128)(2,1)}), bf16[8,64,768]{2,1,0:T(8,128)(2,1)}, u32[]{:S(2)}, u32[]{:S(2)}) async-start(bf16[8,64,768]{2,1,0:T(8,128)(2,1)} %copy.80), calls=%async_computation.2 | async-start | bytes 1572864 | tf_op jit(solution)/shard_map/all_to_all | solution.py:197
  104.6 52.6 %all-to-all-start.1 = ((bf16[8,64,1536]{2,1,0:T(8,128)(2,1)}), bf16[8,64,1536]{2,1,0:T(8,128)(2,1)}, u32[]{:S(2)}, u32[]{:S(2)}) async-start(bf16[8,64,1536]{2,1,0:T(8,128)(2,1)} %copy.79), calls=%async_computation.1 | async-start | bytes 3145728 | tf_op jit(solution)/shard_map/all_to_all | solution.py:197
  108.9 119.4 %all-gather.10.cloned.1.call-start = ((), (), s32[]{:S(2)}) async-start(), calls=%async_computation.11 | async-start | bytes 3932160 | tf_op jit(solution)/shard_map/all_gather | solution.py:198
  109.7 179.4 %all-gather.8.cloned.1.call-start = ((), (), s32[]{:S(2)}) async-start(), calls=%async_computation.10 | async-start | bytes 7864320 | tf_op jit(solution)/shard_map/all_gather | solution.py:198
  157.3 337.0 %reduce-scatter.8.cloned.1.call-start = ((), (), s32[]{:S(2)}) async-start(), calls=%async_computation.14 | async-start | bytes 3932160 | tf_op jit(solution)/shard_map/reduce_scatter | solution.py:270
  165.8 15.2 %collective-permute-start.8 = (bf16[1,2,128,1024]{3,2,1,0:T(8,128)(2,1)}, bf16[1,2,128,1024]{3,2,1,0:T(8,128)(2,1)}, u32[]{:S(2)}, u32[]{:S(2)}) collective-permute-start(bf16[1,2,128,1024]{3,2,1,0:T(8,128)(2,1)} %bitcast.27), channel_id=1, source_target_pairs={{0,4},{1,5},{2,6},{3,7},{4,0},{5,1},{6,2},{7,3},{8,12},{9,13},{10,... | collective-permute-start | bytes 1572872 | tf_op jit(solution)/shard_map/ppermute | solution.py:102
  172.4 17.0 %collective-permute-start.6 = (bf16[2,1,128,1024]{3,2,1,0:T(8,128)(2,1)}, bf16[2,1,128,1024]{3,2,1,0:T(8,128)(2,1)}, u32[]{:S(2)}, u32[]{:S(2)}) collective-permute-start(bf16[2,1,128,1024]{3,2,1,0:T(8,128)(2,1)} %slice.748), channel_id=1, source_target_pairs={{0,2},{1,3},{2,0},{3,1},{4,6},{5,7},{6,4},{7,5},{8,10},{9,11},{10,... | collective-permute-start | bytes 1572872 | tf_op jit(solution)/shard_map/ppermute | solution.py:102
  172.9 18.2 %collective-permute-start.22 = (bf16[1,1,128,1024]{3,2,1,0:T(8,128)(2,1)}, bf16[1,1,128,1024]{3,2,1,0:T(8,128)(2,1)S(1)}, u32[]{:S(2)}, u32[]{:S(2)}) collective-permute-start(bf16[1,1,128,1024]{3,2,1,0:T(8,128)(2,1)} %get-tuple-element.107), channel_id=1, source_target_pairs={{0,4},{1,5},{2,6},{3,7},{4,0},{5,1},{6,2},{7,3},{8,12},{9,13},{10,... | collective-permute-start | bytes 786440 | tf_op jit(solution)/shard_map/ppermute | solution.py:102
  179.1 26.7 %collective-permute-start.21 = (bf16[1,2,128,1024]{3,2,1,0:T(8,128)(2,1)S(1)}, bf16[1,2,128,1024]{3,2,1,0:T(8,128)(2,1)S(1)}, u32[]{:S(2)}, u32[]{:S(2)}) collective-permute-start(bf16[1,2,128,1024]{3,2,1,0:T(8,128)(2,1)S(1)} %pad_maximum_fusion.38), channel_id=1, source_target_pairs={{0,4},{1,5},{2,6},{3,7},{4,0},{5,1},{6,2},{7,3},{8,12},{9,13},{10,... | collective-permute-start | bytes 1572872 | tf_op jit(solution)/shard_map/ppermute | solution.py:102
  192.3 16.2 %collective-permute-start.23 = (bf16[2,1,128,1024]{3,2,1,0:T(8,128)(2,1)S(1)}, bf16[2,1,128,1024]{3,2,1,0:T(8,128)(2,1)S(1)}, u32[]{:S(2)}, u32[]{:S(2)}) collective-permute-start(bf16[2,1,128,1024]{3,2,1,0:T(8,128)(2,1)S(1)} %pad_maximum_fusion.39), channel_id=1, source_target_pairs={{0,2},{1,3},{2,0},{3,1},{4,6},{5,7},{6,4},{7,5},{8,10},{9,11},{10,... | collective-permute-start | bytes 1572872 | tf_op jit(solution)/shard_map/ppermute | solution.py:102
  228.3 60.8 %collective-permute-start.14 = (bf16[512,2048]{1,0:T(8,128)(2,1)}, bf16[512,2048]{1,0:T(8,128)(2,1)}, u32[]{:S(2)}, u32[]{:S(2)}) collective-permute-start(bf16[512,2048]{1,0:T(8,128)(2,1)} %pad_maximum_fusion.8), channel_id=1, source_target_pairs={{0,1},{1,0},{2,3},{3,2},{4,5},{5,4},{6,7},{7,6},{8,9},{9,8},{10,11... | collective-permute-start | bytes 6291464 | tf_op jit(solution)/shard_map/ppermute | solution.py:102
  326.3 14.0 %collective-permute-start.28 = (bf16[1,2,128,1024]{3,2,1,0:T(8,128)(2,1)S(1)}, bf16[1,2,128,1024]{3,2,1,0:T(8,128)(2,1)S(1)}, u32[]{:S(2)}, u32[]{:S(2)}) collective-permute-start(bf16[1,2,128,1024]{3,2,1,0:T(8,128)(2,1)S(1)} %bitcast.315), channel_id=1, source_target_pairs={{0,4},{1,5},{2,6},{3,7},{4,0},{5,1},{6,2},{7,3},{8,12},{9,13},{10,... | collective-permute-start | bytes 1572872 | tf_op jit(solution)/shard_map/ppermute | solution.py:102
  379.9 124.0 %reduce-scatter.4.cloned.1.call-start = ((), (), s32[]{:S(2)}) async-start(), calls=%async_computation.12 | async-start | bytes 3932160 | tf_op jit(solution)/shard_map/reduce_scatter | solution.py:270
  410.4 203.6 %reduce-scatter.6.cloned.1.call-start = ((), (), s32[]{:S(2)}) async-start(), calls=%async_computation.13 | async-start | bytes 7864320 | tf_op jit(solution)/shard_map/reduce_scatter | solution.py:270
  436.4 24.0 %collective-permute-start.35 = (bf16[512,2048]{1,0:T(8,128)(2,1)}, bf16[512,2048]{1,0:T(8,128)(2,1)}, u32[]{:S(2)}, u32[]{:S(2)}) collective-permute-start(bf16[512,2048]{1,0:T(8,128)(2,1)} %slice.737), channel_id=1, source_target_pairs={{0,1},{1,0},{2,3},{3,2},{4,5},{5,4},{6,7},{7,6},{8,9},{9,8},{10,11... | collective-permute-start | bytes 6291464 | tf_op jit(solution)/shard_map/ppermute | solution.py:102
  442.1 14.7 %collective-permute-start.18 = (bf16[1,2,128,1024]{3,2,1,0:T(8,128)(2,1)}, bf16[1,2,128,1024]{3,2,1,0:T(8,128)(2,1)}, u32[]{:S(2)}, u32[]{:S(2)}) collective-permute-start(bf16[1,2,128,1024]{3,2,1,0:T(8,128)(2,1)} %bitcast.43), channel_id=1, source_target_pairs={{0,4},{1,5},{2,6},{3,7},{4,0},{5,1},{6,2},{7,3},{8,12},{9,13},{10,... | collective-permute-start | bytes 1572872 | tf_op jit(solution)/shard_map/ppermute | solution.py:102
  447.5 171.7 %collective-permute-start.16 = (bf16[2,1,128,1024]{3,2,1,0:T(8,128)(2,1)}, bf16[2,1,128,1024]{3,2,1,0:T(8,128)(2,1)S(1)}, u32[]{:S(2)}, u32[]{:S(2)}) collective-permute-start(bf16[2,1,128,1024]{3,2,1,0:T(8,128)(2,1)} %slice.746), channel_id=1, source_target_pairs={{0,2},{1,3},{2,0},{3,1},{4,6},{5,7},{6,4},{7,5},{8,10},{9,11},{10,... | collective-permute-start | bytes 1572872 | tf_op jit(solution)/shard_map/ppermute | solution.py:102
  458.9 170.2 %collective-permute-start.19 = (bf16[1,1,128,1024]{3,2,1,0:T(8,128)(2,1)}, bf16[1,1,128,1024]{3,2,1,0:T(8,128)(2,1)}, u32[]{:S(2)}, u32[]{:S(2)}) collective-permute-start(bf16[1,1,128,1024]{3,2,1,0:T(8,128)(2,1)} %slice.753), channel_id=1, source_target_pairs={{0,2},{1,3},{2,0},{3,1},{4,6},{5,7},{6,4},{7,5},{8,10},{9,11},{10,... | collective-permute-start | bytes 786440 | tf_op jit(solution)/shard_map/ppermute | solution.py:102
  465.8 22.8 %collective-permute-start.38 = (bf16[1,2,128,1024]{3,2,1,0:T(8,128)(2,1)}, bf16[1,2,128,1024]{3,2,1,0:T(8,128)(2,1)}, u32[]{:S(2)}, u32[]{:S(2)}) collective-permute-start(bf16[1,2,128,1024]{3,2,1,0:T(8,128)(2,1)} %bitcast.66), channel_id=1, source_target_pairs={{0,4},{1,5},{2,6},{3,7},{4,0},{5,1},{6,2},{7,3},{8,12},{9,13},{10,... | collective-permute-start | bytes 1572872 | tf_op jit(solution)/shard_map/ppermute | solution.py:102
  469.3 22.7 %collective-permute-start.36 = (bf16[2,1,128,1024]{3,2,1,0:T(8,128)(2,1)S(1)}, bf16[2,1,128,1024]{3,2,1,0:T(8,128)(2,1)S(1)}, u32[]{:S(2)}, u32[]{:S(2)}) collective-permute-start(bf16[2,1,128,1024]{3,2,1,0:T(8,128)(2,1)S(1)} %slice.742), channel_id=1, source_target_pairs={{0,2},{1,3},{2,0},{3,1},{4,6},{5,7},{6,4},{7,5},{8,10},{9,11},{10,... | collective-permute-start | bytes 1572872 | tf_op jit(solution)/shard_map/ppermute | solution.py:102
  470.2 16.4 %collective-permute-start.46 = (f32[272,128]{1,0:T(8,128)S(1)}, f32[272,128]{1,0:T(8,128)S(1)}, u32[]{:S(2)}, u32[]{:S(2)}) collective-permute-start(f32[272,128]{1,0:T(8,128)S(1)} %add.460), channel_id=1, source_target_pairs={{0,2},{1,3},{2,0},{3,1},{4,6},{5,7},{6,4},{7,5},{8,10},{9,11},{10,... | collective-permute-start | bytes 417800 | tf_op jit(solution)/shard_map/ppermute | solution.py:102
  486.6 135.3 %collective-permute-start.47 = (f32[272,128]{1,0:T(8,128)S(1)}, f32[272,128]{1,0:T(8,128)S(1)}, u32[]{:S(2)}, u32[]{:S(2)}) collective-permute-start(f32[272,128]{1,0:T(8,128)S(1)} %add.461), channel_id=1, source_target_pairs={{0,4},{1,5},{2,6},{3,7},{4,0},{5,1},{6,2},{7,3},{8,12},{9,13},{10,... | collective-permute-start | bytes 417800 | tf_op jit(solution)/shard_map/ppermute | solution.py:102
  620.4 20.6 %collective-permute-start.17 = (bf16[1,1,128,1024]{3,2,1,0:T(8,128)(2,1)S(1)}, bf16[1,1,128,1024]{3,2,1,0:T(8,128)(2,1)S(1)}, u32[]{:S(2)}, u32[]{:S(2)}) collective-permute-start(bf16[1,1,128,1024]{3,2,1,0:T(8,128)(2,1)S(1)} %slice.754), channel_id=1, source_target_pairs={{0,4},{1,5},{2,6},{3,7},{4,0},{5,1},{6,2},{7,3},{8,12},{9,13},{10,... | collective-permute-start | bytes 786440 | tf_op jit(solution)/shard_map/ppermute | solution.py:102
  623.5 20.1 %all-to-all-start.5 = ((bf16[8,64,768]{2,1,0:T(8,128)(2,1)}), bf16[8,64,768]{2,1,0:T(8,128)(2,1)S(1)}, u32[]{:S(2)}, u32[]{:S(2)}) async-start(bf16[8,64,768]{2,1,0:T(8,128)(2,1)} %bitcast.78), calls=%async_computation.8 | async-start | bytes 1572864 | tf_op jit(solution)/shard_map/all_to_all | solution.py:342
  655.7 16.1 %all-to-all-start.3 = ((bf16[8,64,768]{2,1,0:T(8,128)(2,1)}), bf16[8,64,768]{2,1,0:T(8,128)(2,1)S(1)}, u32[]{:S(2)}, u32[]{:S(2)}) async-start(bf16[8,64,768]{2,1,0:T(8,128)(2,1)} %bitcast.70), calls=%async_computation.4 | async-start | bytes 1572864 | tf_op jit(solution)/shard_map/all_to_all | solution.py:342
  671.8 24.5 %all-to-all-start.4 = ((bf16[8,64,1536]{2,1,0:T(8,128)(2,1)}), bf16[8,64,1536]{2,1,0:T(8,128)(2,1)S(1)}, u32[]{:S(2)}, u32[]{:S(2)}) async-start(bf16[8,64,1536]{2,1,0:T(8,128)(2,1)} %bitcast.75), calls=%async_computation.6 | async-start | bytes 3145728 | tf_op jit(solution)/shard_map/all_to_all | solution.py:342
  (111 other events, 1020.4 us)
Sparse Core Ops, SparseCore 0:
  32.6 63.6 all-gather.5
  111.4 62.0 all-gather.9
  175.1 113.9 all-gather.7
  380.0 57.9 reduce-scatter.7
  440.2 60.2 reduce-scatter.3
  503.2 110.7 reduce-scatter.5

commit v2 on v1

v2 whole, which is shorter than its diff:
```python
import jax
import jax.numpy as jnp
from jax import lax
from jax.sharding import Mesh
from jax.sharding import PartitionSpec as P

HEADS = 16
KV_HEADS = 8
HEAD_DIM = 128
FF = 6144
TOK_DEV = 128
STEP = 5

eps = 1e-06
theta = 1000000.0
beta_one = 0.5
beta_two = 0.5
rate = 0.02
decay = 0.1
adam_eps = 1e-08
contract_cols = (((1,), (1,)), ((), ()))
contract_rows = (((0,), (0,)), ((), ()))
f32 = jnp.float32
bf16 = jnp.bfloat16


def dot(a, b):
    return jnp.dot(a, b, preferred_element_type=f32)


def dot_nt(a, b):
    return lax.dot_general(a, b, contract_cols, preferred_element_type=f32)


def dot_tn(a, b):
    return lax.dot_general(a, b, contract_rows, preferred_element_type=f32)


def token_info(stored, doc_lengths, groups):
    half = TOK_DEV // 2
    device = stored // TOK_DEV
    within = stored % TOK_DEV
    section = jnp.where(within < half, device, 2 * groups - 1 - device)
    place = section * half + within % half
    ends = jnp.cumsum(doc_lengths)
    segment = jnp.sum((place[:, None] >= ends[None, :]).astype(jnp.int32), axis=1)
    starts = ends - doc_lengths
    picked = segment[:, None] == jnp.arange(doc_lengths.shape[0], dtype=jnp.int32)[None, :]
    begin = jnp.sum(jnp.where(picked, starts[None, :], 0), axis=1)
    return (place, segment, place - begin)


def rms_factor(values):
    return lax.rsqrt(jnp.mean(values * values, axis=-1, keepdims=True) + eps)


def rms(values):
    return values * rms_factor(values)


def norm_back(values, grads):
    factor = rms_factor(values)
    normed = values * factor
    return factor * (grads - normed * jnp.mean(grads * normed, axis=-1, keepdims=True))


def rotary(position):
    half = HEAD_DIM // 2
    freq = theta ** (-jnp.arange(half, dtype=f32) * 2.0 / HEAD_DIM)
    angle = position.astype(f32)[:, None] * freq[None, :]
    cosine, sine = jnp.cos(angle), jnp.sin(angle)
    return (
        jnp.concatenate([cosine, cosine], axis=1),
        jnp.concatenate([-sine, sine], axis=1),
    )


def swap_halves(values):
    half = HEAD_DIM // 2
    return jnp.concatenate([values[:, half:], values[:, :half]], axis=1)


def turn(values, cosine, sine):
    return values * cosine + swap_halves(values) * sine


def turn_back(grads, cosine, sine):
    return grads * cosine - swap_halves(grads) * sine


def adam(weight, first, second, grad):
    first_new = beta_one * first + (1.0 - beta_one) * grad
    second_new = beta_two * second + (1.0 - beta_two) * grad * grad
    fix_one = 1.0 - beta_one**STEP
    fix_two = 1.0 - beta_two**STEP
    weight_new = weight - rate * (
        first_new / fix_one / (jnp.sqrt(second_new / fix_two) + adam_eps) + decay * weight
    )
    return (first_new, second_new, weight_new, weight_new.astype(bf16))


def after(value, *earlier):
    return lax.optimization_barrier((value, *earlier))[0]


def swap(value, axis, bit):
    return shift(value, axis, 1 << bit)


def shift(value, axis, offset):
    return lax.ppermute(value, axis, [(i, i ^ offset) for i in range(lax.axis_size(axis))])


def cp_offsets(groups):
    bits = groups.bit_length() - 1
    order = [0] + list(range(bits - 1, 0, -1))
    offsets = [0]
    for bit in reversed(order):
        offsets = offsets + [o | (1 << bit) for o in offsets]
    return offsets


def halves(value):
    middle = value.shape[1] // 2
    return value[:, :middle], value[:, middle:]


def long_bits(reverse):
    bits = list(range(1, lax.axis_size("cp").bit_length() - 1))
    return bits[::-1] if reverse else bits


def gather_cp(value):
    parts = []
    for reverse, part in enumerate(halves(value)):
        bits = long_bits(reverse)
        columns = part.shape[1]
        part = part.reshape((1,) * len(bits) + part.shape)
        for bit in bits:
            part = jnp.concatenate([part, swap(part, "cp", bit)], axis=len(bits) - bit)
        part = part.reshape(-1, columns)
        parts.append(jnp.concatenate([part, swap(part, "cp", 0)], axis=0))
    return parts


def scatter_cp(left, weights):
    total = left.shape[0]
    half = total // 2
    groups = lax.axis_size("cp")
    sent = [swap(dot_nt(left[half:], w).astype(bf16), "cp", 0) for w in weights]
    parts = []
    for reverse, (w, came) in enumerate(zip(weights, sent)):
        bits = long_bits(reverse)
        columns = w.shape[0]
        part = dot_nt(left[:half], w) + came.astype(f32)
        part = part.reshape((2,) * len(bits) + (total // groups, columns))
        for bit in bits:
            axis = len(bits) - bit
            stays = lax.slice_in_dim(part, 0, 1, axis=axis)
            leaves = lax.slice_in_dim(part, 1, 2, axis=axis).astype(bf16)
            part = stays + swap(leaves, "cp", bit).astype(f32)
        parts.append(part.reshape(-1, columns))
    return jnp.concatenate(parts, axis=1)


def sum_all(value):
    value = value + swap(value, "cp", 0)
    for axis, step in (("cp", 2), (("dh", "dl"), 1)):
        value = sum(
            (shift(value, axis, offset) for offset in range(step, lax.axis_size(axis), step)),
            start=value,
        )
    return value


def squares_of(value):
    value = value.astype(f32)
    return jnp.sum(value * value)


def local(
    tokens,
    cotangent,
    lengths,
    big_weight,
    big_first,
    big_second,
    small_weight,
    small_first,
    small_second,
    qk_gain,
    qk_first,
    qk_second,
):
    groups = lax.axis_size("cp")
    upper_planes = lax.axis_size("dh")
    me = lax.axis_index("cp")
    owner = (lax.axis_index("dh") * 2 + lax.axis_index("dl")) * groups + me
    wr = big_weight.shape[0]
    rows, features = tokens.shape[1:]
    width_attn = HEADS * HEAD_DIM
    width_kv = KV_HEADS * HEAD_DIM
    width_qkv = width_attn + 2 * width_kv
    start_mlp = width_qkv + width_attn
    start_down = start_mlp + 2 * FF
    own_q = HEADS // groups
    own_kv = max(1, KV_HEADS // groups)
    copies = max(1, groups // KV_HEADS)
    share = own_q // own_kv
    wq = own_q * HEAD_DIM
    wkv = own_kv * HEAD_DIM
    win = wq + 2 * wkv
    wff = FF // (2 * groups)
    scale = HEAD_DIM ** (-0.5)
    pair = ("dl", "cp")
    planes = ("dh", "dl")

    def blocks(start, width, count, repeat=1):
        part = big_weight[:, start : start + width].astype(bf16)
        part = part.reshape(wr, count // repeat, -1).transpose(1, 0, 2)
        return jnp.repeat(part, repeat, axis=0) if repeat > 1 else part

    def exchange(part, axis):
        return lax.all_to_all(part, axis, 0, 0, tiled=True)

    def relative(value):
        if upper_planes != 2:
            return value
        first, second = halves(value)
        swapped = jnp.concatenate([second, first], axis=1)
        return jnp.where(lax.axis_index("dh") == 1, swapped, value)

    def gather_rows(part):
        if upper_planes == 2:
            return part, swap(part, "dh", 0)
        full = lax.all_gather(part, "dh", axis=0, tiled=True)
        return full[: features // 2], full[features // 2 :]

    def scatter_rows(first, second):
        if upper_planes == 2:
            return (first + swap(second.astype(bf16), "dh", 0).astype(f32)).astype(bf16)
        joined = jnp.concatenate([first, second], axis=0).astype(bf16)
        return lax.psum_scatter(joined, "dh", scatter_dimension=0, tiled=True)

    attn_blocks = jnp.concatenate(
        [
            blocks(0, width_attn, groups),
            blocks(width_attn, width_kv, groups, copies),
            blocks(width_attn + width_kv, width_kv, groups, copies),
            blocks(width_qkv, width_attn, groups),
        ],
        axis=2,
    )
    attn_rows = exchange(attn_blocks, "cp").reshape(groups * wr, -1)
    in_w = lax.all_gather(attn_rows[:, :win], planes, axis=0, tiled=True)
    out_w = lax.all_gather(attn_rows[:, win:], planes, axis=0, tiled=True)
    gu_blocks = jnp.concatenate(
        [blocks(start_mlp, FF, 2 * groups), blocks(start_mlp + FF, FF, 2 * groups)], axis=2
    )
    gu_rows = exchange(after(gu_blocks, attn_rows), pair).reshape(2 * groups * wr, -1)
    gu_w = gather_rows(gu_rows)
    down_blocks = after(blocks(start_down, FF, 2 * groups), gu_rows)
    down_w = gather_rows(exchange(down_blocks, pair).reshape(2 * groups * wr, -1))

    small_place = lax.dynamic_update_slice_in_dim(
        jnp.zeros((HEADS + 2, features), bf16), small_weight.astype(bf16).T, owner * wr, 1
    )
    small_full = sum_all(small_place.reshape(-1, 128)).reshape(HEADS + 2, features)
    gate_w = lax.dynamic_slice_in_dim(small_full, me * own_q, own_q, 0).T
    gain_one = 1.0 + small_full[HEADS].astype(f32)
    gain_two = 1.0 + small_full[HEADS + 1].astype(f32)

    doc_lengths = lengths[0]
    offsets = jnp.array(cp_offsets(groups), jnp.int32)
    stored = ((me ^ offsets)[:, None] * rows + jnp.arange(rows, dtype=jnp.int32)).reshape(-1)
    place, segment, position = token_info(stored, doc_lengths, groups)
    cosine, sine = rotary(position)
    allowed = (segment[:, None] == segment[None, :]) & (place[None, :] <= place[:, None])
    query_gain = 1.0 + qk_gain[0]
    key_gain = 1.0 + qk_gain[1]

    def gather_pair(value):
        other = swap(value, "dl", 0)
        return gather_cp(value), gather_cp(other)

    def scatter_pair(lefts, weights):
        other = scatter_cp(lefts[1], weights)
        came = swap(other.astype(bf16), "dl", 0)
        return scatter_cp(lefts[0], weights) + came.astype(f32)

    tokens_all = [part.astype(f32) for part in gather_cp(tokens[0])]
    mean = sum(jnp.sum(part * part, axis=1, keepdims=True) for part in tokens_all) / features
    token_factor = lax.rsqrt(mean + eps)
    middle_feature = features // 2
    gain_halves = (gain_one[:middle_feature], gain_one[middle_feature:])
    kept_one = [(p * token_factor * g).astype(bf16) for p, g in zip(tokens_all, gain_halves)]

    def split_rows(weights):
        return weights[:middle_feature], weights[middle_feature:]

    def dots(lefts, rights):
        return sum(dot(a, b) for a, b in zip(lefts, rights))

    sig = jax.nn.sigmoid(dots(kept_one, split_rows(gate_w)))
    proj = dots(kept_one, split_rows(in_w))

    def head(matrix, index):
        return matrix[:, index * HEAD_DIM : (index + 1) * HEAD_DIM]

    q_part = [head(proj, h) for h in range(own_q)]
    k_part = [head(proj, own_q + g) for g in range(own_kv)]
    values = [head(proj, own_q + own_kv + g).astype(bf16) for g in range(own_kv)]
    queries = [turn(rms(q) * query_gain, cosine, sine).astype(bf16) for q in q_part]
    keys = [turn(rms(k) * key_gain, cosine, sine).astype(bf16) for k in k_part]
    probs, heads = [], []
    for h in range(own_q):
        g = h // share
        scores = jnp.where(allowed, dot_nt(queries[h], keys[g]) * scale, -1e30)
        weights = jnp.where(allowed, jnp.exp(scores - jnp.max(scores, axis=-1, keepdims=True)), 0.0)
        prob = (weights / jnp.sum(weights, axis=-1, keepdims=True)).astype(bf16)
        probs.append(prob)
        heads.append(dot(prob, values[g]))
    gated = jnp.concatenate(
        [(heads[h] * sig[:, h : h + 1]).astype(bf16) for h in range(own_q)], axis=1
    )
    inputs = tokens[0].astype(f32)
    middle = inputs + scatter_cp(gated, split_rows(out_w))

    normed_two = rms(middle)
    grad_out = cotangent[0].astype(f32)
    grad_branch = gather_pair(relative(cotangent[0]))
    kept_two = gather_pair(relative((normed_two * gain_two).astype(bf16)))
    hidden, gate_parts = [], []
    for row in range(2):
        gate_up = dots(kept_two[row], gu_w)
        gate, upper = gate_up[:, :wff], gate_up[:, wff:]
        sig_gate = jax.nn.sigmoid(gate)
        hidden.append((gate * sig_gate * upper).astype(bf16))
        gate_parts.append((gate, upper, sig_gate))

    def weight_terms(lefts, rights):
        return [sum(dot_tn(lefts[r][half], rights[r]) for r in range(2)) for half in range(2)]

    down_term = scatter_rows(*weight_terms(grad_branch, hidden))
    grad_gu = [None, None]
    for row in (1, 0):
        gate, upper, sig_gate = gate_parts[row]
        grad_hidden = dots(grad_branch[row], down_w)
        grad_gate = grad_hidden * upper * sig_gate * (1.0 + gate * (1.0 - sig_gate))
        grad_upper = grad_hidden * gate * sig_gate
        grad_gu[row] = jnp.concatenate([grad_gate, grad_upper], axis=1).astype(bf16)
    grad_two = relative(scatter_pair(grad_gu, gu_w))
    gu_term = scatter_rows(*weight_terms(kept_two, grad_gu))
    gain_two_term = jnp.sum(grad_two * normed_two, axis=0)
    grad_middle = grad_out + norm_back(middle, grad_two * gain_two)

    grad_attn_branch = gather_cp(grad_middle.astype(bf16))
    late_hidden = [after(h, *grad_attn_branch) for h in hidden]
    result = middle + relative(scatter_pair(late_hidden, down_w))
    grad_gated = dots(grad_attn_branch, split_rows(out_w))
    grad_q, grad_logits = [], []
    grad_k = [0.0] * own_kv
    grad_v = [0.0] * own_kv
    q_gain_term = jnp.zeros((HEAD_DIM,), f32)
    k_gain_term = jnp.zeros((HEAD_DIM,), f32)
    for h in range(own_q):
        g = h // share
        sig_h = sig[:, h : h + 1]
        back = head(grad_gated, h)
        grad_sig = jnp.sum(back * heads[h], axis=-1, keepdims=True)
        grad_logits.append((grad_sig * sig_h * (1.0 - sig_h)).astype(bf16))
        grad_head = (back * sig_h).astype(bf16)
        delta = jnp.sum(grad_head.astype(f32) * heads[h], axis=-1, keepdims=True)
        grad_probs = dot_nt(grad_head, values[g])
        grad_scores = (probs[h].astype(f32) * (grad_probs - delta)).astype(bf16)
        grad_qn = turn_back(dot(grad_scores, keys[g]) * scale, cosine, sine)
        q_gain_term = q_gain_term + jnp.sum(grad_qn * rms(q_part[h]), axis=0)
        grad_q.append(norm_back(q_part[h], grad_qn * query_gain).astype(bf16))
        grad_k[g] = grad_k[g] + dot_tn(grad_scores, queries[h])
        grad_v[g] = grad_v[g] + dot_tn(probs[h], grad_head)
    grad_keys = []
    for g in range(own_kv):
        grad_kn = turn_back(grad_k[g] * scale, cosine, sine)
        k_gain_term = k_gain_term + jnp.sum(grad_kn * rms(k_part[g]), axis=0)
        grad_keys.append(norm_back(k_part[g], grad_kn * key_gain).astype(bf16))
    grad_proj = jnp.concatenate(
        grad_q + grad_keys + [v.astype(bf16) for v in grad_v] + grad_logits, axis=1
    )

    def sum_rows(parts):
        joined = jnp.concatenate(parts, axis=0).astype(bf16)
        return lax.psum_scatter(joined, planes, scatter_dimension=0, tiled=True)

    out_term = sum_rows([dot_tn(part, gated) for part in grad_attn_branch])
    in_term = sum_rows([dot_tn(part, grad_proj[:, :win]) for part in kept_one])
    gate_term = jnp.concatenate([dot_tn(part, grad_proj[:, win:]) for part in kept_one], axis=0)
    full_in = jnp.concatenate([in_w, gate_w], axis=1)
    grad_one = scatter_cp(grad_proj, split_rows(full_in))
    gain_one_term = jnp.sum(grad_one * rms(inputs), axis=0)
    grad_input = grad_middle + norm_back(inputs, grad_one * gain_one)

    gate_place = lax.dynamic_update_slice_in_dim(
        jnp.zeros((HEADS, features), f32), gate_term.T, me * own_q, 0
    )
    first_small = sum_all(
        jnp.concatenate([gate_place, gain_two_term[None]], axis=0).reshape(-1, 128)
    ).reshape(HEADS + 1, features)

    def kv_sum(part):
        if copies == 1:
            return part
        return part.astype(f32).reshape(groups // copies, copies, wr, -1).sum(axis=1)

    def wide(part):
        return part.transpose(1, 0, 2).reshape(wr, -1).astype(f32)

    def to_owner(part, axis):
        return exchange(part.reshape(-1, wr, part.shape[1]), axis)

    down_own = to_owner(down_term, pair)
    gu_own = to_owner(gu_term, pair)
    out_own = to_owner(out_term, "cp")
    in_own = to_owner(in_term, "cp")
    k_own = kv_sum(in_own[:, :, wq : wq + wkv])
    v_own = kv_sum(in_own[:, :, wq + wkv :])
    if copies == 1:
        in_squares = squares_of(in_term)
    else:
        in_squares = squares_of(in_term[:, :wq]) + squares_of(k_own) + squares_of(v_own)
    local_squares = squares_of(down_term) + squares_of(gu_term) + squares_of(out_term) + in_squares
    last_small = sum_all(
        jnp.concatenate(
            [
                gain_one_term.reshape(-1, 128),
                q_gain_term[None],
                k_gain_term[None],
                jnp.full((1, 128), local_squares, f32),
            ],
            axis=0,
        )
    )
    tall = features // 128
    gain_one_grad = last_small[:tall].reshape(1, features)
    qk_grad = last_small[tall : tall + 2]
    small_all = jnp.concatenate([first_small[:HEADS], gain_one_grad, first_small[HEADS:]], axis=0)
    total = last_small[tall + 2, 0] + jnp.sum(small_all * small_all) + jnp.sum(qk_grad * qk_grad)
    norm_value = jnp.sqrt(total)
    factor = jnp.minimum(1.0, 1.0 / (norm_value + 1e-06))
    small_grad = lax.dynamic_slice_in_dim(small_all, owner * wr, wr, 1).T
    big_grad = jnp.concatenate(
        [
            wide(in_own[:, :, :wq]),
            wide(k_own),
            wide(v_own),
            wide(out_own),
            wide(gu_own[:, :, :wff]),
            wide(gu_own[:, :, wff:]),
            wide(down_own),
        ],
        axis=1,
    )
    big_out = adam(big_weight, big_first, big_second, big_grad * factor)
    small_out = adam(small_weight, small_first, small_second, small_grad * factor)
    qk_out = adam(qk_gain, qk_first, qk_second, qk_grad * factor)
    gain_grads = small_grad[:, HEADS:] * factor
    return (
        result.astype(bf16)[None],
        grad_input.astype(bf16)[None],
        *big_out,
        *small_out,
        *qk_out,
        gain_grads,
        norm_value,
    )


def solution(mesh):
    planes, groups = mesh.shape["dp"], mesh.shape["cp"]
    fine = Mesh(mesh.devices.reshape(planes // 2, 2, groups), ("dh", "dl", "cp"))
    rows = P(("dh", "dl", "cp"), None)
    row_tokens = P(("dh", "dl"), "cp", None)
    return jax.shard_map(
        local,
        mesh=fine,
        in_specs=(row_tokens, row_tokens, P(("dh", "dl"), None)) + (rows,) * 6 + (P(),) * 3,
        out_specs=(row_tokens, row_tokens) + (rows,) * 8 + (P(),) * 4 + (rows, P()),
        check_vma=False,
    )
```

time: 730 us -> 758 us (1.038)
  starting transfers between devices: 77.6 us -> 132 us
  blocking collectives: 47.8 us -> 0 us
  matrix products: 99.3 us -> 133 us
  local copies, waits for them, and re-layouts: 65.2 us -> 50.5 us
    ppermute x50 -> x101, waiting for transfers between devices: 108 us -> 272 us  [shift(): lax.ppermute(value, axis, [(i, i ^ offset) for i in range(lax.axis_size(a...]
    reduce_scatter x3 -> x2, waiting for transfers between devices: 108 us -> 0.02 us  [sum_rows(): return lax.psum_scatter(joined, planes, scatter_dimension=0, tiled=True)]
    all_gather x1 -> x0, blocking collectives: 47.8 us -> none  [local(): lax.all_gather(small_weight.astype(bf16).T, ('dp', 'cp'), axis=0)]
    ppermute x50 -> x101, starting transfers between devices: 52.4 us -> 98.2 us  [shift(): lax.ppermute(value, axis, [(i, i ^ offset) for i in range(lax.axis_size(a...]
    all_gather x3 -> x2, waiting for transfers between devices: 52.4 us -> 15.4 us  [the longest x1 13.3 us: local(): out_w = lax.all_gather(attn_rows[:, win:], planes, axis=0, tiled=True)]
    dot_general x8 -> x28, matrix products: 25.8 us -> 60.5 us  [dot_nt(): return lax.dot_general(a, b, contract_cols, preferred_element_type=f32)]
    concatenate x24 -> x29, other arithmetic: 16.6 us -> 33.4 us  [the longest x24 28.7 us: gather_cp(): part = jnp.concatenate([part, swap(part, 'cp', bit)], axis=len(bits) - bit)]
    all_to_all x6 -> x7, waiting for transfers between devices: 31.5 us -> 16.5 us  [exchange(): return lax.all_to_all(part, axis, 0, 0, tiled=True)]
  transfers between devices with their start and end apart: 62 -> 112, of which waited for: 28 -> 38; matrix products, arithmetic and copies ran while one was open for 27% -> 35% of each run, Pallas kernels for 0% -> 0%
where the time goes in v2:
time: 758 us; the launch traced here: 750 us
  waiting for transfers between devices  304 us (40%)
  matrix products  133 us (18%)
  starting transfers between devices  132 us (17%)
  other arithmetic  107 us (14%)
  local copies, waits for them, and re-layouts  50.5 us (7%)
  between operations  23.2 us (3%)
    ppermute x101, waiting for transfers between devices, shift(): lax.ppermute(value, axis, [(i, i ^ offset) for i in range(lax.axis_size(a...  272 us
    ppermute x101, starting transfers between devices, shift(): lax.ppermute(value, axis, [(i, i ^ offset) for i in range(lax.axis_size(a...  98.2 us
    dot_general x28, matrix products, dot_nt(): return lax.dot_general(a, b, contract_cols, preferred_element_type=f32)  60.5 us
    dot_general x18, matrix products, dot(): return jnp.dot(a, b, preferred_element_type=f32)  42.7 us
    all_to_all x7, starting transfers between devices, exchange(): return lax.all_to_all(part, axis, 0, 0, tiled=True)  33.3 us
    dot_general x18, matrix products, dot_tn(): return lax.dot_general(a, b, contract_rows, preferred_element_type=f32)  29.8 us
    concatenate x24, other arithmetic, gather_cp(): part = jnp.concatenate([part, swap(part, 'cp', bit)], axis=len(bits) - bit)  28.7 us
    unnamed x354, local copies, waits for them, and re-layouts  18.4 us
  transfers between devices with their start and end apart: 112, of which 38 were waited for; matrix products, arithmetic and copies ran while one was open for 35% of the time, Pallas kernels for 0%

profile of v2, /device:TPU:0, one launch (start us, length us, event | category | flops | bytes accessed | tf_op | source)
XLA Modules:
  0.0 750.2 jit_solution(12143324481136193917)
XLA Ops:
  19.0 4.2 all-to-all-start
  25.1 10.7 %all-to-all-done = bf16[8,64,768]{2,1,0:T(8,128)(2,1)} async-done(((bf16[8,64,768]{2,1,0:T(8,128)(2,1)}), bf16[8,64,768]{2,1,0:T(8,128)(2,1)}, u32[]{:S(2)}, u32[]{:S(2)}) %all-to-all-start) | async-done | bytes 786464 | tf_op jit(solution)/shard_map/all_to_all | solution.py:224
  53.0 5.1 collective-permute-done.4
  72.0 8.4 %all-to-all-start.1 = ((bf16[16,64,768]{2,1,0:T(8,128)(2,1)}), bf16[16,64,768]{2,1,0:T(8,128)(2,1)}, u32[]{:S(2)}, u32[]{:S(2)}) async-start(bf16[16,64,768]{2,1,0:T(8,128)(2,1)} %copy.78), calls=%async_computation.1 | async-start | bytes 3145728 | tf_op jit(solution)/shard_map/all_to_all | solution.py:224
  108.2 13.3 %all-gather.5.cloned.1.call-done = bf16[2048,256]{1,0:T(8,128)(2,1)} async-done(((bf16[512,256]{1,0:T(8,128)(2,1)}), bf16[2048,256]{1,0:T(8,128)(2,1)}) %all-gather.5.cloned.1.call-update) | async-done | bytes 1048592 | tf_op jit(solution)/shard_map/all_gather | solution.py:256
  142.6 15.9 %collective-permute-done.14 = bf16[2,1,128,1024]{3,2,1,0:T(8,128)(2,1)S(1)} collective-permute-done((bf16[2,1,128,1024]{3,2,1,0:T(8,128)(2,1)S(1)}, bf16[2,1,128,1024]{3,2,1,0:T(8,128)(2,1)S(1)}, u32[]{:S(2)}, u32[]{:S(2)}) %collective-permute-start.14) | collective-permute-done | bytes 524320 | tf_op jit(solution)/shard_map/ppermute | solution.py:111
  171.7 4.3 all-to-all-start.2
  188.0 5.2 collective-permute-done.22
  207.6 13.7 %collective-permute-done.47 = bf16[1,1,128,1024]{3,2,1,0:T(8,128)(2,1)} collective-permute-done((bf16[1,1,128,1024]{3,2,1,0:T(8,128)(2,1)}, bf16[1,1,128,1024]{3,2,1,0:T(8,128)(2,1)}, u32[]{:S(2)}, u32[]{:S(2)}) %collective-permute-start.47) | collective-permute-done | bytes 262176 | tf_op jit(solution)/shard_map/ppermute | solution.py:111
  230.6 6.8 collective-permute-done.20
  240.9 84.9 %collective-permute-done.32 = bf16[1024,384]{1,0:T(8,128)(2,1)S(1)} collective-permute-done((bf16[1024,384]{1,0:T(8,128)(2,1)}, bf16[1024,384]{1,0:T(8,128)(2,1)S(1)}, u32[]{:S(2)}, u32[]{:S(2)}) %collective-permute-start.32) | collective-permute-done | bytes 786464 | tf_op jit(solution)/shard_map/ppermute | solution.py:111
  341.8 4.4 multiply_convert_fusion.5
  361.0 4.4 multiply_convert_fusion.3
  394.9 5.4 collective-permute-done.34
  402.5 8.4 %collective-permute-done.54 = bf16[2,1,128,1024]{3,2,1,0:T(8,128)(2,1)S(1)} collective-permute-done((bf16[2,1,128,1024]{3,2,1,0:T(8,128)(2,1)S(1)}, bf16[2,1,128,1024]{3,2,1,0:T(8,128)(2,1)S(1)}, u32[]{:S(2)}, u32[]{:S(2)}) %collective-permute-start.54) | collective-permute-done | bytes 524320 | tf_op jit(solution)/shard_map/ppermute | solution.py:111
  415.2 7.3 collective-permute-done.55
  429.2 19.6 %collective-permute-done.59 = bf16[128,2048]{1,0:T(8,128)(2,1)S(1)} collective-permute-done((bf16[128,2048]{1,0:T(8,128)(2,1)S(1)}, bf16[128,2048]{1,0:T(8,128)(2,1)S(1)}, u32[]{:S(2)}, u32[]{:S(2)}) %collective-permute-start.59) | collective-permute-done | bytes 524320 | tf_op jit(solution)/shard_map/ppermute | solution.py:111
  454.7 4.2 collective-permute-done.60
  463.6 18.4 %collective-permute-done.86 = bf16[1024,384]{1,0:T(8,128)(2,1)S(1)} collective-permute-done((bf16[1024,384]{1,0:T(8,128)(2,1)S(1)}, bf16[1024,384]{1,0:T(8,128)(2,1)S(1)}, u32[]{:S(2)}, u32[]{:S(2)}) %collective-permute-start.86) | collective-permute-done | bytes 786464 | tf_op jit(solution)/shard_map/ppermute | solution.py:111
  483.9 4.3 all-to-all-start.6
  497.6 4.0 multiply_reduce_fusion
  503.0 5.1 all-to-all-start.5
  546.3 4.1 concatenate.277
  576.4 4.2 collective-permute-done.96
  582.7 9.3 %collective-permute-done.100 = f32[272,128]{1,0:T(8,128)S(1)} collective-permute-done((f32[272,128]{1,0:T(8,128)S(1)}, f32[272,128]{1,0:T(8,128)S(1)}, u32[]{:S(2)}, u32[]{:S(2)}) %collective-permute-start.100) | collective-permute-done | bytes 139296 | tf_op jit(solution)/shard_map/ppermute | solution.py:111
  591.9 4.6 collective-permute-start.99
  600.0 12.4 %collective-permute-done.99 = f32[272,128]{1,0:T(8,128)} collective-permute-done((f32[272,128]{1,0:T(8,128)S(1)}, f32[272,128]{1,0:T(8,128)}, u32[]{:S(2)}, u32[]{:S(2)}) %collective-permute-start.99) | collective-permute-done | bytes 139296 | tf_op jit(solution)/shard_map/ppermute | solution.py:111
  637.1 5.3 collective-permute-done.80
  645.0 8.7 %collective-permute-done.73 = bf16[2,1,128,1024]{3,2,1,0:T(8,128)(2,1)S(1)} collective-permute-done((bf16[2,1,128,1024]{3,2,1,0:T(8,128)(2,1)S(1)}, bf16[2,1,128,1024]{3,2,1,0:T(8,128)(2,1)S(1)}, u32[]{:S(2)}, u32[]{:S(2)}) %collective-permute-start.73) | collective-permute-done | bytes 524320 | tf_op jit(solution)/shard_map/ppermute | solution.py:111
  656.3 8.6 %collective-permute-done.67 = bf16[2,1,128,1024]{3,2,1,0:T(8,128)(2,1)S(1)} collective-permute-done((bf16[2,1,128,1024]{3,2,1,0:T(8,128)(2,1)S(1)}, bf16[2,1,128,1024]{3,2,1,0:T(8,128)(2,1)S(1)}, u32[]{:S(2)}, u32[]{:S(2)}) %collective-permute-start.67) | collective-permute-done | bytes 524320 | tf_op jit(solution)/shard_map/ppermute | solution.py:111
  667.5 9.6 %collective-permute-done.74 = bf16[1,1,128,1024]{3,2,1,0:T(8,128)(2,1)S(1)} collective-permute-done((bf16[1,1,128,1024]{3,2,1,0:T(8,128)(2,1)S(1)}, bf16[1,1,128,1024]{3,2,1,0:T(8,128)(2,1)S(1)}, u32[]{:S(2)}, u32[]{:S(2)}) %collective-permute-start.74) | collective-permute-done | bytes 262176 | tf_op jit(solution)/shard_map/ppermute | solution.py:111
  728.3 13.7 %fusion.189 = (bf16[64,24576]{1,0:T(8,128)(2,1)}, f32[64,24576]{1,0:T(8,128)}, f32[64,24576]{1,0:T(8,128)}, f32[64,24576]{1,0:T(8,128)}) fusion(f32[64,24576]{1,0:T(8,128)} %param.16, f32[]{:T(128)S(6)} %min.3, bf16[64,24576]{1,0:T(8,128)(2,1)S(1)} %constant_dynamic-update-slice_fusion, f32[64,24576]{1,0:T(8,128)} %param.18, f32[64,24576]{1,0:T(8,128)} %param.17), kind=kLoop, calls=%fused_computation.476 | loop fusion | flops 26738688 | bytes 44040196 | tf_op jit(solution)/shard_map/convert_element_type | solution.py:99
  (819 shorter events, 388.6 us)
Async XLA Ops:
  8.2 32.5 %collective-permute-start.6 = (bf16[288,128]{1,0:T(8,128)(2,1)S(1)}, bf16[288,128]{1,0:T(8,128)(2,1)S(1)}, u32[]{:S(2)}, u32[]{:S(2)}) collective-permute-start(bf16[288,128]{1,0:T(8,128)(2,1)S(1)} %reshape.596), channel_id=1, source_target_pairs={{0,1},{1,0},{2,3},{3,2},{4,5},{5,4},{6,7},{7,6},{8,9},{9,8},{10,11... | collective-permute-start | bytes 221192 | tf_op jit(solution)/shard_map/ppermute | solution.py:111
  10.7 33.6 %collective-permute-start.3 = (bf16[1,1,128,1024]{3,2,1,0:T(8,128)(2,1)}, bf16[1,1,128,1024]{3,2,1,0:T(8,128)(2,1)}, u32[]{:S(2)}, u32[]{:S(2)}) collective-permute-start(bf16[1,1,128,1024]{3,2,1,0:T(8,128)(2,1)} %get-tuple-element.132), channel_id=1, source_target_pairs={{0,4},{1,5},{2,6},{3,7},{4,0},{5,1},{6,2},{7,3},{8,12},{9,13},{10,... | collective-permute-start | bytes 786440 | tf_op jit(solution)/shard_map/ppermute | solution.py:111
  13.1 32.9 %collective-permute-start = (bf16[1,1,128,1024]{3,2,1,0:T(8,128)(2,1)}, bf16[1,1,128,1024]{3,2,1,0:T(8,128)(2,1)}, u32[]{:S(2)}, u32[]{:S(2)}) collective-permute-start(bf16[1,1,128,1024]{3,2,1,0:T(8,128)(2,1)} %get-tuple-element.133), channel_id=1, source_target_pairs={{0,2},{1,3},{2,0},{3,1},{4,6},{5,7},{6,4},{7,5},{8,10},{9,11},{10,... | collective-permute-start | bytes 786440 | tf_op jit(solution)/shard_map/ppermute | solution.py:111
  23.3 66.2 %all-gather.3.cloned.1.call-start = ((), (), s32[]{:S(2)}) async-start(), calls=%async_computation.9 | async-start | bytes 2621440 | tf_op jit(solution)/shard_map/all_gather | solution.py:255
  72.0 97.6 %all-to-all-start.1 = ((bf16[16,64,768]{2,1,0:T(8,128)(2,1)}), bf16[16,64,768]{2,1,0:T(8,128)(2,1)}, u32[]{:S(2)}, u32[]{:S(2)}) async-start(bf16[16,64,768]{2,1,0:T(8,128)(2,1)} %copy.78), calls=%async_computation.1 | async-start | bytes 3145728 | tf_op jit(solution)/shard_map/all_to_all | solution.py:224
  80.3 41.1 %all-gather.5.cloned.1.call-start = ((), (), s32[]{:S(2)}) async-start(), calls=%async_computation.10 | async-start | bytes 1310720 | tf_op jit(solution)/shard_map/all_gather | solution.py:256
  133.8 51.3 %collective-permute-start.30 = (bf16[2,1,128,1024]{3,2,1,0:T(8,128)(2,1)}, bf16[2,1,128,1024]{3,2,1,0:T(8,128)(2,1)}, u32[]{:S(2)}, u32[]{:S(2)}) collective-permute-start(bf16[2,1,128,1024]{3,2,1,0:T(8,128)(2,1)} %pad_maximum_fusion.61), channel_id=1, source_target_pairs={{0,2},{1,3},{2,0},{3,1},{4,6},{5,7},{6,4},{7,5},{8,10},{9,11},{10,... | collective-permute-start | bytes 1572872 | tf_op jit(solution)/shard_map/ppermute | solution.py:111
  136.0 65.0 %collective-permute-start.27 = (bf16[1,2,128,1024]{3,2,1,0:T(8,128)(2,1)}, bf16[1,2,128,1024]{3,2,1,0:T(8,128)(2,1)}, u32[]{:S(2)}, u32[]{:S(2)}) collective-permute-start(bf16[1,2,128,1024]{3,2,1,0:T(8,128)(2,1)} %pad_maximum_fusion.60), channel_id=1, source_target_pairs={{0,4},{1,5},{2,6},{3,7},{4,0},{5,1},{6,2},{7,3},{8,12},{9,13},{10,... | collective-permute-start | bytes 1572872 | tf_op jit(solution)/shard_map/ppermute | solution.py:111
  171.7 51.6 %all-to-all-start.2 = ((bf16[16,64,384]{2,1,0:T(8,128)(2,1)}), bf16[16,64,384]{2,1,0:T(8,128)(2,1)}, u32[]{:S(2)}, u32[]{:S(2)}) async-start(bf16[16,64,384]{2,1,0:T(8,128)(2,1)} %copy.79), calls=%async_computation.2 | async-start | bytes 1572864 | tf_op jit(solution)/shard_map/all_to_all | solution.py:224
  204.4 34.2 %collective-permute-start.31 = (bf16[512,1024]{1,0:T(8,128)(2,1)}, bf16[512,1024]{1,0:T(8,128)(2,1)}, u32[]{:S(2)}, u32[]{:S(2)}) collective-permute-start(bf16[512,1024]{1,0:T(8,128)(2,1)} %bitcast.42), channel_id=1, source_target_pairs={{0,1},{1,0},{2,3},{3,2},{4,5},{5,4},{6,7},{7,6},{8,9},{9,8},{10,11... | collective-permute-start | bytes 3145736 | tf_op jit(solution)/shard_map/ppermute | solution.py:111
  205.5 34.7 %collective-permute-start.45 = (bf16[512,1024]{1,0:T(8,128)(2,1)}, bf16[512,1024]{1,0:T(8,128)(2,1)}, u32[]{:S(2)}, u32[]{:S(2)}) collective-permute-start(bf16[512,1024]{1,0:T(8,128)(2,1)} %bitcast.51), channel_id=1, source_target_pairs={{0,1},{1,0},{2,3},{3,2},{4,5},{5,4},{6,7},{7,6},{8,9},{9,8},{10,11... | collective-permute-start | bytes 3145736 | tf_op jit(solution)/shard_map/ppermute | solution.py:111
  221.3 112.9 %collective-permute-start.25 = (bf16[1024,768]{1,0:T(8,128)(2,1)}, bf16[1024,768]{1,0:T(8,128)(2,1)}, u32[]{:S(2)}, u32[]{:S(2)}) collective-permute-start(bf16[1024,768]{1,0:T(8,128)(2,1)} %bitcast.33), channel_id=1, source_target_pairs={{0,16},{16,0},{1,17},{17,1},{2,18},{18,2},{3,19},{19,3},{4,20},{20... | collective-permute-start | bytes 4718600 | tf_op jit(solution)/shard_map/ppermute | solution.py:111
  223.3 102.5 %collective-permute-start.32 = (bf16[1024,384]{1,0:T(8,128)(2,1)}, bf16[1024,384]{1,0:T(8,128)(2,1)S(1)}, u32[]{:S(2)}, u32[]{:S(2)}) collective-permute-start(bf16[1024,384]{1,0:T(8,128)(2,1)} %bitcast.40), channel_id=1, source_target_pairs={{0,16},{16,0},{1,17},{17,1},{2,18},{18,2},{3,19},{19,3},{4,20},{20... | collective-permute-start | bytes 2359304 | tf_op jit(solution)/shard_map/ppermute | solution.py:111
  237.4 97.1 %collective-permute-start.24 = (bf16[512,1024]{1,0:T(8,128)(2,1)S(1)}, bf16[512,1024]{1,0:T(8,128)(2,1)S(1)}, u32[]{:S(2)}, u32[]{:S(2)}) collective-permute-start(bf16[512,1024]{1,0:T(8,128)(2,1)S(1)} %bitcast.351), channel_id=1, source_target_pairs={{0,1},{1,0},{2,3},{3,2},{4,5},{5,4},{6,7},{7,6},{8,9},{9,8},{10,11... | collective-permute-start | bytes 3145736 | tf_op jit(solution)/shard_map/ppermute | solution.py:111
  238.7 92.6 %collective-permute-start.48 = (bf16[1,2,128,1024]{3,2,1,0:T(8,128)(2,1)S(1)}, bf16[1,2,128,1024]{3,2,1,0:T(8,128)(2,1)S(1)}, u32[]{:S(2)}, u32[]{:S(2)}) collective-permute-start(bf16[1,2,128,1024]{3,2,1,0:T(8,128)(2,1)S(1)} %pad_maximum_fusion.64), channel_id=1, source_target_pairs={{0,4},{1,5},{2,6},{3,7},{4,0},{5,1},{6,2},{7,3},{8,12},{9,13},{10,... | collective-permute-start | bytes 1572872 | tf_op jit(solution)/shard_map/ppermute | solution.py:111
  240.2 92.5 %collective-permute-start.51 = (bf16[2,1,128,1024]{3,2,1,0:T(8,128)(2,1)S(1)}, bf16[2,1,128,1024]{3,2,1,0:T(8,128)(2,1)S(1)}, u32[]{:S(2)}, u32[]{:S(2)}) collective-permute-start(bf16[2,1,128,1024]{3,2,1,0:T(8,128)(2,1)S(1)} %pad_maximum_fusion.65), channel_id=1, source_target_pairs={{0,2},{1,3},{2,0},{3,1},{4,6},{5,7},{6,4},{7,5},{8,10},{9,11},{10,... | collective-permute-start | bytes 1572872 | tf_op jit(solution)/shard_map/ppermute | solution.py:111
  332.7 28.3 %collective-permute-start.42 = (bf16[512,1024]{1,0:T(8,128)(2,1)S(1)}, bf16[512,1024]{1,0:T(8,128)(2,1)S(1)}, u32[]{:S(2)}, u32[]{:S(2)}) collective-permute-start(bf16[512,1024]{1,0:T(8,128)(2,1)S(1)} %bitcast.348), channel_id=1, source_target_pairs={{0,1},{1,0},{2,3},{3,2},{4,5},{5,4},{6,7},{7,6},{8,9},{9,8},{10,11... | collective-permute-start | bytes 3145736 | tf_op jit(solution)/shard_map/ppermute | solution.py:111
  349.5 32.7 %collective-permute-start.33 = (bf16[512,1024]{1,0:T(8,128)(2,1)S(1)}, bf16[512,1024]{1,0:T(8,128)(2,1)S(1)}, u32[]{:S(2)}, u32[]{:S(2)}) collective-permute-start(bf16[512,1024]{1,0:T(8,128)(2,1)S(1)} %convolution_convert_fusion.3), channel_id=1, source_target_pairs={{0,1},{1,0},{2,3},{3,2},{4,5},{5,4},{6,7},{7,6},{8,9},{9,8},{10,11... | collective-permute-start | bytes 3145736 | tf_op jit(solution)/shard_map/ppermute | solution.py:111
  376.8 120.8 %collective-permute-start.85 = (bf16[1024,768]{1,0:T(8,128)(2,1)}, bf16[1024,768]{1,0:T(8,128)(2,1)}, u32[]{:S(2)}, u32[]{:S(2)}) collective-permute-start(bf16[1024,768]{1,0:T(8,128)(2,1)} %add_convert_fusion.1), channel_id=1, source_target_pairs={{0,16},{16,0},{1,17},{17,1},{2,18},{18,2},{3,19},{19,3},{4,20},{20... | collective-permute-start | bytes 4718600 | tf_op jit(solution)/shard_map/ppermute | solution.py:111
  386.2 27.7 %collective-permute-start.37 = (bf16[1,2,128,1024]{3,2,1,0:T(8,128)(2,1)S(1)}, bf16[1,2,128,1024]{3,2,1,0:T(8,128)(2,1)S(1)}, u32[]{:S(2)}, u32[]{:S(2)}) collective-permute-start(bf16[1,2,128,1024]{3,2,1,0:T(8,128)(2,1)S(1)} %bitcast.373), channel_id=1, source_target_pairs={{0,4},{1,5},{2,6},{3,7},{4,0},{5,1},{6,2},{7,3},{8,12},{9,13},{10,... | collective-permute-start | bytes 1572872 | tf_op jit(solution)/shard_map/ppermute | solution.py:111
  401.0 28.1 %collective-permute-start.35 = (bf16[1,1,128,1024]{3,2,1,0:T(8,128)(2,1)S(1)}, bf16[1,1,128,1024]{3,2,1,0:T(8,128)(2,1)S(1)}, u32[]{:S(2)}, u32[]{:S(2)}) collective-permute-start(bf16[1,1,128,1024]{3,2,1,0:T(8,128)(2,1)S(1)} %slice.1102), channel_id=1, source_target_pairs={{0,4},{1,5},{2,6},{3,7},{4,0},{5,1},{6,2},{7,3},{8,12},{9,13},{10,... | collective-permute-start | bytes 786440 | tf_op jit(solution)/shard_map/ppermute | solution.py:111
  428.7 53.3 %collective-permute-start.86 = (bf16[1024,384]{1,0:T(8,128)(2,1)S(1)}, bf16[1024,384]{1,0:T(8,128)(2,1)S(1)}, u32[]{:S(2)}, u32[]{:S(2)}) collective-permute-start(bf16[1024,384]{1,0:T(8,128)(2,1)S(1)} %add_convert_fusion.3), channel_id=1, source_target_pairs={{0,16},{16,0},{1,17},{17,1},{2,18},{18,2},{3,19},{19,3},{4,20},{20... | collective-permute-start | bytes 2359304 | tf_op jit(solution)/shard_map/ppermute | solution.py:111
  459.8 31.6 %collective-permute-start.61 = (bf16[1,2,128,1024]{3,2,1,0:T(8,128)(2,1)}, bf16[1,2,128,1024]{3,2,1,0:T(8,128)(2,1)}, u32[]{:S(2)}, u32[]{:S(2)}) collective-permute-start(bf16[1,2,128,1024]{3,2,1,0:T(8,128)(2,1)} %pad_maximum_fusion.67), channel_id=1, source_target_pairs={{0,4},{1,5},{2,6},{3,7},{4,0},{5,1},{6,2},{7,3},{8,12},{9,13},{10,... | collective-permute-start | bytes 1572872 | tf_op jit(solution)/shard_map/ppermute | solution.py:111
  503.0 93.5 %all-to-all-start.5 = ((bf16[16,64,768]{2,1,0:T(8,128)(2,1)}), bf16[16,64,768]{2,1,0:T(8,128)(2,1)}, u32[]{:S(2)}, u32[]{:S(2)}) async-start(bf16[16,64,768]{2,1,0:T(8,128)(2,1)} %bitcast.322), calls=%async_computation.7 | async-start | bytes 3145728 | tf_op jit(solution)/shard_map/all_to_all | solution.py:224
  508.1 176.3 %reduce-scatter.5.cloned.1.call-start = ((), (), s32[]{:S(2)}) async-start(), calls=%async_computation.12 | async-start | bytes 1310720 | tf_op jit(solution)/shard_map/reduce_scatter | solution.py:392
  524.3 44.9 %collective-permute-start.94 = (f32[272,128]{1,0:T(8,128)S(1)}, f32[272,128]{1,0:T(8,128)}, u32[]{:S(2)}, u32[]{:S(2)}) collective-permute-start(f32[272,128]{1,0:T(8,128)S(1)} %reshape.652), channel_id=1, source_target_pairs={{0,1},{1,0},{2,3},{3,2},{4,5},{5,4},{6,7},{7,6},{8,9},{9,8},{10,11... | collective-permute-start | bytes 417800 | tf_op jit(solution)/shard_map/ppermute | solution.py:111
  540.4 154.3 %reduce-scatter.3.cloned.1.call-start = ((), (), s32[]{:S(2)}) async-start(), calls=%async_computation.11 | async-start | bytes 2621440 | tf_op jit(solution)/shard_map/reduce_scatter | solution.py:392
  554.9 62.3 %collective-permute-start.82 = (bf16[512,1024]{1,0:T(8,128)(2,1)}, bf16[512,1024]{1,0:T(8,128)(2,1)}, u32[]{:S(2)}, u32[]{:S(2)}) collective-permute-start(bf16[512,1024]{1,0:T(8,128)(2,1)} %convolution_convert_fusion.6), channel_id=1, source_target_pairs={{0,1},{1,0},{2,3},{3,2},{4,5},{5,4},{6,7},{7,6},{8,9},{9,8},{10,11... | collective-permute-start | bytes 3145736 | tf_op jit(solution)/shard_map/ppermute | solution.py:111
  556.8 57.5 %collective-permute-start.75 = (bf16[512,1024]{1,0:T(8,128)(2,1)}, bf16[512,1024]{1,0:T(8,128)(2,1)}, u32[]{:S(2)}, u32[]{:S(2)}) collective-permute-start(bf16[512,1024]{1,0:T(8,128)(2,1)} %convolution_convert_fusion.8), channel_id=1, source_target_pairs={{0,1},{1,0},{2,3},{3,2},{4,5},{5,4},{6,7},{7,6},{8,9},{9,8},{10,11... | collective-permute-start | bytes 3145736 | tf_op jit(solution)/shard_map/ppermute | solution.py:111
  576.4 45.2 %collective-permute-start.69 = (bf16[512,1024]{1,0:T(8,128)(2,1)}, bf16[512,1024]{1,0:T(8,128)(2,1)}, u32[]{:S(2)}, u32[]{:S(2)}) collective-permute-start(bf16[512,1024]{1,0:T(8,128)(2,1)} %convolution_convert_fusion.10), channel_id=1, source_target_pairs={{0,1},{1,0},{2,3},{3,2},{4,5},{5,4},{6,7},{7,6},{8,9},{9,8},{10,11... | collective-permute-start | bytes 3145736 | tf_op jit(solution)/shard_map/ppermute | solution.py:111
  636.0 28.8 %collective-permute-start.67 = (bf16[2,1,128,1024]{3,2,1,0:T(8,128)(2,1)S(1)}, bf16[2,1,128,1024]{3,2,1,0:T(8,128)(2,1)S(1)}, u32[]{:S(2)}, u32[]{:S(2)}) collective-permute-start(bf16[2,1,128,1024]{3,2,1,0:T(8,128)(2,1)S(1)} %slice.1086), channel_id=1, source_target_pairs={{0,2},{1,3},{2,0},{3,1},{4,6},{5,7},{6,4},{7,5},{8,10},{9,11},{10,... | collective-permute-start | bytes 1572872 | tf_op jit(solution)/shard_map/ppermute | solution.py:111
  643.8 34.7 %collective-permute-start.81 = (bf16[1,1,128,1024]{3,2,1,0:T(8,128)(2,1)S(1)}, bf16[1,1,128,1024]{3,2,1,0:T(8,128)(2,1)S(1)}, u32[]{:S(2)}, u32[]{:S(2)}) collective-permute-start(bf16[1,1,128,1024]{3,2,1,0:T(8,128)(2,1)S(1)} %slice.1094), channel_id=1, source_target_pairs={{0,4},{1,5},{2,6},{3,7},{4,0},{5,1},{6,2},{7,3},{8,12},{9,13},{10,... | collective-permute-start | bytes 786440 | tf_op jit(solution)/shard_map/ppermute | solution.py:111
  (255 other events, 2875.5 us)
Sparse Core Ops, SparseCore 0:
  37.9 51.5 all-gather.2
  91.0 30.4 all-gather.4
  540.5 26.4 reduce-scatter.4
  569.8 51.3 reduce-scatter.2

commit v3 on v1

v3 whole, which is shorter than its diff:
```python
import functools

import jax
import jax.numpy as jnp
from jax import lax
from jax.experimental import pallas as pl
from jax.experimental.pallas import tpu as pltpu
from jax.sharding import PartitionSpec as P

HEADS = 16
KV_HEADS = 8
HEAD_DIM = 128
FF = 6144
TOK_DEV = 128
STEP = 5
QUERY_ROWS = 256
KERNEL_VMEM = 40 * 2**20

eps = 1e-06
theta = 1000000.0
beta_one = 0.5
beta_two = 0.5
rate = 0.02
decay = 0.1
adam_eps = 1e-08
contract_cols = (((1,), (1,)), ((), ()))
contract_rows = (((0,), (0,)), ((), ()))
f32 = jnp.float32
bf16 = jnp.bfloat16


def dot(a, b):
    return jnp.dot(a, b, preferred_element_type=f32)


def dot_nt(a, b):
    return lax.dot_general(a, b, contract_cols, preferred_element_type=f32)


def dot_tn(a, b):
    return lax.dot_general(a, b, contract_rows, preferred_element_type=f32)


def token_info(stored, doc_lengths, groups):
    half = TOK_DEV // 2
    device = stored // TOK_DEV
    within = stored % TOK_DEV
    section = jnp.where(within < half, device, 2 * groups - 1 - device)
    place = section * half + within % half
    ends = jnp.cumsum(doc_lengths)
    segment = jnp.sum((place[:, None] >= ends[None, :]).astype(jnp.int32), axis=1)
    starts = ends - doc_lengths
    picked = segment[:, None] == jnp.arange(doc_lengths.shape[0], dtype=jnp.int32)[None, :]
    begin = jnp.sum(jnp.where(picked, starts[None, :], 0), axis=1)
    return (place, segment, place - begin)


def rms_factor(values):
    return lax.rsqrt(jnp.mean(values * values, axis=-1, keepdims=True) + eps)


def rms(values):
    return values * rms_factor(values)


def norm_back(values, grads):
    factor = rms_factor(values)
    normed = values * factor
    return factor * (grads - normed * jnp.mean(grads * normed, axis=-1, keepdims=True))


def rotary(position):
    half = HEAD_DIM // 2
    freq = theta ** (-jnp.arange(half, dtype=f32) * 2.0 / HEAD_DIM)
    angle = position.astype(f32)[:, None] * freq[None, :]
    cosine, sine = jnp.cos(angle), jnp.sin(angle)
    return (
        jnp.concatenate([cosine, cosine], axis=1),
        jnp.concatenate([-sine, sine], axis=1),
    )


def swap_halves(values):
    return pltpu.roll(values, HEAD_DIM // 2, 1)


def turn(values, cosine, sine):
    return values * cosine + swap_halves(values) * sine


def turn_back(grads, cosine, sine):
    return grads * cosine - swap_halves(grads) * sine


def adam(weight, first, second, grad):
    first_new = beta_one * first + (1.0 - beta_one) * grad
    second_new = beta_two * second + (1.0 - beta_two) * grad * grad
    fix_one = 1.0 - beta_one**STEP
    fix_two = 1.0 - beta_two**STEP
    weight_new = weight - rate * (
        first_new / fix_one / (jnp.sqrt(second_new / fix_two) + adam_eps) + decay * weight
    )
    return (first_new, second_new, weight_new, weight_new.astype(bf16))


def head(index):
    return slice(index * HEAD_DIM, (index + 1) * HEAD_DIM)


def key_blocks(own_q, own_kv):
    return [(g, own_q + g, own_q + own_kv + g) for g in range(own_kv)]


def query_blocks(length):
    size = min(length, QUERY_ROWS)
    return [slice(start, start + size) for start in range(0, length, size)]


def allowed_keys(spots, spot_row, rows):
    return (spot_row[:, :] <= spots[rows, 0:1]) & (spot_row[:, :] >= spots[rows, 1:2])


def attend_kernel(
    own_q, own_kv, proj, sig, cosine, sine, spots, spot_row, gains,
    gated, heads, tops, queries, keys, values,
):
    scale = HEAD_DIM ** (-0.5)
    for g, key, value in key_blocks(own_q, own_kv):
        normed = rms(proj[:, head(key)]) * (1.0 + gains[1:2, :])
        keys[:, head(g)] = turn(normed, cosine[:, :], sine[:, :]).astype(bf16)
        values[:, head(g)] = proj[:, head(value)].astype(bf16)
    for rows in query_blocks(proj.shape[0]):
        allowed = allowed_keys(spots, spot_row, rows)
        for h in range(own_q):
            g = h * own_kv // own_q
            normed = rms(proj[rows, head(h)]) * (1.0 + gains[0:1, :])
            query = turn(normed, cosine[rows, :], sine[rows, :]).astype(bf16)
            queries[rows, head(h)] = query
            scores = jnp.where(allowed, dot_nt(query, keys[:, head(g)]) * scale, -1e30)
            top = jnp.max(scores, axis=-1, keepdims=True)
            weights = jnp.exp(scores - top)
            total = jnp.sum(weights, axis=-1, keepdims=True)
            probs = (weights * (1.0 / total)).astype(bf16)
            out = dot(probs, values[:, head(g)])
            heads[rows, head(h)] = out
            tops[rows, h : h + 1] = top + jnp.log(total)
            gated[rows, head(h)] = (out * sig[rows, h : h + 1]).astype(bf16)


def attend_back_kernel(
    own_q, own_kv, proj, sig, cosine, sine, spots, spot_row, gains, heads, tops, queries, keys,
    values, grad_gated, grad_proj, grad_logits, gain_terms, grad_keys, grad_values,
):
    scale = HEAD_DIM ** (-0.5)
    grad_keys[:, :] = jnp.zeros(grad_keys.shape, f32)
    grad_values[:, :] = jnp.zeros(grad_values.shape, f32)
    query_term = jnp.zeros((1, HEAD_DIM), f32)
    key_term = jnp.zeros((1, HEAD_DIM), f32)
    for rows in query_blocks(proj.shape[0]):
        allowed = allowed_keys(spots, spot_row, rows)
        for h in range(own_q):
            g = h * own_kv // own_q
            gate = sig[rows, h : h + 1]
            back = grad_gated[rows, head(h)]
            out = heads[rows, head(h)]
            grad_sig = jnp.sum(back * out, axis=-1, keepdims=True)
            grad_logits[rows, h : h + 1] = grad_sig * gate * (1.0 - gate)
            grad_head = (back * gate).astype(bf16)
            delta = jnp.sum(grad_head.astype(f32) * out, axis=-1, keepdims=True)
            query = queries[rows, head(h)]
            scores = dot_nt(query, keys[:, head(g)]) * scale
            probs = jnp.exp(jnp.where(allowed, scores - tops[rows, h : h + 1], -1e30))
            grad_probs = dot_nt(grad_head, values[:, head(g)])
            grad_scores = (probs * (grad_probs - delta)).astype(bf16)
            grad_keys[:, head(g)] += dot_tn(grad_scores, query)
            grad_values[:, head(g)] += dot_tn(probs.astype(bf16), grad_head)
            grad_qn = turn_back(
                dot(grad_scores, keys[:, head(g)]) * scale, cosine[rows, :], sine[rows, :]
            )
            raw = proj[rows, head(h)]
            query_term += jnp.sum(grad_qn * rms(raw), axis=0, keepdims=True)
            grad_proj[rows, head(h)] = norm_back(raw, grad_qn * (1.0 + gains[0:1, :])).astype(bf16)
    for g, key, value in key_blocks(own_q, own_kv):
        grad_kn = turn_back(grad_keys[:, head(g)] * scale, cosine[:, :], sine[:, :])
        raw = proj[:, head(key)]
        key_term += jnp.sum(grad_kn * rms(raw), axis=0, keepdims=True)
        grad_proj[:, head(key)] = norm_back(raw, grad_kn * (1.0 + gains[1:2, :])).astype(bf16)
        grad_proj[:, head(value)] = grad_values[:, head(g)].astype(bf16)
    gain_terms[0:1, :] = query_term
    gain_terms[1:2, :] = key_term


def call_kernel(kernel, shapes, scratch, *args):
    spec = pl.BlockSpec(memory_space=pltpu.VMEM)
    return pl.pallas_call(
        kernel,
        out_shape=[jax.ShapeDtypeStruct(shape, dtype) for shape, dtype in shapes],
        in_specs=[spec] * len(args),
        out_specs=[spec] * len(shapes),
        scratch_shapes=scratch,
        compiler_params=pltpu.CompilerParams(vmem_limit_bytes=KERNEL_VMEM),
        cost_estimate=pl.CostEstimate(flops=10**7, bytes_accessed=10**5, transcendentals=0),
    )(*args)


def attend(own_q, own_kv, proj, sig, *info):
    length = proj.shape[0]
    wide, narrow = (length, own_q * HEAD_DIM), (length, own_kv * HEAD_DIM)
    shapes = [(wide, bf16), (wide, f32), ((length, own_q), f32), (wide, bf16)]
    shapes += [(narrow, bf16), (narrow, bf16)]
    kernel = functools.partial(attend_kernel, own_q, own_kv)
    return call_kernel(kernel, shapes, [], proj, sig, *info)


def attend_back(own_q, own_kv, *args):
    length, width = args[0].shape
    shapes = [((length, width), bf16), ((length, own_q), f32), ((2, HEAD_DIM), f32)]
    scratch = [pltpu.VMEM((length, own_kv * HEAD_DIM), f32)] * 2
    kernel = functools.partial(attend_back_kernel, own_q, own_kv)
    return call_kernel(kernel, shapes, scratch, *args)


def tie(*values):
    return lax.optimization_barrier(values)


def shift(value, axis, offset):
    return lax.ppermute(value, axis, [(i, i ^ offset) for i in range(lax.axis_size(axis))])


def cp_offsets(groups):
    return list(range(0, groups, 2)) + list(range(1, groups, 2))


def far_first(groups):
    return sorted(range(2, groups, 2), key=lambda offset: -offset.bit_count())


def gather_chips(value):
    groups = lax.axis_size("cp")
    came = {offset: shift(value, "cp", offset) for offset in far_first(groups)}
    return [value] + [came[offset] for offset in range(2, groups, 2)]


def gather_cores(parts):
    same = jnp.concatenate(parts, axis=0)
    return jnp.concatenate([same, shift(same, "cp", 1)], axis=0)


def gather_cp(value):
    return gather_cores(gather_chips(value))


def scatter_first(left, weights):
    half = left.shape[0] // 2
    return left[:half], dot_nt(left[half:], weights).astype(bf16)


def scatter_rest(left, weights, started):
    groups = lax.axis_size("cp")
    rows = left.shape[0] * 2 // groups
    part = dot_nt(left, weights) + shift(started, "cp", 1).astype(f32)
    total = part[:rows]
    low = part[rows:].astype(bf16)
    for offset in far_first(groups):
        place = (offset // 2 - 1) * rows
        total = total + shift(low[place : place + rows], "cp", offset).astype(f32)
    return total


def scatter_cp(left, weights):
    kept, started = scatter_first(left, weights)
    return scatter_rest(kept, weights, started)


def sum_shifts(value, axis, step):
    shifts = range(step, lax.axis_size(axis), step)
    return sum((shift(value, axis, offset) for offset in shifts), start=value)


def sum_cp(value):
    return sum_shifts(value + shift(value, "cp", 1), "cp", 2)


def sum_dp(value):
    return sum_shifts(value, "dp", 1)


def squares_of(value):
    value = value.astype(f32)
    return jnp.sum(value * value)


def local(
    tokens,
    cotangent,
    lengths,
    big_weight,
    big_first,
    big_second,
    small_weight,
    small_first,
    small_second,
    qk_gain,
    qk_first,
    qk_second,
):
    groups = lax.axis_size("cp")
    planes = lax.axis_size("dp")
    me = lax.axis_index("cp")
    owner = lax.axis_index("dp") * groups + me
    wr = big_weight.shape[0]
    rows, features = tokens.shape[1:]
    width_attn = HEADS * HEAD_DIM
    width_kv = KV_HEADS * HEAD_DIM
    width_qkv = width_attn + 2 * width_kv
    start_mlp = width_qkv + width_attn
    start_down = start_mlp + 2 * FF
    own_q = HEADS // groups
    own_kv = max(1, KV_HEADS // groups)
    copies = max(1, groups // KV_HEADS)
    wq = own_q * HEAD_DIM
    wkv = own_kv * HEAD_DIM
    win = wq + 2 * wkv
    wff = FF // groups

    def blocks(start, width, repeat=1):
        part = big_weight[:, start : start + width].astype(bf16)
        part = part.reshape(wr, groups // repeat, -1).transpose(1, 0, 2)
        return jnp.repeat(part, repeat, axis=0) if repeat > 1 else part

    def exchange(part):
        return lax.all_to_all(part, "cp", 0, 0, tiled=True)

    def sum_rows(part):
        return lax.psum_scatter(part, "dp", scatter_dimension=0, tiled=True)

    def to_columns(part):
        return exchange(part).reshape(groups * wr, -1)

    attn_blocks = jnp.concatenate(
        [
            blocks(0, width_attn),
            blocks(width_attn, width_kv, copies),
            blocks(width_attn + width_kv, width_kv, copies),
            blocks(width_qkv, width_attn),
        ],
        axis=2,
    )
    attn_rows = to_columns(attn_blocks)
    gu_blocks = jnp.concatenate([blocks(start_mlp, FF), blocks(start_mlp + FF, FF)], axis=2)
    gu_blocks, attn_rows = tie(gu_blocks, attn_rows)
    attn_w = lax.all_gather(attn_rows, "dp", axis=0, tiled=True)
    gu_rows = to_columns(gu_blocks)
    down_blocks, gu_rows = tie(blocks(start_down, FF), gu_rows)
    down_rows = to_columns(down_blocks)

    small_place = lax.dynamic_update_slice_in_dim(
        jnp.zeros((HEADS + 2, features), bf16), small_weight.astype(bf16).T, owner * wr, 1
    ).reshape(-1, 128)
    own_tokens, small_full = tie(tokens[0], sum_cp(small_place))
    small_full = sum_dp(small_full).reshape(HEADS + 2, features)
    gate_w = lax.dynamic_slice_in_dim(small_full, me * own_q, own_q, 0).T
    gain_one = 1.0 + small_full[HEADS].astype(f32)
    gain_two = 1.0 + small_full[HEADS + 1].astype(f32)

    doc_lengths = lengths[0]
    offsets = jnp.array(cp_offsets(groups), jnp.int32)
    stored = ((me ^ offsets)[:, None] * rows + jnp.arange(rows, dtype=jnp.int32)).reshape(-1)
    place, segment, position = token_info(stored, doc_lengths, groups)
    cosine, sine = rotary(position)
    spots = jnp.stack([place, place - position], axis=1)
    info = (cosine, sine, spots, place[None, :], qk_gain)

    own_branch, gu_rows, *tokens_all = tie(cotangent[0], gu_rows, *gather_chips(own_tokens))
    gu_w = lax.all_gather(gu_rows, "dp", axis=0, tiled=True)
    tokens_all = gather_cores(tokens_all)
    kept_one = (rms(tokens_all.astype(f32)) * gain_one).astype(bf16)

    sig = jax.nn.sigmoid(dot(kept_one, gate_w))
    kept_one, down_rows = tie(kept_one, down_rows)
    down_w = lax.all_gather(down_rows, "dp", axis=0, tiled=True)
    grad_branch = gather_chips(own_branch)
    proj = dot(kept_one, attn_w[:, :win])
    gated, heads, tops, queries, keys, values = attend(own_q, own_kv, proj, sig, *info)
    inputs = tokens[0].astype(f32)
    gated, *grad_branch = tie(gated, *grad_branch)
    grad_branch = gather_cores(grad_branch)
    middle = inputs + scatter_cp(gated, attn_w[:, win:])

    normed_two = rms(middle)
    kept_two = gather_cp((normed_two * gain_two).astype(bf16))
    gate_up = dot(kept_two, gu_w)
    gate, upper = gate_up[:, :wff], gate_up[:, wff:]
    sig_gate = jax.nn.sigmoid(gate)
    hidden = (gate * sig_gate * upper).astype(bf16)
    down_grad, grad_branch = tie(dot_tn(grad_branch, hidden).astype(bf16), grad_branch)
    down_term = sum_rows(down_grad)
    grad_hidden = dot(grad_branch, down_w)
    grad_gate = grad_hidden * upper * sig_gate * (1.0 + gate * (1.0 - sig_gate))
    grad_upper = grad_hidden * gate * sig_gate
    grad_gu = jnp.concatenate([grad_gate, grad_upper], axis=1).astype(bf16)

    left, started = scatter_first(grad_gu, gu_w)
    late_gu, started = tie(grad_gu, started)
    gu_grad, left = tie(dot_tn(kept_two, late_gu).astype(bf16), left)
    gu_term = sum_rows(gu_grad)
    grad_two = scatter_rest(left, gu_w, started)
    gain_two_term = jnp.sum(grad_two * normed_two, axis=0)
    grad_out = cotangent[0].astype(f32)
    grad_middle = grad_out + norm_back(middle, grad_two * gain_two)

    grad_middle, hidden, down_term = tie(grad_middle, hidden, down_term)
    grad_attn_branch = gather_cp(grad_middle.astype(bf16))
    left, started = scatter_first(hidden, down_w)
    left, grad_attn_branch, started = tie(left, grad_attn_branch, started)
    result = middle + scatter_rest(left, down_w, started)
    grad_gated = dot(grad_attn_branch, attn_w[:, win:])
    grad_proj, grad_logits, qk_terms = attend_back(
        own_q, own_kv, proj, sig, *info, heads, tops, queries, keys, values, grad_gated
    )
    grad_logits = grad_logits.astype(bf16)
    attn_grad = jnp.concatenate(
        [dot_tn(kept_one, grad_proj), dot_tn(grad_attn_branch, gated)], axis=1
    ).astype(bf16)
    attn_grad, late_proj, gu_term = tie(attn_grad, grad_proj, gu_term)
    attn_term = sum_rows(attn_grad)
    gate_term = dot_tn(kept_one, grad_logits)
    full_in = jnp.concatenate([attn_w[:, :win], gate_w], axis=1)
    grad_all = jnp.concatenate([late_proj, grad_logits], axis=1)
    grad_one = scatter_cp(grad_all, full_in)
    gain_one_term = jnp.sum(grad_one * rms(inputs), axis=0)
    grad_input = grad_middle + norm_back(inputs, grad_one * gain_one)

    gate_place = lax.dynamic_update_slice_in_dim(
        jnp.zeros((HEADS, features), f32), gate_term.T, me * own_q, 0
    )
    def kv_sum(part):
        if copies == 1:
            return part
        return part.astype(f32).reshape(groups // copies, copies, wr, -1).sum(axis=1)

    def wide(part):
        return part.transpose(1, 0, 2).reshape(wr, -1).astype(f32)

    def to_owner(part):
        return exchange(part.reshape(groups, wr, -1))

    down_own = to_owner(down_term)
    gu_term, down_own = tie(gu_term, down_own)
    gu_own = to_owner(gu_term)
    attn_term, result, grad_input, gain_one_term, down_own, gu_own = tie(
        attn_term, result, grad_input, gain_one_term, down_own, gu_own
    )
    attn_own = to_owner(attn_term)
    k_own = kv_sum(attn_own[:, :, wq : wq + wkv])
    v_own = kv_sum(attn_own[:, :, wq + wkv : win])
    if copies == 1:
        attn_squares = squares_of(attn_term)
    else:
        attn_squares = squares_of(attn_term[:, :wq]) + squares_of(attn_term[:, win:])
        attn_squares = attn_squares + squares_of(k_own) + squares_of(v_own)
    local_squares = squares_of(down_term) + squares_of(gu_term) + attn_squares
    small_term = jnp.concatenate([gate_place, gain_one_term[None], gain_two_term[None]], axis=0)
    last_small = sum_dp(
        sum_cp(
            jnp.concatenate(
                [small_term.reshape(-1, 128), qk_terms, jnp.full((1, 128), local_squares, f32)],
                axis=0,
            )
        )
    )
    tall = (HEADS + 2) * features // 128
    qk_grad = last_small[tall : tall + 2]
    total = last_small[tall + 2, 0] + squares_of(last_small[: tall + 2])
    norm_value = jnp.sqrt(total)
    factor = jnp.minimum(1.0, 1.0 / (norm_value + 1e-06))
    small_grad = lax.dynamic_slice_in_dim(
        last_small[:tall].reshape(HEADS + 2, features), owner * wr, wr, 1
    ).T
    big_grad = jnp.concatenate(
        [
            wide(attn_own[:, :, :wq]),
            wide(k_own),
            wide(v_own),
            wide(attn_own[:, :, win:]),
            wide(gu_own[:, :, :wff]),
            wide(gu_own[:, :, wff:]),
            wide(down_own),
        ],
        axis=1,
    )
    big_out = adam(big_weight, big_first, big_second, big_grad * factor)
    small_out = adam(small_weight, small_first, small_second, small_grad * factor)
    qk_out = adam(qk_gain, qk_first, qk_second, qk_grad * factor)
    gain_grads = small_grad[:, HEADS:] * factor
    return (
        result.astype(bf16)[None],
        grad_input.astype(bf16)[None],
        *big_out,
        *small_out,
        *qk_out,
        gain_grads,
        norm_value,
    )


def solution(mesh):
    rows = P(("dp", "cp"), None)
    row_tokens = P("dp", "cp", None)
    return jax.shard_map(
        local,
        mesh=mesh,
        in_specs=(row_tokens, row_tokens, P("dp", None)) + (rows,) * 6 + (P(),) * 3,
        out_specs=(row_tokens, row_tokens) + (rows,) * 8 + (P(),) * 4 + (rows, P()),
        check_vma=False,
    )
```

time: 730 us -> 626 us (0.86)
  other arithmetic: 111 us -> 55.2 us
  blocking collectives: 47.8 us -> 0 us
  Pallas kernels: 0 us -> 18.5 us
  waiting for transfers between devices: 301 us -> 319 us
  local copies, waits for them, and re-layouts: 65.2 us -> 47.4 us
  matrix products: 99.3 us -> 87.2 us
    ppermute x50 -> x46, waiting for transfers between devices: 108 us -> 193 us  [shift(): lax.ppermute(value, axis, [(i, i ^ offset) for i in range(lax.axis_size(a...]
    reduce_scatter x3, waiting for transfers between devices: 108 us -> 53.2 us  [sum_rows(): return lax.psum_scatter(part, 'dp', scatter_dimension=0, tiled=True)]
    all_gather x1 -> x0, blocking collectives: 47.8 us -> none  [local(): lax.all_gather(small_weight.astype(bf16).T, ('dp', 'cp'), axis=0)]
    pallas_call x0 -> x2, Pallas kernels: none -> 18.5 us  [call_kernel(): pl.pallas_call(kernel, out_shape=[jax.ShapeDtypeStruct(shape, dtype) for...]
    slice x42 -> x9, local copies, waits for them, and re-layouts: 23.1 us -> 5.19 us  [the longest x4 2.7 us: scatter_rest(): total = total + shift(low[place:place + rows], 'cp', offset).astype(f32)]
    convert_element_type x9 -> x3, other arithmetic: 21.1 us -> 4.01 us  [the longest x1 3.03 us: local(): kept_one = (rms(tokens_all.astype(f32)) * gain_one).astype(bf16)]
    concatenate x28 -> x10, other arithmetic: 23.5 us -> 11.6 us  [the longest x4 7.74 us: gather_cores(): same = jnp.concatenate(parts, axis=0)]
    dot_general x9 -> x5, matrix products: 43.3 us -> 31.5 us  [dot(): return jnp.dot(a, b, preferred_element_type=f32)]
  transfers between devices with their start and end apart: 62 -> 58, of which waited for: 28 -> 30; matrix products, arithmetic and copies ran while one was open for 27% -> 26% of each run, Pallas kernels for 0% -> 3%
where the time goes in v3:
time: 626 us; the launch traced here: 619 us
  waiting for transfers between devices  319 us (51%)
  matrix products  87.2 us (14%)
  starting transfers between devices  71.1 us (11%)
  other arithmetic  55.2 us (9%)
  local copies, waits for them, and re-layouts  47.4 us (8%)
  between operations  20.5 us (3%)
  Pallas kernels  18.5 us (3%)
    ppermute x46, waiting for transfers between devices, shift(): lax.ppermute(value, axis, [(i, i ^ offset) for i in range(lax.axis_size(a...  193 us
    reduce_scatter x3, waiting for transfers between devices, sum_rows(): return lax.psum_scatter(part, 'dp', scatter_dimension=0, tiled=True)  53.2 us
    ppermute x46, starting transfers between devices, shift(): lax.ppermute(value, axis, [(i, i ^ offset) for i in range(lax.axis_size(a...  45.5 us
    all_gather x1, waiting for transfers between devices, local(): down_w = lax.all_gather(down_rows, 'dp', axis=0, tiled=True)  42.8 us
    dot_general x8, matrix products, dot_nt(): return lax.dot_general(a, b, contract_cols, preferred_element_type=f32)  32.9 us
    dot_general x5, matrix products, dot(): return jnp.dot(a, b, preferred_element_type=f32)  31.5 us
    all_to_all x6, waiting for transfers between devices, exchange(): return lax.all_to_all(part, 'cp', 0, 0, tiled=True)  27.4 us
    all_to_all x6, starting transfers between devices, exchange(): return lax.all_to_all(part, 'cp', 0, 0, tiled=True)  24.8 us
  transfers between devices with their start and end apart: 58, of which 30 were waited for; matrix products, arithmetic and copies ran while one was open for 26% of the time, Pallas kernels for 3%

profile of v3, /device:TPU:0, one launch (start us, length us, event | category | flops | bytes accessed | tf_op | source)
XLA Modules:
  0.0 618.6 jit_solution(17935859803692729031)
XLA Ops:
  11.6 5.2 all-to-all-start
  18.4 11.1 %all-to-all-done = bf16[8,64,768]{2,1,0:T(8,128)(2,1)} async-done(((bf16[8,64,768]{2,1,0:T(8,128)(2,1)}), bf16[8,64,768]{2,1,0:T(8,128)(2,1)}, u32[]{:S(2)}, u32[]{:S(2)}) %all-to-all-start) | async-done | bytes 786464 | tf_op jit(solution)/shard_map/all_to_all | solution.py:333
  40.3 18.3 %collective-permute-done.1 = bf16[288,128]{1,0:T(8,128)(2,1)S(1)} collective-permute-done((bf16[288,128]{1,0:T(8,128)(2,1)S(1)}, bf16[288,128]{1,0:T(8,128)(2,1)S(1)}, u32[]{:S(2)}, u32[]{:S(2)}) %collective-permute-start.1) | collective-permute-done | bytes 73760 | tf_op jit(solution)/shard_map/ppermute | solution.py:228
  65.5 10.1 %collective-permute-done.4 = bf16[128,2048]{1,0:T(8,128)(2,1)S(1)} collective-permute-done((bf16[128,2048]{1,0:T(8,128)(2,1)S(1)}, bf16[128,2048]{1,0:T(8,128)(2,1)S(1)}, u32[]{:S(2)}, u32[]{:S(2)}) %collective-permute-start.4) | collective-permute-done | bytes 524320 | tf_op jit(solution)/shard_map/ppermute | solution.py:228
  75.6 10.2 %collective-permute-done.5 = bf16[128,2048]{1,0:T(8,128)(2,1)S(1)} collective-permute-done((bf16[128,2048]{1,0:T(8,128)(2,1)S(1)}, bf16[128,2048]{1,0:T(8,128)(2,1)S(1)}, u32[]{:S(2)}, u32[]{:S(2)}) %collective-permute-start.5) | collective-permute-done | bytes 524320 | tf_op jit(solution)/shard_map/ppermute | solution.py:228
  119.0 16.3 %all-to-all-done.2 = bf16[8,64,768]{2,1,0:T(8,128)(2,1)S(1)} async-done(((bf16[8,64,768]{2,1,0:T(8,128)(2,1)}), bf16[8,64,768]{2,1,0:T(8,128)(2,1)S(1)}, u32[]{:S(2)}, u32[]{:S(2)}) %all-to-all-start.2) | async-done | bytes 786464 | tf_op jit(solution)/shard_map/all_to_all | solution.py:333
  139.8 5.3 fusion.60.proj
  145.1 7.5 %shard_map.252 = (bf16[1024,256]{1,0:T(8,128)(2,1)S(1)}, f32[1024,256]{1,0:T(8,128)S(1)}, f32[1024,2]{1,0:T(8,128)S(1)}, bf16[1024,256]{1,0:T(8,128)(2,1)S(1)}, ...) custom-call(f32[1024,512]{1,0:T(8,128)S(1)} %fusion.60.proj, f32[1024,2]{1,0:T(8,128)S(1)} %copy-done.2, ...), custom_call_target="tpu_custom_call" | custom-call | flops 10000000 | bytes 100000 | tf_op jit(solution)/shard_map/pallas_call | solution.py:195
  165.5 9.2 %collective-permute-done.15 = bf16[128,2048]{1,0:T(8,128)(2,1)S(1)} collective-permute-done((bf16[128,2048]{1,0:T(8,128)(2,1)S(1)}, bf16[128,2048]{1,0:T(8,128)(2,1)S(1)}, u32[]{:S(2)}, u32[]{:S(2)}) %collective-permute-start.15) | collective-permute-done | bytes 524320 | tf_op jit(solution)/shard_map/ppermute | solution.py:228
  174.6 9.5 %collective-permute-done.16 = bf16[128,2048]{1,0:T(8,128)(2,1)S(1)} collective-permute-done((bf16[128,2048]{1,0:T(8,128)(2,1)S(1)}, bf16[128,2048]{1,0:T(8,128)(2,1)S(1)}, u32[]{:S(2)}, u32[]{:S(2)}) %collective-permute-start.16) | collective-permute-done | bytes 524320 | tf_op jit(solution)/shard_map/ppermute | solution.py:228
  191.0 11.3 %collective-permute-done.18 = bf16[128,2048]{1,0:T(8,128)(2,1)S(1)} collective-permute-done((bf16[128,2048]{1,0:T(8,128)(2,1)S(1)}, bf16[128,2048]{1,0:T(8,128)(2,1)S(1)}, u32[]{:S(2)}, u32[]{:S(2)}) %collective-permute-start.18) | collective-permute-done | bytes 524320 | tf_op jit(solution)/shard_map/ppermute | solution.py:228
  202.3 10.7 %collective-permute-done.19 = bf16[128,2048]{1,0:T(8,128)(2,1)S(1)} collective-permute-done((bf16[128,2048]{1,0:T(8,128)(2,1)S(1)}, bf16[128,2048]{1,0:T(8,128)(2,1)S(1)}, u32[]{:S(2)}, u32[]{:S(2)}) %collective-permute-start.19) | collective-permute-done | bytes 524320 | tf_op jit(solution)/shard_map/ppermute | solution.py:228
  228.6 10.0 %fusion.80 = f32[1024,1536]{1,0:T(8,128)S(1)} fusion(bf16[1024,2048]{1,0:T(8,128)(2,1)} %constant_dynamic-update-slice_fusion.5, bf16[2048,1536]{1,0:T(8,128)(2,1)} %all-gather.6.cloned.1.call-done), kind=kOutput, calls=%fused_computation.232 | convolution fusion | flops 6442450944 | bytes 16777216 | tf_op jit(solution)/shard_map/dot_general | solution.py:33
  243.7 5.0 convolution_convert_fusion.1
  249.1 42.8 %all-gather.8.cloned.1.call-done = bf16[2048,768]{1,0:T(8,128)(2,1)} async-done(((bf16[512,768]{1,0:T(8,128)(2,1)}), bf16[2048,768]{1,0:T(8,128)(2,1)}) %all-gather.8.cloned.1.call-update) | async-done | bytes 3145744 | tf_op jit(solution)/shard_map/all_gather | solution.py:382
  292.0 9.1 %multiply_convert_fusion.1 = (bf16[1024,768]{1,0:T(8,128)(2,1)S(1)}, bf16[1024,768]{1,0:T(8,128)(2,1)S(1)}) fusion(f32[1024,1536]{1,0:T(8,128)} %copy-done.31, bf16[1024,2048]{1,0:T(8,128)(2,1)} %copy-done.55, bf16[2048,768]{1,0:T(8,128)(2,1)} %all-gather.8.cloned.1.call-done), kind=kOutput, calls=%fused_computation.24 | convolution fusion | flops 3231449088 | bytes 16777216 | tf_op jit(solution)/shard_map/dot_general | solution.py:33
  301.3 7.4 %convolution_convert_fusion.5 = bf16[512,2048]{1,0:T(8,128)(2,1)} fusion(bf16[2048,1536]{1,0:T(8,128)(2,1)} %all-gather.6.cloned.1.call-done, bf16[1024,768]{1,0:T(8,128)(2,1)S(1)} %get-tuple-element.143, bf16[1024,768]{1,0:T(8,128)(2,1)S(1)} %get-tuple-element.144), kind=kOutput, calls=%fused_computation.30 | convolution fusion | flops 3225419776 | bytes 11534336 | tf_op jit(solution)/shard_map/dot_general | solution.py:37
  310.0 11.0 %convolution_convert_fusion = bf16[2048,1536]{1,0:T(8,128)(2,1)} fusion(bf16[1024,2048]{1,0:T(8,128)(2,1)} %constant_dynamic-update-slice_fusion.5, bf16[1024,1536]{1,0:T(8,128)(2,1)S(1)} %pad_maximum_fusion), kind=kOutput, calls=%fused_computation.7 | convolution fusion | flops 6445596672 | bytes 13631488 | tf_op jit(solution)/shard_map/dot_general | solution.py:41
  325.5 6.2 %fusion.77 = (bf16[512,2048]{1,0:T(8,128)(2,1)S(1)}, f32[512,2048]{1,0:T(8,128)S(1)}) fusion(bf16[512,2048]{1,0:T(8,128)(2,1)S(1)} %collective-permute-done.23, bf16[512,1536]{1,0:T(8,128)(2,1)} %fusion.7, bf16[2048,1536]{1,0:T(8,128)(2,1)} %all-gather.6.cloned.1.call-done), kind=kOutput, calls=%fused_computation.229 | convolution fusion | flops 3224371200 | bytes 16252928 | tf_op jit(solution)/shard_map/dot_general | solution.py:37
  335.5 12.2 %collective-permute-done.24 = bf16[128,2048]{1,0:T(8,128)(2,1)S(1)} collective-permute-done((bf16[128,2048]{1,0:T(8,128)(2,1)S(1)}, bf16[128,2048]{1,0:T(8,128)(2,1)S(1)}, u32[]{:S(2)}, u32[]{:S(2)}) %collective-permute-start.24) | collective-permute-done | bytes 524320 | tf_op jit(solution)/shard_map/ppermute | solution.py:228
  347.8 10.4 %collective-permute-done.25 = bf16[128,2048]{1,0:T(8,128)(2,1)S(1)} collective-permute-done((bf16[128,2048]{1,0:T(8,128)(2,1)S(1)}, bf16[128,2048]{1,0:T(8,128)(2,1)S(1)}, u32[]{:S(2)}, u32[]{:S(2)}) %collective-permute-start.25) | collective-permute-done | bytes 524320 | tf_op jit(solution)/shard_map/ppermute | solution.py:228
  365.6 11.3 %collective-permute-done.27 = bf16[128,2048]{1,0:T(8,128)(2,1)S(1)} collective-permute-done((bf16[128,2048]{1,0:T(8,128)(2,1)S(1)}, bf16[128,2048]{1,0:T(8,128)(2,1)S(1)}, u32[]{:S(2)}, u32[]{:S(2)}) %collective-permute-start.27) | collective-permute-done | bytes 524320 | tf_op jit(solution)/shard_map/ppermute | solution.py:228
  376.9 11.4 %collective-permute-done.28 = bf16[128,2048]{1,0:T(8,128)(2,1)S(1)} collective-permute-done((bf16[128,2048]{1,0:T(8,128)(2,1)S(1)}, bf16[128,2048]{1,0:T(8,128)(2,1)S(1)}, u32[]{:S(2)}, u32[]{:S(2)}) %collective-permute-start.28) | collective-permute-done | bytes 524320 | tf_op jit(solution)/shard_map/ppermute | solution.py:228
  395.8 11.0 %shard_map.253 = (bf16[1024,512]{1,0:T(8,128)(2,1)S(1)}, f32[1024,2]{1,0:T(8,128)S(1)}, f32[2,128]{1,0:T(2,128)S(1)}) custom-call(f32[1024,512]{1,0:T(8,128)S(1)} %fusion.60.proj, f32[1024,2]{1,0:T(8,128)S(1)} %copy-done.3, f32[1024,128]{1,0:T(8,128)S(1)} %get-tuple-element.184.cosine, f32[1024,128]{1,0:T(8,128)S(1)} %get-tuple-element.185.sine, ...), custom_call_target="tpu_custom_call" | custom-call | flops 10000000 | bytes 100000 | tf_op jit(solution)/shard_map/pallas_call | solution.py:195
  414.0 53.2 %reduce-scatter.6.cloned.1.call-done = bf16[512,1536]{1,0:T(8,128)(2,1)} async-done(((bf16[2048,1536]{1,0:T(8,128)(2,1)}), bf16[512,1536]{1,0:T(8,128)(2,1)}) %reduce-scatter.6.cloned.1.call-update) | async-done | bytes 1572880 | tf_op jit(solution)/shard_map/reduce_scatter | solution.py:336
  482.9 5.5 fusion.78
  497.7 5.7 fusion.79
  508.2 9.2 %collective-permute-done.33 = bf16[128,2048]{1,0:T(8,128)(2,1)} collective-permute-done((bf16[128,2048]{1,0:T(8,128)(2,1)}, bf16[128,2048]{1,0:T(8,128)(2,1)}, u32[]{:S(2)}, u32[]{:S(2)}) %collective-permute-start.33) | collective-permute-done | bytes 524320 | tf_op jit(solution)/shard_map/ppermute | solution.py:228
  523.0 22.1 %collective-permute-done.36 = bf16[128,2048]{1,0:T(8,128)(2,1)} collective-permute-done((bf16[128,2048]{1,0:T(8,128)(2,1)}, bf16[128,2048]{1,0:T(8,128)(2,1)}, u32[]{:S(2)}, u32[]{:S(2)}) %collective-permute-start.36) | collective-permute-done | bytes 524320 | tf_op jit(solution)/shard_map/ppermute | solution.py:228
  545.0 10.9 %collective-permute-done.37 = bf16[128,2048]{1,0:T(8,128)(2,1)} collective-permute-done((bf16[128,2048]{1,0:T(8,128)(2,1)}, bf16[128,2048]{1,0:T(8,128)(2,1)}, u32[]{:S(2)}, u32[]{:S(2)}) %collective-permute-start.37) | collective-permute-done | bytes 524320 | tf_op jit(solution)/shard_map/ppermute | solution.py:228
  584.6 5.6 collective-permute-done.44
  597.6 12.6 %fusion.66 = (bf16[64,24576]{1,0:T(8,128)(2,1)}, f32[64,24576]{1,0:T(8,128)}, f32[64,24576]{1,0:T(8,128)}, f32[64,24576]{1,0:T(8,128)}) fusion(f32[64,24576]{1,0:T(8,128)S(1)} %bitcast.168, f32[]{:T(128)S(6)} %min.3, bf16[64,24576]{1,0:T(8,128)(2,1)S(1)} %constant_dynamic-update-slice_fusion.20, f32[64,24576]{1,0:T(8,128)} %param.18, f32[64,24576]{1,0:T(8,128)} %param.17), kind=kLoop, calls=%fused_computation.221 | loop fusion | flops 26738688 | bytes 44040196 | tf_op jit(solution)/shard_map/convert_element_type | solution.py:103
  (377 shorter events, 200.8 us)
Async XLA Ops:
  16.8 123.0 %all-gather.4.cloned.1.call-start = ((), (), s32[]{:S(2)}) async-start(), calls=%async_computation.9 | async-start | bytes 3932160 | tf_op jit(solution)/shard_map/all_gather | solution.py:353
  32.9 32.5 %all-to-all-start.1 = ((bf16[8,64,1536]{2,1,0:T(8,128)(2,1)}), bf16[8,64,1536]{2,1,0:T(8,128)(2,1)S(1)}, u32[]{:S(2)}, u32[]{:S(2)}) async-start(bf16[8,64,1536]{2,1,0:T(8,128)(2,1)} %copy.108), calls=%async_computation.1 | async-start | bytes 3145728 | tf_op jit(solution)/shard_map/all_to_all | solution.py:333
  36.7 21.9 %collective-permute-start.1 = (bf16[288,128]{1,0:T(8,128)(2,1)S(1)}, bf16[288,128]{1,0:T(8,128)(2,1)S(1)}, u32[]{:S(2)}, u32[]{:S(2)}) collective-permute-start(bf16[288,128]{1,0:T(8,128)(2,1)S(1)} %add.377), channel_id=1, source_target_pairs={{0,2},{1,3},{2,0},{3,1},{4,6},{5,7},{6,4},{7,5},{8,10},{9,11},{10,... | collective-permute-start | bytes 221192 | tf_op jit(solution)/shard_map/ppermute | solution.py:228
  61.3 24.5 %collective-permute-start.5 = (bf16[128,2048]{1,0:T(8,128)(2,1)S(1)}, bf16[128,2048]{1,0:T(8,128)(2,1)S(1)}, u32[]{:S(2)}, u32[]{:S(2)}) collective-permute-start(bf16[128,2048]{1,0:T(8,128)(2,1)S(1)} %bitcast.170), channel_id=1, source_target_pairs={{0,4},{1,5},{2,6},{3,7},{4,0},{5,1},{6,2},{7,3},{8,12},{9,13},{10,... | collective-permute-start | bytes 1572872 | tf_op jit(solution)/shard_map/ppermute | solution.py:228
  61.7 24.2 %collective-permute-start.6 = (bf16[128,2048]{1,0:T(8,128)(2,1)S(1)}, bf16[128,2048]{1,0:T(8,128)(2,1)}, u32[]{:S(2)}, u32[]{:S(2)}) collective-permute-start(bf16[128,2048]{1,0:T(8,128)(2,1)S(1)} %bitcast.171), channel_id=1, source_target_pairs={{0,6},{1,7},{2,4},{3,5},{4,2},{5,3},{6,0},{7,1},{8,14},{9,15},{10,... | collective-permute-start | bytes 1572872 | tf_op jit(solution)/shard_map/ppermute | solution.py:228
  88.6 24.5 %collective-permute-start.7 = (bf16[512,2048]{1,0:T(8,128)(2,1)}, bf16[512,2048]{1,0:T(8,128)(2,1)}, u32[]{:S(2)}, u32[]{:S(2)}) collective-permute-start(bf16[512,2048]{1,0:T(8,128)(2,1)} %pad_maximum_fusion.3), channel_id=1, source_target_pairs={{0,1},{1,0},{2,3},{3,2},{4,5},{5,4},{6,7},{7,6},{8,9},{9,8},{10,11... | collective-permute-start | bytes 6291464 | tf_op jit(solution)/shard_map/ppermute | solution.py:228
  101.7 51.0 %collective-permute-start.11 = (bf16[128,2048]{1,0:T(8,128)(2,1)}, bf16[128,2048]{1,0:T(8,128)(2,1)}, u32[]{:S(2)}, u32[]{:S(2)}) collective-permute-start(bf16[128,2048]{1,0:T(8,128)(2,1)} %bitcast.176), channel_id=1, source_target_pairs={{0,2},{1,3},{2,0},{3,1},{4,6},{5,7},{6,4},{7,5},{8,10},{9,11},{10,... | collective-permute-start | bytes 1572872 | tf_op jit(solution)/shard_map/ppermute | solution.py:228
  103.2 49.4 %collective-permute-start.12 = (bf16[128,2048]{1,0:T(8,128)(2,1)}, bf16[128,2048]{1,0:T(8,128)(2,1)}, u32[]{:S(2)}, u32[]{:S(2)}) collective-permute-start(bf16[128,2048]{1,0:T(8,128)(2,1)} %bitcast.177), channel_id=1, source_target_pairs={{0,4},{1,5},{2,6},{3,7},{4,0},{5,1},{6,2},{7,3},{8,12},{9,13},{10,... | collective-permute-start | bytes 1572872 | tf_op jit(solution)/shard_map/ppermute | solution.py:228
  103.8 48.9 %collective-permute-start.13 = (bf16[128,2048]{1,0:T(8,128)(2,1)}, bf16[128,2048]{1,0:T(8,128)(2,1)}, u32[]{:S(2)}, u32[]{:S(2)}) collective-permute-start(bf16[128,2048]{1,0:T(8,128)(2,1)} %bitcast.178), channel_id=1, source_target_pairs={{0,6},{1,7},{2,4},{3,5},{4,2},{5,3},{6,0},{7,1},{8,14},{9,15},{10,... | collective-permute-start | bytes 1572872 | tf_op jit(solution)/shard_map/ppermute | solution.py:228
  107.4 27.8 %all-to-all-start.2 = ((bf16[8,64,768]{2,1,0:T(8,128)(2,1)}), bf16[8,64,768]{2,1,0:T(8,128)(2,1)S(1)}, u32[]{:S(2)}, u32[]{:S(2)}) async-start(bf16[8,64,768]{2,1,0:T(8,128)(2,1)} %copy.109), calls=%async_computation.2 | async-start | bytes 1572864 | tf_op jit(solution)/shard_map/all_to_all | solution.py:333
  111.0 117.7 %all-gather.6.cloned.1.call-start = ((), (), s32[]{:S(2)}) async-start(), calls=%async_computation.10 | async-start | bytes 7864320 | tf_op jit(solution)/shard_map/all_gather | solution.py:376
  111.7 180.2 %all-gather.8.cloned.1.call-start = ((), (), s32[]{:S(2)}) async-start(), calls=%async_computation.11 | async-start | bytes 3932160 | tf_op jit(solution)/shard_map/all_gather | solution.py:382
  160.0 24.1 %collective-permute-start.16 = (bf16[128,2048]{1,0:T(8,128)(2,1)S(1)}, bf16[128,2048]{1,0:T(8,128)(2,1)S(1)}, u32[]{:S(2)}, u32[]{:S(2)}) collective-permute-start(bf16[128,2048]{1,0:T(8,128)(2,1)S(1)} %get-tuple-element.163), channel_id=1, source_target_pairs={{0,2},{1,3},{2,0},{3,1},{4,6},{5,7},{6,4},{7,5},{8,10},{9,11},{10,... | collective-permute-start | bytes 1572872 | tf_op jit(solution)/shard_map/ppermute | solution.py:228
  160.9 24.1 %collective-permute-start.17 = (bf16[128,2048]{1,0:T(8,128)(2,1)S(1)}, bf16[128,2048]{1,0:T(8,128)(2,1)S(1)}, u32[]{:S(2)}, u32[]{:S(2)}) collective-permute-start(bf16[128,2048]{1,0:T(8,128)(2,1)S(1)} %get-tuple-element.162), channel_id=1, source_target_pairs={{0,4},{1,5},{2,6},{3,7},{4,0},{5,1},{6,2},{7,3},{8,12},{9,13},{10,... | collective-permute-start | bytes 1572872 | tf_op jit(solution)/shard_map/ppermute | solution.py:228
  165.5 53.8 %collective-permute-start.22 = (bf16[512,2048]{1,0:T(8,128)(2,1)}, bf16[512,2048]{1,0:T(8,128)(2,1)}, u32[]{:S(2)}, u32[]{:S(2)}) collective-permute-start(bf16[512,2048]{1,0:T(8,128)(2,1)} %pad_maximum_fusion.5), channel_id=1, source_target_pairs={{0,1},{1,0},{2,3},{3,2},{4,5},{5,4},{6,7},{7,6},{8,9},{9,8},{10,11... | collective-permute-start | bytes 6291464 | tf_op jit(solution)/shard_map/ppermute | solution.py:228
  188.1 24.9 %collective-permute-start.19 = (bf16[128,2048]{1,0:T(8,128)(2,1)S(1)}, bf16[128,2048]{1,0:T(8,128)(2,1)S(1)}, u32[]{:S(2)}, u32[]{:S(2)}) collective-permute-start(bf16[128,2048]{1,0:T(8,128)(2,1)S(1)} %get-tuple-element.140), channel_id=1, source_target_pairs={{0,4},{1,5},{2,6},{3,7},{4,0},{5,1},{6,2},{7,3},{8,12},{9,13},{10,... | collective-permute-start | bytes 1572872 | tf_op jit(solution)/shard_map/ppermute | solution.py:228
  189.2 23.8 %collective-permute-start.20 = (bf16[128,2048]{1,0:T(8,128)(2,1)S(1)}, bf16[128,2048]{1,0:T(8,128)(2,1)S(1)}, u32[]{:S(2)}, u32[]{:S(2)}) collective-permute-start(bf16[128,2048]{1,0:T(8,128)(2,1)S(1)} %get-tuple-element.140), channel_id=1, source_target_pairs={{0,6},{1,7},{2,4},{3,5},{4,2},{5,3},{6,0},{7,1},{8,14},{9,15},{10,... | collective-permute-start | bytes 1572872 | tf_op jit(solution)/shard_map/ppermute | solution.py:228
  214.7 145.9 %reduce-scatter.4.cloned.1.call-start = ((), (), s32[]{:S(2)}) async-start(), calls=%async_computation.12 | async-start | bytes 3932160 | tf_op jit(solution)/shard_map/reduce_scatter | solution.py:336
  248.7 218.5 %reduce-scatter.6.cloned.1.call-start = ((), (), s32[]{:S(2)}) async-start(), calls=%async_computation.13 | async-start | bytes 7864320 | tf_op jit(solution)/shard_map/reduce_scatter | solution.py:336
  321.0 238.3 %reduce-scatter.8.cloned.1.call-start = ((), (), s32[]{:S(2)}) async-start(), calls=%async_computation.14 | async-start | bytes 3932160 | tf_op jit(solution)/shard_map/reduce_scatter | solution.py:336
  334.4 23.7 %collective-permute-start.25 = (bf16[128,2048]{1,0:T(8,128)(2,1)S(1)}, bf16[128,2048]{1,0:T(8,128)(2,1)S(1)}, u32[]{:S(2)}, u32[]{:S(2)}) collective-permute-start(bf16[128,2048]{1,0:T(8,128)(2,1)S(1)} %get-tuple-element.160), channel_id=1, source_target_pairs={{0,2},{1,3},{2,0},{3,1},{4,6},{5,7},{6,4},{7,5},{8,10},{9,11},{10,... | collective-permute-start | bytes 1572872 | tf_op jit(solution)/shard_map/ppermute | solution.py:228
  335.0 23.2 %collective-permute-start.26 = (bf16[128,2048]{1,0:T(8,128)(2,1)S(1)}, bf16[128,2048]{1,0:T(8,128)(2,1)S(1)}, u32[]{:S(2)}, u32[]{:S(2)}) collective-permute-start(bf16[128,2048]{1,0:T(8,128)(2,1)S(1)} %get-tuple-element.159), channel_id=1, source_target_pairs={{0,4},{1,5},{2,6},{3,7},{4,0},{5,1},{6,2},{7,3},{8,12},{9,13},{10,... | collective-permute-start | bytes 1572872 | tf_op jit(solution)/shard_map/ppermute | solution.py:228
  363.5 24.8 %collective-permute-start.28 = (bf16[128,2048]{1,0:T(8,128)(2,1)S(1)}, bf16[128,2048]{1,0:T(8,128)(2,1)S(1)}, u32[]{:S(2)}, u32[]{:S(2)}) collective-permute-start(bf16[128,2048]{1,0:T(8,128)(2,1)S(1)} %get-tuple-element.137), channel_id=1, source_target_pairs={{0,4},{1,5},{2,6},{3,7},{4,0},{5,1},{6,2},{7,3},{8,12},{9,13},{10,... | collective-permute-start | bytes 1572872 | tf_op jit(solution)/shard_map/ppermute | solution.py:228
  365.0 23.3 %collective-permute-start.29 = (bf16[128,2048]{1,0:T(8,128)(2,1)S(1)}, bf16[128,2048]{1,0:T(8,128)(2,1)S(1)}, u32[]{:S(2)}, u32[]{:S(2)}) collective-permute-start(bf16[128,2048]{1,0:T(8,128)(2,1)S(1)} %get-tuple-element.137), channel_id=1, source_target_pairs={{0,6},{1,7},{2,4},{3,5},{4,2},{5,3},{6,0},{7,1},{8,14},{9,15},{10,... | collective-permute-start | bytes 1572872 | tf_op jit(solution)/shard_map/ppermute | solution.py:228
  472.9 24.8 %collective-permute-start.35 = (bf16[512,2048]{1,0:T(8,128)(2,1)}, bf16[512,2048]{1,0:T(8,128)(2,1)}, u32[]{:S(2)}, u32[]{:S(2)}) collective-permute-start(bf16[512,2048]{1,0:T(8,128)(2,1)} %convolution_convert_fusion.6), channel_id=1, source_target_pairs={{0,1},{1,0},{2,3},{3,2},{4,5},{5,4},{6,7},{7,6},{8,9},{9,8},{10,11... | collective-permute-start | bytes 6291464 | tf_op jit(solution)/shard_map/ppermute | solution.py:228
  492.4 24.9 %collective-permute-start.33 = (bf16[128,2048]{1,0:T(8,128)(2,1)}, bf16[128,2048]{1,0:T(8,128)(2,1)}, u32[]{:S(2)}, u32[]{:S(2)}) collective-permute-start(bf16[128,2048]{1,0:T(8,128)(2,1)} %get-tuple-element.157), channel_id=1, source_target_pairs={{0,2},{1,3},{2,0},{3,1},{4,6},{5,7},{6,4},{7,5},{8,10},{9,11},{10,... | collective-permute-start | bytes 1572872 | tf_op jit(solution)/shard_map/ppermute | solution.py:228
  493.0 24.3 %collective-permute-start.34 = (bf16[128,2048]{1,0:T(8,128)(2,1)}, bf16[128,2048]{1,0:T(8,128)(2,1)}, u32[]{:S(2)}, u32[]{:S(2)}) collective-permute-start(bf16[128,2048]{1,0:T(8,128)(2,1)} %get-tuple-element.156), channel_id=1, source_target_pairs={{0,4},{1,5},{2,6},{3,7},{4,0},{5,1},{6,2},{7,3},{8,12},{9,13},{10,... | collective-permute-start | bytes 1572872 | tf_op jit(solution)/shard_map/ppermute | solution.py:228
  493.1 66.3 %all-to-all-start.4 = ((bf16[8,64,1536]{2,1,0:T(8,128)(2,1)}), bf16[8,64,1536]{2,1,0:T(8,128)(2,1)}, u32[]{:S(2)}, u32[]{:S(2)}) async-start(bf16[8,64,1536]{2,1,0:T(8,128)(2,1)} %bitcast.175), calls=%async_computation.7 | async-start | bytes 3145728 | tf_op jit(solution)/shard_map/all_to_all | solution.py:333
  504.6 40.4 %collective-permute-start.36 = (bf16[128,2048]{1,0:T(8,128)(2,1)}, bf16[128,2048]{1,0:T(8,128)(2,1)}, u32[]{:S(2)}, u32[]{:S(2)}) collective-permute-start(bf16[128,2048]{1,0:T(8,128)(2,1)} %get-tuple-element.152), channel_id=1, source_target_pairs={{0,6},{1,7},{2,4},{3,5},{4,2},{5,3},{6,0},{7,1},{8,14},{9,15},{10,... | collective-permute-start | bytes 1572872 | tf_op jit(solution)/shard_map/ppermute | solution.py:228
  507.5 48.4 %collective-permute-start.37 = (bf16[128,2048]{1,0:T(8,128)(2,1)}, bf16[128,2048]{1,0:T(8,128)(2,1)}, u32[]{:S(2)}, u32[]{:S(2)}) collective-permute-start(bf16[128,2048]{1,0:T(8,128)(2,1)} %get-tuple-element.154), channel_id=1, source_target_pairs={{0,2},{1,3},{2,0},{3,1},{4,6},{5,7},{6,4},{7,5},{8,10},{9,11},{10,... | collective-permute-start | bytes 1572872 | tf_op jit(solution)/shard_map/ppermute | solution.py:228
  508.1 47.8 %collective-permute-start.38 = (bf16[128,2048]{1,0:T(8,128)(2,1)}, bf16[128,2048]{1,0:T(8,128)(2,1)}, u32[]{:S(2)}, u32[]{:S(2)}) collective-permute-start(bf16[128,2048]{1,0:T(8,128)(2,1)} %get-tuple-element.153), channel_id=1, source_target_pairs={{0,4},{1,5},{2,6},{3,7},{4,0},{5,1},{6,2},{7,3},{8,12},{9,13},{10,... | collective-permute-start | bytes 1572872 | tf_op jit(solution)/shard_map/ppermute | solution.py:228
  569.8 24.9 %all-to-all-start.5 = ((bf16[8,64,768]{2,1,0:T(8,128)(2,1)}), bf16[8,64,768]{2,1,0:T(8,128)(2,1)S(1)}, u32[]{:S(2)}, u32[]{:S(2)}) async-start(bf16[8,64,768]{2,1,0:T(8,128)(2,1)} %bitcast.28), calls=%async_computation.8 | async-start | bytes 1572864 | tf_op jit(solution)/shard_map/all_to_all | solution.py:333
  (97 other events, 1048.5 us)
Sparse Core Ops, SparseCore 0:
  29.6 63.2 all-gather.3
  113.4 115.1 all-gather.5
  230.2 61.7 all-gather.7
  294.7 58.8 reduce-scatter.3
  356.3 110.7 reduce-scatter.5
  469.9 60.7 reduce-scatter.7

commit v4 on v3

--- a/solution.py
+++ b/solution.py
@@ -251,26 +251,33 @@
     return gather_cores(gather_chips(value))
 
 
-def scatter_first(left, weights):
-    half = left.shape[0] // 2
-    return left[:half], dot_nt(left[half:], weights).astype(bf16)
-
-
-def scatter_rest(left, weights, started):
-    groups = lax.axis_size("cp")
-    rows = left.shape[0] * 2 // groups
-    part = dot_nt(left, weights) + shift(started, "cp", 1).astype(f32)
-    total = part[:rows]
-    low = part[rows:].astype(bf16)
-    for offset in far_first(groups):
+def dots_nt(lefts, weights):
+    return sum(dot_nt(left, w) for left, w in zip(lefts, weights))
+
+
+def scatter_first(lefts, weights):
+    half = lefts[0].shape[0] // 2
+    other = dots_nt([left[half:] for left in lefts], weights)
+    return [left[:half] for left in lefts], other.astype(bf16)
+
+
+def scatter_cores(lefts, weights, started):
+    rows = lefts[0].shape[0] * 2 // lax.axis_size("cp")
+    part = dots_nt(lefts, weights) + shift(started, "cp", 1).astype(f32)
+    return part[:rows], part[rows:].astype(bf16)
+
+
+def scatter_chips(total, low):
+    rows = total.shape[0]
+    for offset in far_first(lax.axis_size("cp")):
         place = (offset // 2 - 1) * rows
         total = total + shift(low[place : place + rows], "cp", offset).astype(f32)
     return total
 
 
-def scatter_cp(left, weights):
-    kept, started = scatter_first(left, weights)
-    return scatter_rest(kept, weights, started)
+def scatter_cp(lefts, weights):
+    kept, started = scatter_first(lefts, weights)
+    return scatter_chips(*scatter_cores(kept, weights, started))
 
 
 def sum_shifts(value, axis, step):
@@ -308,7 +315,8 @@
     groups = lax.axis_size("cp")
     planes = lax.axis_size("dp")
     me = lax.axis_index("cp")
-    owner = lax.axis_index("dp") * groups + me
+    plane = lax.axis_index("dp")
+    owner = plane * groups + me
     wr = big_weight.shape[0]
     rows, features = tokens.shape[1:]
     width_attn = HEADS * HEAD_DIM
@@ -335,6 +343,9 @@
     def sum_rows(part):
         return lax.psum_scatter(part, "dp", scatter_dimension=0, tiled=True)
 
+    def to_owner(part):
+        return exchange(part.reshape(groups, wr, -1))
+
     def to_columns(part):
         return exchange(part).reshape(groups * wr, -1)
 
@@ -348,18 +359,28 @@
         axis=2,
     )
     attn_rows = to_columns(attn_blocks)
-    gu_blocks = jnp.concatenate([blocks(start_mlp, FF), blocks(start_mlp + FF, FF)], axis=2)
-    gu_blocks, attn_rows = tie(gu_blocks, attn_rows)
+    half_ff = wff // 2
+    mlp_blocks = [blocks(start_mlp + i * FF, FF) for i in range(3)]
+
+    def unit_blocks(i):
+        return jnp.concatenate(
+            [b[:, :, i * half_ff : (i + 1) * half_ff] for b in mlp_blocks], axis=2
+        )
+
+    first_blocks, attn_rows = tie(unit_blocks(0), attn_rows)
     attn_w = lax.all_gather(attn_rows, "dp", axis=0, tiled=True)
-    gu_rows = to_columns(gu_blocks)
-    down_blocks, gu_rows = tie(blocks(start_down, FF), gu_rows)
-    down_rows = to_columns(down_blocks)
-
+    mlp_rows = [to_columns(first_blocks)]
+
+    size = groups * wr
     small_place = lax.dynamic_update_slice_in_dim(
-        jnp.zeros((HEADS + 2, features), bf16), small_weight.astype(bf16).T, owner * wr, 1
-    ).reshape(-1, 128)
-    own_tokens, small_full = tie(tokens[0], sum_cp(small_place))
-    small_full = sum_dp(small_full).reshape(HEADS + 2, features)
+        jnp.zeros((HEADS + 2, size), bf16), small_weight.astype(bf16).T, me * wr, 1
+    )
+    own_tokens, small_plane, mlp_rows[0] = tie(tokens[0], sum_cp(small_place), mlp_rows[0])
+    mlp_w = [lax.all_gather(mlp_rows[0], "dp", axis=0, tiled=True)]
+    small_full = jnp.zeros((HEADS + 2, features), bf16)
+    for offset in range(planes):
+        part = shift(small_plane, "dp", offset) if offset else small_plane
+        small_full = lax.dynamic_update_slice_in_dim(small_full, part, (plane ^ offset) * size, 1)
     gate_w = lax.dynamic_slice_in_dim(small_full, me * own_q, own_q, 0).T
     gain_one = 1.0 + small_full[HEADS].astype(f32)
     gain_two = 1.0 + small_full[HEADS + 1].astype(f32)
@@ -372,69 +393,91 @@
     spots = jnp.stack([place, place - position], axis=1)
     info = (cosine, sine, spots, place[None, :], qk_gain)
 
-    own_branch, gu_rows, *tokens_all = tie(cotangent[0], gu_rows, *gather_chips(own_tokens))
-    gu_w = lax.all_gather(gu_rows, "dp", axis=0, tiled=True)
+    second_blocks, own_branch, *tokens_all = tie(
+        unit_blocks(1), cotangent[0], *gather_chips(own_tokens)
+    )
+    mlp_rows.append(to_columns(second_blocks))
     tokens_all = gather_cores(tokens_all)
     kept_one = (rms(tokens_all.astype(f32)) * gain_one).astype(bf16)
 
     sig = jax.nn.sigmoid(dot(kept_one, gate_w))
-    kept_one, down_rows = tie(kept_one, down_rows)
-    down_w = lax.all_gather(down_rows, "dp", axis=0, tiled=True)
+    own_branch, attn_w = tie(own_branch, attn_w)
     grad_branch = gather_chips(own_branch)
     proj = dot(kept_one, attn_w[:, :win])
     gated, heads, tops, queries, keys, values = attend(own_q, own_kv, proj, sig, *info)
     inputs = tokens[0].astype(f32)
-    gated, *grad_branch = tie(gated, *grad_branch)
+    gated, mlp_rows[1], *grad_branch = tie(gated, mlp_rows[1], *grad_branch)
     grad_branch = gather_cores(grad_branch)
-    middle = inputs + scatter_cp(gated, attn_w[:, win:])
+    mlp_w.append(lax.all_gather(mlp_rows[1], "dp", axis=0, tiled=True))
+    middle = inputs + scatter_cp([gated], [attn_w[:, win:]])
 
     normed_two = rms(middle)
     kept_two = gather_cp((normed_two * gain_two).astype(bf16))
-    gate_up = dot(kept_two, gu_w)
-    gate, upper = gate_up[:, :wff], gate_up[:, wff:]
-    sig_gate = jax.nn.sigmoid(gate)
-    hidden = (gate * sig_gate * upper).astype(bf16)
-    down_grad, grad_branch = tie(dot_tn(grad_branch, hidden).astype(bf16), grad_branch)
-    down_term = sum_rows(down_grad)
-    grad_hidden = dot(grad_branch, down_w)
-    grad_gate = grad_hidden * upper * sig_gate * (1.0 + gate * (1.0 - sig_gate))
-    grad_upper = grad_hidden * gate * sig_gate
-    grad_gu = jnp.concatenate([grad_gate, grad_upper], axis=1).astype(bf16)
-
+    gu_w = [w[:, : 2 * half_ff] for w in mlp_w]
+    down_w = [w[:, 2 * half_ff :] for w in mlp_w]
+    hidden, grad_gu, mlp_grads, mlp_terms = [], [], [], []
+    for i in range(2):
+        gate_up = dot(kept_two, gu_w[i])
+        gate, upper = gate_up[:, :half_ff], gate_up[:, half_ff:]
+        sig_gate = jax.nn.sigmoid(gate)
+        hidden.append((gate * sig_gate * upper).astype(bf16))
+        grad_hidden = dot(grad_branch, down_w[i])
+        grad_gate = grad_hidden * upper * sig_gate * (1.0 + gate * (1.0 - sig_gate))
+        grad_upper = grad_hidden * gate * sig_gate
+        grad_gu.append(jnp.concatenate([grad_gate, grad_upper], axis=1).astype(bf16))
+
+    def mlp_grad(i):
+        terms = [dot_tn(kept_two, grad_gu[i]), dot_tn(grad_branch, hidden[i])]
+        return jnp.concatenate(terms, axis=1).astype(bf16)
+
+    first_grad, kept_two = tie(mlp_grad(0), kept_two)
+    mlp_terms.append(sum_rows(first_grad))
     left, started = scatter_first(grad_gu, gu_w)
-    late_gu, started = tie(grad_gu, started)
-    gu_grad, left = tie(dot_tn(kept_two, late_gu).astype(bf16), left)
-    gu_term = sum_rows(gu_grad)
-    grad_two = scatter_rest(left, gu_w, started)
+    started, *grad_gu = tie(started, *grad_gu)
+    second_grad, *left = tie(mlp_grad(1), *left)
+    mlp_terms.append(sum_rows(second_grad))
+    own_two, far_two = scatter_cores(left, gu_w, started)
+    far_two, *hidden = tie(far_two, *hidden)
+    left, started = scatter_first(hidden, down_w)
+    tail, far_tail = scatter_cores(left, down_w, started)
+    grad_two = scatter_chips(own_two, far_two)
     gain_two_term = jnp.sum(grad_two * normed_two, axis=0)
     grad_out = cotangent[0].astype(f32)
     grad_middle = grad_out + norm_back(middle, grad_two * gain_two)
 
-    grad_middle, hidden, down_term = tie(grad_middle, hidden, down_term)
     grad_attn_branch = gather_cp(grad_middle.astype(bf16))
-    left, started = scatter_first(hidden, down_w)
-    left, grad_attn_branch, started = tie(left, grad_attn_branch, started)
-    result = middle + scatter_rest(left, down_w, started)
+    grad_attn_branch, far_tail = tie(grad_attn_branch, far_tail)
+    tail = scatter_chips(tail, far_tail)
     grad_gated = dot(grad_attn_branch, attn_w[:, win:])
     grad_proj, grad_logits, qk_terms = attend_back(
         own_q, own_kv, proj, sig, *info, heads, tops, queries, keys, values, grad_gated
     )
     grad_logits = grad_logits.astype(bf16)
+    grad_proj, tail = tie(grad_proj, tail)
+    result = middle + tail
     attn_grad = jnp.concatenate(
         [dot_tn(kept_one, grad_proj), dot_tn(grad_attn_branch, gated)], axis=1
     ).astype(bf16)
-    attn_grad, late_proj, gu_term = tie(attn_grad, grad_proj, gu_term)
+    attn_grad, late_proj = tie(attn_grad, grad_proj)
     attn_term = sum_rows(attn_grad)
     gate_term = dot_tn(kept_one, grad_logits)
     full_in = jnp.concatenate([attn_w[:, :win], gate_w], axis=1)
     grad_all = jnp.concatenate([late_proj, grad_logits], axis=1)
-    grad_one = scatter_cp(grad_all, full_in)
+    grad_one = scatter_cp([grad_all], [full_in])
     gain_one_term = jnp.sum(grad_one * rms(inputs), axis=0)
     grad_input = grad_middle + norm_back(inputs, grad_one * gain_one)
 
+    def tall(value):
+        return value.reshape(-1, 128)
+
+    small_terms = jnp.concatenate([gate_term.T, gain_one_term[None], gain_two_term[None]], axis=0)
+    small_terms = sum_dp(jnp.concatenate([tall(small_terms), qk_terms], axis=0))
+    edge = own_q * features // 128
     gate_place = lax.dynamic_update_slice_in_dim(
-        jnp.zeros((HEADS, features), f32), gate_term.T, me * own_q, 0
-    )
+        jnp.zeros((HEADS * features // 128, 128), f32), small_terms[:edge], me * edge, 0
+    )
+    small_sum = sum_cp(jnp.concatenate([gate_place, small_terms[edge:]], axis=0))
+
     def kv_sum(part):
         if copies == 1:
             return part
@@ -443,14 +486,11 @@
     def wide(part):
         return part.transpose(1, 0, 2).reshape(wr, -1).astype(f32)
 
-    def to_owner(part):
-        return exchange(part.reshape(groups, wr, -1))
-
-    down_own = to_owner(down_term)
-    gu_term, down_own = tie(gu_term, down_own)
-    gu_own = to_owner(gu_term)
-    attn_term, result, grad_input, gain_one_term, down_own, gu_own = tie(
-        attn_term, result, grad_input, gain_one_term, down_own, gu_own
+    mlp_own = [to_owner(mlp_terms[0])]
+    mlp_terms[1], mlp_own[0] = tie(mlp_terms[1], mlp_own[0])
+    mlp_own.append(to_owner(mlp_terms[1]))
+    attn_term, result, grad_input, small_sum, mlp_own[1] = tie(
+        attn_term, result, grad_input, small_sum, mlp_own[1]
     )
     attn_own = to_owner(attn_term)
     k_own = kv_sum(attn_own[:, :, wq : wq + wkv])
@@ -460,23 +500,15 @@
     else:
         attn_squares = squares_of(attn_term[:, :wq]) + squares_of(attn_term[:, win:])
         attn_squares = attn_squares + squares_of(k_own) + squares_of(v_own)
-    local_squares = squares_of(down_term) + squares_of(gu_term) + attn_squares
-    small_term = jnp.concatenate([gate_place, gain_one_term[None], gain_two_term[None]], axis=0)
-    last_small = sum_dp(
-        sum_cp(
-            jnp.concatenate(
-                [small_term.reshape(-1, 128), qk_terms, jnp.full((1, 128), local_squares, f32)],
-                axis=0,
-            )
-        )
-    )
-    tall = (HEADS + 2) * features // 128
-    qk_grad = last_small[tall : tall + 2]
-    total = last_small[tall + 2, 0] + squares_of(last_small[: tall + 2])
+    local_squares = squares_of(mlp_terms[0]) + squares_of(mlp_terms[1]) + attn_squares
+    local_squares = sum_cp(sum_dp(jnp.full((1, 128), local_squares, f32)))
+    edge = (HEADS + 2) * features // 128
+    qk_grad = small_sum[edge:]
+    total = local_squares[0, 0] + squares_of(small_sum)
     norm_value = jnp.sqrt(total)
     factor = jnp.minimum(1.0, 1.0 / (norm_value + 1e-06))
     small_grad = lax.dynamic_slice_in_dim(
-        last_small[:tall].reshape(HEADS + 2, features), owner * wr, wr, 1
+        small_sum[:edge].reshape(HEADS + 2, features), owner * wr, wr, 1
     ).T
     big_grad = jnp.concatenate(
         [
@@ -484,9 +516,10 @@
             wide(k_own),
             wide(v_own),
             wide(attn_own[:, :, win:]),
-            wide(gu_own[:, :, :wff]),
-            wide(gu_own[:, :, wff:]),
-            wide(down_own),
+        ]
+        + [
+            wide(jnp.concatenate([m[:, :, i * half_ff : (i + 1) * half_ff] for m in mlp_own], axis=2))
+            for i in range(3)
         ],
         axis=1,
     )

time: 626 us -> 572 us (0.914)
  waiting for transfers between devices: 319 us -> 243 us
  starting transfers between devices: 71.1 us -> 80.5 us
  other arithmetic: 55.2 us -> 62.4 us
    reduce_scatter x3, waiting for transfers between devices: 53.2 us -> 28 us  [sum_rows(): return lax.psum_scatter(part, 'dp', scatter_dimension=0, tiled=True)]
    all_gather x2, waiting for transfers between devices: 44.1 us -> 23.3 us  [the longest x1 23.3 us: local(): mlp_w.append(lax.all_gather(mlp_rows[1], 'dp', axis=0, tiled=True))]
    ppermute x46 -> x53, waiting for transfers between devices: 193 us -> 173 us  [shift(): lax.ppermute(value, axis, [(i, i ^ offset) for i in range(lax.axis_size(a...]
    concatenate x5 -> x9, other arithmetic: 1.77 us -> 10.7 us  [the longest x2 5.12 us: mlp_grad(): return jnp.concatenate(terms, axis=1).astype(bf16)]
    all_to_all x6, waiting for transfers between devices: 27.4 us -> 18.6 us  [exchange(): return lax.all_to_all(part, 'cp', 0, 0, tiled=True)]
    ppermute x46 -> x53, starting transfers between devices: 45.5 us -> 53.4 us  [shift(): lax.ppermute(value, axis, [(i, i ^ offset) for i in range(lax.axis_size(a...]
    dot_general x8 -> x12, matrix products: 32.9 us -> 39.4 us  [dot_nt(): return lax.dot_general(a, b, contract_cols, preferred_element_type=f32)]
    unnamed x173 -> x167, local copies, waits for them, and re-layouts: 21.6 us -> 17.3 us
  transfers between devices with their start and end apart: 58 -> 65, of which waited for: 30 -> 32; matrix products, arithmetic and copies ran while one was open for 26% -> 31% of each run, Pallas kernels for 3% -> 3%
where the time goes in v4:
time: 572 us; the launch traced here: 565 us
  waiting for transfers between devices  243 us (42%)
  matrix products  89 us (16%)
  starting transfers between devices  80.5 us (14%)
  other arithmetic  62.4 us (11%)
  local copies, waits for them, and re-layouts  51 us (9%)
  between operations  20 us (3%)
  Pallas kernels  18.1 us (3%)
    ppermute x53, waiting for transfers between devices, shift(): lax.ppermute(value, axis, [(i, i ^ offset) for i in range(lax.axis_size(a...  173 us
    ppermute x53, starting transfers between devices, shift(): lax.ppermute(value, axis, [(i, i ^ offset) for i in range(lax.axis_size(a...  53.4 us
    dot_general x12, matrix products, dot_nt(): return lax.dot_general(a, b, contract_cols, preferred_element_type=f32)  39.4 us
    dot_general x7, matrix products, dot(): return jnp.dot(a, b, preferred_element_type=f32)  28.1 us
    reduce_scatter x3, waiting for transfers between devices, sum_rows(): return lax.psum_scatter(part, 'dp', scatter_dimension=0, tiled=True)  28 us
    all_to_all x6, starting transfers between devices, exchange(): return lax.all_to_all(part, 'cp', 0, 0, tiled=True)  25.7 us
    all_gather x1, waiting for transfers between devices, local(): mlp_w.append(lax.all_gather(mlp_rows[1], 'dp', axis=0, tiled=True))  23.3 us
    dot_general x7, matrix products, dot_tn(): return lax.dot_general(a, b, contract_rows, preferred_element_type=f32)  21.5 us
  transfers between devices with their start and end apart: 65, of which 32 were waited for; matrix products, arithmetic and copies ran while one was open for 31% of the time, Pallas kernels for 3%

profile of v4, /device:TPU:0, one launch (start us, length us, event | category | flops | bytes accessed | tf_op | source)
XLA Modules:
  0.0 564.6 jit_solution(3027848823466309124)
XLA Ops:
  11.6 5.2 all-to-all-start
  19.5 10.0 %all-to-all-done = bf16[8,64,768]{2,1,0:T(8,128)(2,1)} async-done(((bf16[8,64,768]{2,1,0:T(8,128)(2,1)}), bf16[8,64,768]{2,1,0:T(8,128)(2,1)}, u32[]{:S(2)}, u32[]{:S(2)}) %all-to-all-start) | async-done | bytes 786464 | tf_op jit(solution)/shard_map/all_to_all | solution.py:341
  39.1 13.4 %collective-permute-done.3 = bf16[18,512]{1,0:T(8,128)(2,1)S(1)} collective-permute-done((bf16[18,512]{1,0:T(8,128)(2,1)S(1)}, bf16[18,512]{1,0:T(8,128)(2,1)S(1)}, u32[]{:S(2)}, u32[]{:S(2)}) %collective-permute-start.3) | collective-permute-done | bytes 18464 | tf_op jit(solution)/shard_map/ppermute | solution.py:228
  60.2 7.9 %collective-permute-done.4 = bf16[128,2048]{1,0:T(8,128)(2,1)S(1)} collective-permute-done((bf16[128,2048]{1,0:T(8,128)(2,1)S(1)}, bf16[128,2048]{1,0:T(8,128)(2,1)S(1)}, u32[]{:S(2)}, u32[]{:S(2)}) %collective-permute-start.4) | collective-permute-done | bytes 524320 | tf_op jit(solution)/shard_map/ppermute | solution.py:228
  68.1 10.9 %collective-permute-done.5 = bf16[128,2048]{1,0:T(8,128)(2,1)S(1)} collective-permute-done((bf16[128,2048]{1,0:T(8,128)(2,1)S(1)}, bf16[128,2048]{1,0:T(8,128)(2,1)S(1)}, u32[]{:S(2)}, u32[]{:S(2)}) %collective-permute-start.5) | collective-permute-done | bytes 524320 | tf_op jit(solution)/shard_map/ppermute | solution.py:228
  115.0 5.3 fusion.87.proj
  120.3 7.5 %shard_map.252 = (bf16[1024,256]{1,0:T(8,128)(2,1)S(1)}, f32[1024,256]{1,0:T(8,128)S(1)}, f32[1024,2]{1,0:T(8,128)S(1)}, bf16[1024,256]{1,0:T(8,128)(2,1)S(1)}, ...) custom-call(f32[1024,512]{1,0:T(8,128)S(1)} %fusion.87.proj, f32[1024,2]{1,0:T(8,128)S(1)} %copy-done.2, ...), custom_call_target="tpu_custom_call" | custom-call | flops 10000000 | bytes 100000 | tf_op jit(solution)/shard_map/pallas_call | solution.py:195
  131.8 11.2 %collective-permute-done.13 = bf16[128,2048]{1,0:T(8,128)(2,1)} collective-permute-done((bf16[128,2048]{1,0:T(8,128)(2,1)}, bf16[128,2048]{1,0:T(8,128)(2,1)}, u32[]{:S(2)}, u32[]{:S(2)}) %collective-permute-start.13) | collective-permute-done | bytes 524320 | tf_op jit(solution)/shard_map/ppermute | solution.py:228
  161.4 7.6 %collective-permute-done.17 = bf16[128,2048]{1,0:T(8,128)(2,1)} collective-permute-done((bf16[128,2048]{1,0:T(8,128)(2,1)}, bf16[128,2048]{1,0:T(8,128)(2,1)}, u32[]{:S(2)}, u32[]{:S(2)}) %collective-permute-start.17) | collective-permute-done | bytes 524320 | tf_op jit(solution)/shard_map/ppermute | solution.py:228
  170.4 11.0 %collective-permute-done.15 = bf16[128,2048]{1,0:T(8,128)(2,1)} collective-permute-done((bf16[128,2048]{1,0:T(8,128)(2,1)}, bf16[128,2048]{1,0:T(8,128)(2,1)}, u32[]{:S(2)}, u32[]{:S(2)}) %collective-permute-start.15) | collective-permute-done | bytes 524320 | tf_op jit(solution)/shard_map/ppermute | solution.py:228
  189.3 11.4 %collective-permute-done.18 = bf16[128,2048]{1,0:T(8,128)(2,1)S(1)} collective-permute-done((bf16[128,2048]{1,0:T(8,128)(2,1)S(1)}, bf16[128,2048]{1,0:T(8,128)(2,1)S(1)}, u32[]{:S(2)}, u32[]{:S(2)}) %collective-permute-start.18) | collective-permute-done | bytes 524320 | tf_op jit(solution)/shard_map/ppermute | solution.py:228
  200.7 9.5 %collective-permute-done.19 = bf16[128,2048]{1,0:T(8,128)(2,1)S(1)} collective-permute-done((bf16[128,2048]{1,0:T(8,128)(2,1)S(1)}, bf16[128,2048]{1,0:T(8,128)(2,1)S(1)}, u32[]{:S(2)}, u32[]{:S(2)}) %collective-permute-start.19) | collective-permute-done | bytes 524320 | tf_op jit(solution)/shard_map/ppermute | solution.py:228
  221.2 6.4 %fusion.12 = f32[1024,768]{0,1:T(8,128)S(1)} fusion(bf16[1024,2048]{1,0:T(8,128)(2,1)} %constant_dynamic-update-slice_fusion.10, bf16[2048,1152]{1,0:T(8,128)(2,1)} %all-gather.6.cloned.1.call-done), kind=kOutput, calls=%fused_computation.38 | convolution fusion | flops 3221225472 | bytes 10485760 | tf_op jit(solution)/shard_map/dot_general | solution.py:33
  233.4 6.5 %convolution_convert_fusion.1 = bf16[2048,768]{0,1:T(8,128)(2,1)S(1)} fusion(bf16[1024,2048]{1,0:T(8,128)(2,1)} %constant_dynamic-update-slice_fusion.10, bf16[1024,384]{0,1:T(8,128)(2,1)S(1)} %get-tuple-element.147, bf16[1024,384]{0,1:T(8,128)(2,1)S(1)} %get-tuple-element.148), kind=kOutput, calls=%fused_computation.19 | convolution fusion | flops 3225944064 | bytes 8912896 | tf_op jit(solution)/shard_map/dot_general | solution.py:41
  244.8 6.0 %fusion.10 = f32[512,2048]{1,0:T(8,128)} fusion(bf16[2048,1152]{1,0:T(8,128)(2,1)} %all-gather.6.cloned.1.call-done, bf16[1024,384]{0,1:T(8,128)(2,1)} %copy-done.51, bf16[1024,384]{0,1:T(8,128)(2,1)} %copy-done.50), kind=kOutput, calls=%fused_computation.36 | convolution fusion | flops 1612185600 | bytes 8912896 | tf_op jit(solution)/shard_map/dot_general | solution.py:37
  250.8 23.3 %all-gather.8.cloned.1.call-done = bf16[2048,1152]{1,0:T(8,128)(2,1)} async-done(((bf16[512,1152]{1,0:T(8,128)(2,1)}), bf16[2048,1152]{1,0:T(8,128)(2,1)}) %all-gather.8.cloned.1.call-update) | async-done | bytes 4718608 | tf_op jit(solution)/shard_map/all_gather | solution.py:411
  274.1 6.4 %fusion.6 = f32[1024,768]{0,1:T(8,128)S(1)} fusion(bf16[1024,2048]{1,0:T(8,128)(2,1)} %constant_dynamic-update-slice_fusion.10, bf16[2048,1152]{1,0:T(8,128)(2,1)} %all-gather.8.cloned.1.call-done), kind=kOutput, calls=%fused_computation.32 | convolution fusion | flops 3221225472 | bytes 10485760 | tf_op jit(solution)/shard_map/dot_general | solution.py:33
  289.4 5.9 %convolution_convert_fusion = bf16[2048,768]{0,1:T(8,128)(2,1)S(1)} fusion(bf16[1024,768]{0,1:T(8,128)(2,1)S(1)} %pad_maximum_fusion.9, bf16[1024,2048]{1,0:T(8,128)(2,1)} %constant_dynamic-update-slice_fusion.10), kind=kOutput, calls=%fused_computation.18 | convolution fusion | flops 3222798336 | bytes 8912896 | tf_op jit(solution)/shard_map/dot_general | solution.py:41
  302.5 4.6 convert_add_fusion.2
  312.4 9.5 %collective-permute-done.26 = bf16[128,2048]{1,0:T(8,128)(2,1)S(1)} collective-permute-done((bf16[128,2048]{1,0:T(8,128)(2,1)S(1)}, bf16[128,2048]{1,0:T(8,128)(2,1)S(1)}, u32[]{:S(2)}, u32[]{:S(2)}) %collective-permute-start.26) | collective-permute-done | bytes 524320 | tf_op jit(solution)/shard_map/ppermute | solution.py:228
  324.0 10.4 %collective-permute-done.24 = bf16[128,2048]{1,0:T(8,128)(2,1)S(1)} collective-permute-done((bf16[128,2048]{1,0:T(8,128)(2,1)S(1)}, bf16[128,2048]{1,0:T(8,128)(2,1)S(1)}, u32[]{:S(2)}, u32[]{:S(2)}) %collective-permute-start.24) | collective-permute-done | bytes 524320 | tf_op jit(solution)/shard_map/ppermute | solution.py:228
  341.7 9.9 %collective-permute-done.27 = bf16[128,2048]{1,0:T(8,128)(2,1)S(1)} collective-permute-done((bf16[128,2048]{1,0:T(8,128)(2,1)S(1)}, bf16[128,2048]{1,0:T(8,128)(2,1)S(1)}, u32[]{:S(2)}, u32[]{:S(2)}) %collective-permute-start.27) | collective-permute-done | bytes 524320 | tf_op jit(solution)/shard_map/ppermute | solution.py:228
  351.6 10.9 %collective-permute-done.28 = bf16[128,2048]{1,0:T(8,128)(2,1)S(1)} collective-permute-done((bf16[128,2048]{1,0:T(8,128)(2,1)S(1)}, bf16[128,2048]{1,0:T(8,128)(2,1)S(1)}, u32[]{:S(2)}, u32[]{:S(2)}) %collective-permute-start.28) | collective-permute-done | bytes 524320 | tf_op jit(solution)/shard_map/ppermute | solution.py:228
  374.0 10.7 %shard_map.253 = (bf16[1024,512]{1,0:T(8,128)(2,1)S(1)}, f32[1024,2]{1,0:T(8,128)S(1)}, f32[2,128]{1,0:T(2,128)S(1)}) custom-call(f32[1024,512]{1,0:T(8,128)S(1)} %fusion.87.proj, f32[1024,2]{1,0:T(8,128)S(1)} %copy-done.3, f32[1024,128]{1,0:T(8,128)S(1)} %get-tuple-element.198.cosine, f32[1024,128]{1,0:T(8,128)S(1)} %get-tuple-element.199.sine, ...), custom_call_target="tpu_custom_call" | custom-call | flops 10000000 | bytes 100000 | tf_op jit(solution)/shard_map/pallas_call | solution.py:195
  386.0 9.6 %collective-permute-done.32 = bf16[128,2048]{1,0:T(8,128)(2,1)S(1)} collective-permute-done((bf16[128,2048]{1,0:T(8,128)(2,1)S(1)}, bf16[128,2048]{1,0:T(8,128)(2,1)S(1)}, u32[]{:S(2)}, u32[]{:S(2)}) %collective-permute-start.32) | collective-permute-done | bytes 524320 | tf_op jit(solution)/shard_map/ppermute | solution.py:228
  407.2 4.5 collective-permute-done.35
  411.7 5.8 %fusion.116 = (bf16[512,2048]{1,0:T(8,128)(2,1)S(1)}, f32[512,2048]{1,0:T(8,128)}) fusion(bf16[512,2048]{1,0:T(8,128)(2,1)} %collective-permute-done.35, bf16[2048,2]{1,0:T(8,128)(2,1)} %dynamic-slice_bitcast_fusion, bf16[2048,512]{1,0:T(8,128)(2,1)S(1)} %copy-done.27, bf16[1024,512]{1,0:T(8,128)(2,1)S(1)} %copy-done.5, ...), kind=kOutput, calls=%fused_computation.287 | convolution fusion | flops 1086345216 | bytes 11546624 | tf_op jit(solution)/shard_map/dot_general | solution.py:37
  435.2 11.4 %collective-permute-done.36 = bf16[128,2048]{1,0:T(8,128)(2,1)} collective-permute-done((bf16[128,2048]{1,0:T(8,128)(2,1)}, bf16[128,2048]{1,0:T(8,128)(2,1)}, u32[]{:S(2)}, u32[]{:S(2)}) %collective-permute-start.36) | collective-permute-done | bytes 524320 | tf_op jit(solution)/shard_map/ppermute | solution.py:228
  463.3 4.5 all-to-all-start.4
  476.0 8.6 %all-to-all-done.4 = bf16[8,64,1152]{2,1,0:T(8,128)(2,1)} async-done(((bf16[8,64,1152]{2,1,0:T(8,128)(2,1)}), bf16[8,64,1152]{2,1,0:T(8,128)(2,1)}, u32[]{:S(2)}, u32[]{:S(2)}) %all-to-all-start.4) | async-done | bytes 1179680 | tf_op jit(solution)/shard_map/all_to_all | solution.py:341
  484.6 28.0 %reduce-scatter.4.cloned.1.call-done = bf16[512,768]{0,1:T(8,128)(2,1)} async-done(((bf16[2048,768]{0,1:T(8,128)(2,1)}), bf16[512,768]{0,1:T(8,128)(2,1)}) %reduce-scatter.4.cloned.1.call-update) | async-done | bytes 786448 | tf_op jit(solution)/shard_map/reduce_scatter | solution.py:344
  542.4 13.7 %fusion.99 = (bf16[64,24576]{1,0:T(8,128)(2,1)}, f32[64,24576]{1,0:T(8,128)}, f32[64,24576]{1,0:T(8,128)}, f32[64,24576]{1,0:T(8,128)}) fusion(f32[64,24576]{1,0:T(8,128)} %param.16, f32[]{:T(128)S(6)} %min.3, bf16[64,24576]{1,0:T(8,128)(2,1)S(1)} %constant_dynamic-update-slice_fusion.22, f32[64,24576]{1,0:T(8,128)} %param.18, f32[64,24576]{1,0:T(8,128)} %param.17), kind=kLoop, calls=%fused_computation.274 | loop fusion | flops 26738688 | bytes 44040196 | tf_op jit(solution)/shard_map/convert_element_type | solution.py:103
  (418 shorter events, 237.3 us)
Async XLA Ops:
  11.6 17.9 %all-to-all-start = ((bf16[8,64,768]{2,1,0:T(8,128)(2,1)}), bf16[8,64,768]{2,1,0:T(8,128)(2,1)}, u32[]{:S(2)}, u32[]{:S(2)}) async-start(bf16[8,64,768]{2,1,0:T(8,128)(2,1)} %copy.108), calls=%async_computation | async-start | bytes 1572864 | tf_op jit(solution)/shard_map/all_to_all | solution.py:341
  16.8 94.6 %all-gather.4.cloned.1.call-start = ((), (), s32[]{:S(2)}) async-start(), calls=%async_computation.9 | async-start | bytes 3932160 | tf_op jit(solution)/shard_map/all_gather | solution.py:371
  31.4 21.7 %all-to-all-start.1 = ((bf16[8,64,1152]{2,1,0:T(8,128)(2,1)}), bf16[8,64,1152]{2,1,0:T(8,128)(2,1)S(1)}, u32[]{:S(2)}, u32[]{:S(2)}) async-start(bf16[8,64,1152]{2,1,0:T(8,128)(2,1)} %copy.109), calls=%async_computation.1 | async-start | bytes 2359296 | tf_op jit(solution)/shard_map/all_to_all | solution.py:341
  35.0 186.2 %all-gather.6.cloned.1.call-start = ((), (), s32[]{:S(2)}) async-start(), calls=%async_computation.10 | async-start | bytes 5898240 | tf_op jit(solution)/shard_map/all_gather | solution.py:379
  35.5 17.0 %collective-permute-start.3 = (bf16[18,512]{1,0:T(8,128)(2,1)S(1)}, bf16[18,512]{1,0:T(8,128)(2,1)S(1)}, u32[]{:S(2)}, u32[]{:S(2)}) collective-permute-start(bf16[18,512]{1,0:T(8,128)(2,1)S(1)} %add.409), channel_id=1, source_target_pairs={{0,6},{1,7},{2,4},{3,5},{4,2},{5,3},{6,0},{7,1},{8,14},{9,15},{10,... | collective-permute-start | bytes 55304 | tf_op jit(solution)/shard_map/ppermute | solution.py:228
  54.0 25.0 %collective-permute-start.5 = (bf16[128,2048]{1,0:T(8,128)(2,1)S(1)}, bf16[128,2048]{1,0:T(8,128)(2,1)S(1)}, u32[]{:S(2)}, u32[]{:S(2)}) collective-permute-start(bf16[128,2048]{1,0:T(8,128)(2,1)S(1)} %bitcast.167), channel_id=1, source_target_pairs={{0,4},{1,5},{2,6},{3,7},{4,0},{5,1},{6,2},{7,3},{8,12},{9,13},{10,... | collective-permute-start | bytes 1572872 | tf_op jit(solution)/shard_map/ppermute | solution.py:228
  54.6 24.3 %collective-permute-start.6 = (bf16[128,2048]{1,0:T(8,128)(2,1)S(1)}, bf16[128,2048]{1,0:T(8,128)(2,1)S(1)}, u32[]{:S(2)}, u32[]{:S(2)}) collective-permute-start(bf16[128,2048]{1,0:T(8,128)(2,1)S(1)} %bitcast.168), channel_id=1, source_target_pairs={{0,6},{1,7},{2,4},{3,5},{4,2},{5,3},{6,0},{7,1},{8,14},{9,15},{10,... | collective-permute-start | bytes 1572872 | tf_op jit(solution)/shard_map/ppermute | solution.py:228
  80.5 24.8 %collective-permute-start.7 = (bf16[512,2048]{1,0:T(8,128)(2,1)}, bf16[512,2048]{1,0:T(8,128)(2,1)}, u32[]{:S(2)}, u32[]{:S(2)}) collective-permute-start(bf16[512,2048]{1,0:T(8,128)(2,1)} %pad_maximum_fusion.4), channel_id=1, source_target_pairs={{0,1},{1,0},{2,3},{3,2},{4,5},{5,4},{6,7},{7,6},{8,9},{9,8},{10,11... | collective-permute-start | bytes 6291464 | tf_op jit(solution)/shard_map/ppermute | solution.py:228
  99.3 32.5 %all-to-all-start.2 = ((bf16[8,64,1152]{2,1,0:T(8,128)(2,1)}), bf16[8,64,1152]{2,1,0:T(8,128)(2,1)}, u32[]{:S(2)}, u32[]{:S(2)}) async-start(bf16[8,64,1152]{2,1,0:T(8,128)(2,1)} %copy.118), calls=%async_computation.2 | async-start | bytes 2359296 | tf_op jit(solution)/shard_map/all_to_all | solution.py:341
  103.7 170.4 %all-gather.8.cloned.1.call-start = ((), (), s32[]{:S(2)}) async-start(), calls=%async_computation.11 | async-start | bytes 5898240 | tf_op jit(solution)/shard_map/all_gather | solution.py:411
  111.4 20.4 %collective-permute-start.11 = (bf16[128,2048]{1,0:T(8,128)(2,1)}, bf16[128,2048]{1,0:T(8,128)(2,1)}, u32[]{:S(2)}, u32[]{:S(2)}) collective-permute-start(bf16[128,2048]{1,0:T(8,128)(2,1)} %bitcast.3), channel_id=1, source_target_pairs={{0,2},{1,3},{2,0},{3,1},{4,6},{5,7},{6,4},{7,5},{8,10},{9,11},{10,... | collective-permute-start | bytes 1572872 | tf_op jit(solution)/shard_map/ppermute | solution.py:228
  113.3 18.5 %collective-permute-start.12 = (bf16[128,2048]{1,0:T(8,128)(2,1)}, bf16[128,2048]{1,0:T(8,128)(2,1)}, u32[]{:S(2)}, u32[]{:S(2)}) collective-permute-start(bf16[128,2048]{1,0:T(8,128)(2,1)} %bitcast.3), channel_id=1, source_target_pairs={{0,4},{1,5},{2,6},{3,7},{4,0},{5,1},{6,2},{7,3},{8,12},{9,13},{10,... | collective-permute-start | bytes 1572872 | tf_op jit(solution)/shard_map/ppermute | solution.py:228
  114.8 28.2 %collective-permute-start.13 = (bf16[128,2048]{1,0:T(8,128)(2,1)}, bf16[128,2048]{1,0:T(8,128)(2,1)}, u32[]{:S(2)}, u32[]{:S(2)}) collective-permute-start(bf16[128,2048]{1,0:T(8,128)(2,1)} %bitcast.3), channel_id=1, source_target_pairs={{0,6},{1,7},{2,4},{3,5},{4,2},{5,3},{6,0},{7,1},{8,14},{9,15},{10,... | collective-permute-start | bytes 1572872 | tf_op jit(solution)/shard_map/ppermute | solution.py:228
  155.7 25.8 %collective-permute-start.15 = (bf16[128,2048]{1,0:T(8,128)(2,1)}, bf16[128,2048]{1,0:T(8,128)(2,1)}, u32[]{:S(2)}, u32[]{:S(2)}) collective-permute-start(bf16[128,2048]{1,0:T(8,128)(2,1)} %get-tuple-element.161), channel_id=1, source_target_pairs={{0,6},{1,7},{2,4},{3,5},{4,2},{5,3},{6,0},{7,1},{8,14},{9,15},{10,... | collective-permute-start | bytes 1572872 | tf_op jit(solution)/shard_map/ppermute | solution.py:228
  161.4 53.5 %collective-permute-start.22 = (bf16[512,2048]{1,0:T(8,128)(2,1)}, bf16[512,2048]{1,0:T(8,128)(2,1)}, u32[]{:S(2)}, u32[]{:S(2)}) collective-permute-start(bf16[512,2048]{1,0:T(8,128)(2,1)} %pad_maximum_fusion.5), channel_id=1, source_target_pairs={{0,1},{1,0},{2,3},{3,2},{4,5},{5,4},{6,7},{7,6},{8,9},{9,8},{10,11... | collective-permute-start | bytes 6291464 | tf_op jit(solution)/shard_map/ppermute | solution.py:228
  161.4 261.9 %reduce-scatter.8.cloned.1.call-start = ((), (), s32[]{:S(2)}) async-start(), calls=%async_computation.14 | async-start | bytes 5898240 | tf_op jit(solution)/shard_map/reduce_scatter | solution.py:344
  186.4 23.8 %collective-permute-start.19 = (bf16[128,2048]{1,0:T(8,128)(2,1)S(1)}, bf16[128,2048]{1,0:T(8,128)(2,1)S(1)}, u32[]{:S(2)}, u32[]{:S(2)}) collective-permute-start(bf16[128,2048]{1,0:T(8,128)(2,1)S(1)} %get-tuple-element.142), channel_id=1, source_target_pairs={{0,4},{1,5},{2,6},{3,7},{4,0},{5,1},{6,2},{7,3},{8,12},{9,13},{10,... | collective-permute-start | bytes 1572872 | tf_op jit(solution)/shard_map/ppermute | solution.py:228
  186.7 23.4 %collective-permute-start.20 = (bf16[128,2048]{1,0:T(8,128)(2,1)S(1)}, bf16[128,2048]{1,0:T(8,128)(2,1)S(1)}, u32[]{:S(2)}, u32[]{:S(2)}) collective-permute-start(bf16[128,2048]{1,0:T(8,128)(2,1)S(1)} %get-tuple-element.142), channel_id=1, source_target_pairs={{0,6},{1,7},{2,4},{3,5},{4,2},{5,3},{6,0},{7,1},{8,14},{9,15},{10,... | collective-permute-start | bytes 1572872 | tf_op jit(solution)/shard_map/ppermute | solution.py:228
  242.5 218.4 %reduce-scatter.6.cloned.1.call-start = ((), (), s32[]{:S(2)}) async-start(), calls=%async_computation.13 | async-start | bytes 5898240 | tf_op jit(solution)/shard_map/reduce_scatter | solution.py:344
  286.6 15.9 %collective-permute-start.23 = (bf16[512,2048]{1,0:T(8,128)(2,1)}, bf16[512,2048]{1,0:T(8,128)(2,1)}, u32[]{:S(2)}, u32[]{:S(2)}) collective-permute-start(bf16[512,2048]{1,0:T(8,128)(2,1)} %add_convert_fusion.1), channel_id=1, source_target_pairs={{0,1},{1,0},{2,3},{3,2},{4,5},{5,4},{6,7},{7,6},{8,9},{9,8},{10,11... | collective-permute-start | bytes 6291464 | tf_op jit(solution)/shard_map/ppermute | solution.py:228
  297.9 214.7 %reduce-scatter.4.cloned.1.call-start = ((), (), s32[]{:S(2)}) async-start(), calls=%async_computation.12 | async-start | bytes 3932160 | tf_op jit(solution)/shard_map/reduce_scatter | solution.py:344
  310.7 23.7 %collective-permute-start.24 = (bf16[128,2048]{1,0:T(8,128)(2,1)S(1)}, bf16[128,2048]{1,0:T(8,128)(2,1)S(1)}, u32[]{:S(2)}, u32[]{:S(2)}) collective-permute-start(bf16[128,2048]{1,0:T(8,128)(2,1)S(1)} %get-tuple-element.167), channel_id=1, source_target_pairs={{0,6},{1,7},{2,4},{3,5},{4,2},{5,3},{6,0},{7,1},{8,14},{9,15},{10,... | collective-permute-start | bytes 1572872 | tf_op jit(solution)/shard_map/ppermute | solution.py:228
  338.4 24.2 %collective-permute-start.28 = (bf16[128,2048]{1,0:T(8,128)(2,1)S(1)}, bf16[128,2048]{1,0:T(8,128)(2,1)S(1)}, u32[]{:S(2)}, u32[]{:S(2)}) collective-permute-start(bf16[128,2048]{1,0:T(8,128)(2,1)S(1)} %get-tuple-element.139), channel_id=1, source_target_pairs={{0,4},{1,5},{2,6},{3,7},{4,0},{5,1},{6,2},{7,3},{8,12},{9,13},{10,... | collective-permute-start | bytes 1572872 | tf_op jit(solution)/shard_map/ppermute | solution.py:228
  339.8 22.7 %collective-permute-start.29 = (bf16[128,2048]{1,0:T(8,128)(2,1)S(1)}, bf16[128,2048]{1,0:T(8,128)(2,1)S(1)}, u32[]{:S(2)}, u32[]{:S(2)}) collective-permute-start(bf16[128,2048]{1,0:T(8,128)(2,1)S(1)} %get-tuple-element.139), channel_id=1, source_target_pairs={{0,6},{1,7},{2,4},{3,5},{4,2},{5,3},{6,0},{7,1},{8,14},{9,15},{10,... | collective-permute-start | bytes 1572872 | tf_op jit(solution)/shard_map/ppermute | solution.py:228
  341.6 25.2 %collective-permute-start.31 = (bf16[512,2048]{1,0:T(8,128)(2,1)S(1)}, bf16[512,2048]{1,0:T(8,128)(2,1)S(1)}, u32[]{:S(2)}, u32[]{:S(2)}) collective-permute-start(bf16[512,2048]{1,0:T(8,128)(2,1)S(1)} %add_convert_fusion), channel_id=1, source_target_pairs={{0,1},{1,0},{2,3},{3,2},{4,5},{5,4},{6,7},{7,6},{8,9},{9,8},{10,11... | collective-permute-start | bytes 6291464 | tf_op jit(solution)/shard_map/ppermute | solution.py:228
  368.8 17.2 %collective-permute-start.34 = (bf16[128,2048]{1,0:T(8,128)(2,1)S(1)}, bf16[128,2048]{1,0:T(8,128)(2,1)S(1)}, u32[]{:S(2)}, u32[]{:S(2)}) collective-permute-start(bf16[128,2048]{1,0:T(8,128)(2,1)S(1)} %get-tuple-element.165), channel_id=1, source_target_pairs={{0,4},{1,5},{2,6},{3,7},{4,0},{5,1},{6,2},{7,3},{8,12},{9,13},{10,... | collective-permute-start | bytes 1572872 | tf_op jit(solution)/shard_map/ppermute | solution.py:228
  370.3 15.7 %collective-permute-start.33 = (bf16[128,2048]{1,0:T(8,128)(2,1)S(1)}, bf16[128,2048]{1,0:T(8,128)(2,1)S(1)}, u32[]{:S(2)}, u32[]{:S(2)}) collective-permute-start(bf16[128,2048]{1,0:T(8,128)(2,1)S(1)} %get-tuple-element.166), channel_id=1, source_target_pairs={{0,2},{1,3},{2,0},{3,1},{4,6},{5,7},{6,4},{7,5},{8,10},{9,11},{10,... | collective-permute-start | bytes 1572872 | tf_op jit(solution)/shard_map/ppermute | solution.py:228
  370.9 24.7 %collective-permute-start.32 = (bf16[128,2048]{1,0:T(8,128)(2,1)S(1)}, bf16[128,2048]{1,0:T(8,128)(2,1)S(1)}, u32[]{:S(2)}, u32[]{:S(2)}) collective-permute-start(bf16[128,2048]{1,0:T(8,128)(2,1)S(1)} %get-tuple-element.164), channel_id=1, source_target_pairs={{0,6},{1,7},{2,4},{3,5},{4,2},{5,3},{6,0},{7,1},{8,14},{9,15},{10,... | collective-permute-start | bytes 1572872 | tf_op jit(solution)/shard_map/ppermute | solution.py:228
  420.7 25.8 %collective-permute-start.36 = (bf16[128,2048]{1,0:T(8,128)(2,1)}, bf16[128,2048]{1,0:T(8,128)(2,1)}, u32[]{:S(2)}, u32[]{:S(2)}) collective-permute-start(bf16[128,2048]{1,0:T(8,128)(2,1)} %get-tuple-element.158), channel_id=1, source_target_pairs={{0,6},{1,7},{2,4},{3,5},{4,2},{5,3},{6,0},{7,1},{8,14},{9,15},{10,... | collective-permute-start | bytes 1572872 | tf_op jit(solution)/shard_map/ppermute | solution.py:228
  425.8 35.1 %all-to-all-start.3 = ((bf16[8,64,1152]{2,1,0:T(8,128)(2,1)}), bf16[8,64,1152]{2,1,0:T(8,128)(2,1)}, u32[]{:S(2)}, u32[]{:S(2)}) async-start(bf16[8,64,1152]{2,1,0:T(8,128)(2,1)} %bitcast.24), calls=%async_computation.6 | async-start | bytes 2359296 | tf_op jit(solution)/shard_map/all_to_all | solution.py:341
  463.3 21.4 %all-to-all-start.4 = ((bf16[8,64,1152]{2,1,0:T(8,128)(2,1)}), bf16[8,64,1152]{2,1,0:T(8,128)(2,1)}, u32[]{:S(2)}, u32[]{:S(2)}) async-start(bf16[8,64,1152]{2,1,0:T(8,128)(2,1)} %bitcast.172), calls=%async_computation.7 | async-start | bytes 2359296 | tf_op jit(solution)/shard_map/all_to_all | solution.py:341
  522.2 19.7 %all-to-all-start.5 = ((bf16[8,64,768]{2,1,0:T(8,128)(2,1)}), bf16[8,64,768]{2,1,0:T(8,128)(2,1)S(1)}, u32[]{:S(2)}, u32[]{:S(2)}) async-start(bf16[8,64,768]{2,1,0:T(8,128)(2,1)} %bitcast.28), calls=%async_computation.8 | async-start | bytes 1572864 | tf_op jit(solution)/shard_map/all_to_all | solution.py:341
  (102 other events, 1019.0 us)
Sparse Core Ops, SparseCore 0:
  29.6 65.3 all-gather.3
  96.6 87.9 all-gather.5
  186.2 87.8 all-gather.7
  276.8 83.6 reduce-scatter.7
  363.3 85.7 reduce-scatter.5
  451.8 60.7 reduce-scatter.3

commit v5 on v4

--- a/solution.py
+++ b/solution.py
@@ -14,7 +14,7 @@
 TOK_DEV = 128
 STEP = 5
 QUERY_ROWS = 256
-KERNEL_VMEM = 40 * 2**20
+KERNEL_VMEM = 32 * 2**20
 
 eps = 1e-06
 theta = 1000000.0
@@ -220,6 +220,26 @@
     return call_kernel(kernel, shapes, scratch, *args)
 
 
+def squares_kernel(part, out):
+    total = jnp.zeros((1, 128), f32)
+    for start in range(0, part.shape[1], 128):
+        value = part[:, start : start + 128].astype(f32)
+        total += jnp.sum(value * value, axis=0, keepdims=True)
+    out[:, :] = total
+
+
+def lane_squares(part):
+    spec = pl.BlockSpec(memory_space=pltpu.VMEM)
+    return pl.pallas_call(
+        squares_kernel,
+        out_shape=jax.ShapeDtypeStruct((1, 128), f32),
+        in_specs=[spec],
+        out_specs=spec,
+        compiler_params=pltpu.CompilerParams(vmem_limit_bytes=4 * 2**20),
+        cost_estimate=pl.CostEstimate(flops=2 * 10**10, bytes_accessed=10**6, transcendentals=0),
+    )(part)
+
+
 def tie(*values):
     return lax.optimization_barrier(values)
 
@@ -359,12 +379,12 @@
         axis=2,
     )
     attn_rows = to_columns(attn_blocks)
-    half_ff = wff // 2
-    mlp_blocks = [blocks(start_mlp + i * FF, FF) for i in range(3)]
+    part_ff = (5 * wff // 6, wff // 6)
 
     def unit_blocks(i):
+        start = sum(part_ff[:i]) * groups
         return jnp.concatenate(
-            [b[:, :, i * half_ff : (i + 1) * half_ff] for b in mlp_blocks], axis=2
+            [blocks(start_mlp + k * FF + start, part_ff[i] * groups) for k in range(3)], axis=2
         )
 
     first_blocks, attn_rows = tie(unit_blocks(0), attn_rows)
@@ -408,17 +428,18 @@
     inputs = tokens[0].astype(f32)
     gated, mlp_rows[1], *grad_branch = tie(gated, mlp_rows[1], *grad_branch)
     grad_branch = gather_cores(grad_branch)
+    mlp_w[0], mlp_rows[1] = tie(mlp_w[0], mlp_rows[1])
     mlp_w.append(lax.all_gather(mlp_rows[1], "dp", axis=0, tiled=True))
     middle = inputs + scatter_cp([gated], [attn_w[:, win:]])
 
     normed_two = rms(middle)
     kept_two = gather_cp((normed_two * gain_two).astype(bf16))
-    gu_w = [w[:, : 2 * half_ff] for w in mlp_w]
-    down_w = [w[:, 2 * half_ff :] for w in mlp_w]
-    hidden, grad_gu, mlp_grads, mlp_terms = [], [], [], []
+    gu_w = [w[:, : 2 * n] for w, n in zip(mlp_w, part_ff)]
+    down_w = [w[:, 2 * n :] for w, n in zip(mlp_w, part_ff)]
+    hidden, grad_gu = [], []
     for i in range(2):
         gate_up = dot(kept_two, gu_w[i])
-        gate, upper = gate_up[:, :half_ff], gate_up[:, half_ff:]
+        gate, upper = gate_up[:, : part_ff[i]], gate_up[:, part_ff[i] :]
         sig_gate = jax.nn.sigmoid(gate)
         hidden.append((gate * sig_gate * upper).astype(bf16))
         grad_hidden = dot(grad_branch, down_w[i])
@@ -426,21 +447,27 @@
         grad_upper = grad_hidden * gate * sig_gate
         grad_gu.append(jnp.concatenate([grad_gate, grad_upper], axis=1).astype(bf16))
 
+    def side_by_side(terms):
+        full = jnp.zeros((features, sum(term.shape[1] for term in terms)), bf16)
+        start = 0
+        for term in terms:
+            full = lax.dynamic_update_slice_in_dim(full, term.astype(bf16), start, 1)
+            start += term.shape[1]
+        return full
+
     def mlp_grad(i):
-        terms = [dot_tn(kept_two, grad_gu[i]), dot_tn(grad_branch, hidden[i])]
-        return jnp.concatenate(terms, axis=1).astype(bf16)
-
-    first_grad, kept_two = tie(mlp_grad(0), kept_two)
-    mlp_terms.append(sum_rows(first_grad))
+        return side_by_side([dot_tn(kept_two, grad_gu[i]), dot_tn(grad_branch, hidden[i])])
+
+    first_grad, grad_gu[0] = tie(mlp_grad(0), grad_gu[0])
+    mlp_term = sum_rows(first_grad)
     left, started = scatter_first(grad_gu, gu_w)
-    started, *grad_gu = tie(started, *grad_gu)
-    second_grad, *left = tie(mlp_grad(1), *left)
-    mlp_terms.append(sum_rows(second_grad))
-    own_two, far_two = scatter_cores(left, gu_w, started)
-    far_two, *hidden = tie(far_two, *hidden)
+    near_two, far_two = scatter_cores(left, gu_w, started)
+    far_two, grad_gu[1], *hidden = tie(far_two, grad_gu[1], *hidden)
+    second_grad = mlp_grad(1)
     left, started = scatter_first(hidden, down_w)
     tail, far_tail = scatter_cores(left, down_w, started)
-    grad_two = scatter_chips(own_two, far_two)
+    grad_two = scatter_chips(near_two, far_two)
+    grad_two, second_grad, far_tail = tie(grad_two, second_grad, far_tail)
     gain_two_term = jnp.sum(grad_two * normed_two, axis=0)
     grad_out = cotangent[0].astype(f32)
     grad_middle = grad_out + norm_back(middle, grad_two * gain_two)
@@ -453,13 +480,13 @@
         own_q, own_kv, proj, sig, *info, heads, tops, queries, keys, values, grad_gated
     )
     grad_logits = grad_logits.astype(bf16)
-    grad_proj, tail = tie(grad_proj, tail)
     result = middle + tail
-    attn_grad = jnp.concatenate(
-        [dot_tn(kept_one, grad_proj), dot_tn(grad_attn_branch, gated)], axis=1
-    ).astype(bf16)
-    attn_grad, late_proj = tie(attn_grad, grad_proj)
-    attn_term = sum_rows(attn_grad)
+    out_grad = dot_tn(grad_attn_branch, gated).astype(bf16)
+    in_grad = dot_tn(kept_one, grad_proj).astype(bf16)
+    late_grad, late_proj = tie(
+        side_by_side([second_grad, out_grad, in_grad]), grad_proj
+    )
+    late_term = sum_rows(late_grad)
     gate_term = dot_tn(kept_one, grad_logits)
     full_in = jnp.concatenate([attn_w[:, :win], gate_w], axis=1)
     grad_all = jnp.concatenate([late_proj, grad_logits], axis=1)
@@ -486,25 +513,26 @@
     def wide(part):
         return part.transpose(1, 0, 2).reshape(wr, -1).astype(f32)
 
-    mlp_own = [to_owner(mlp_terms[0])]
-    mlp_terms[1], mlp_own[0] = tie(mlp_terms[1], mlp_own[0])
-    mlp_own.append(to_owner(mlp_terms[1]))
-    attn_term, result, grad_input, small_sum, mlp_own[1] = tie(
-        attn_term, result, grad_input, small_sum, mlp_own[1]
-    )
-    attn_own = to_owner(attn_term)
+    mlp_own = to_owner(mlp_term)
+    late_term, result, grad_input, small_sum, mlp_own = tie(
+        late_term, result, grad_input, small_sum, mlp_own
+    )
+    late_own = to_owner(late_term)
+    own_parts = (mlp_own, late_own[:, :, : 3 * part_ff[1]])
+    cut = 3 * part_ff[1]
+    out_own, attn_own = late_own[:, :, cut : cut + wq], late_own[:, :, cut + wq :]
     k_own = kv_sum(attn_own[:, :, wq : wq + wkv])
     v_own = kv_sum(attn_own[:, :, wq + wkv : win])
     if copies == 1:
-        attn_squares = squares_of(attn_term)
+        late_squares = lane_squares(late_term)
     else:
-        attn_squares = squares_of(attn_term[:, :wq]) + squares_of(attn_term[:, win:])
-        attn_squares = attn_squares + squares_of(k_own) + squares_of(v_own)
-    local_squares = squares_of(mlp_terms[0]) + squares_of(mlp_terms[1]) + attn_squares
-    local_squares = sum_cp(sum_dp(jnp.full((1, 128), local_squares, f32)))
+        late_squares = squares_of(late_term[:, : cut + 2 * wq]) + squares_of(k_own)
+        late_squares = jnp.full((1, 128), (late_squares + squares_of(v_own)) / 128, f32)
+    early_squares = squares_of(mlp_term) / 128
+    local_squares = sum_cp(sum_dp(late_squares + jnp.full((1, 128), early_squares, f32)))
     edge = (HEADS + 2) * features // 128
     qk_grad = small_sum[edge:]
-    total = local_squares[0, 0] + squares_of(small_sum)
+    total = jnp.sum(local_squares) + squares_of(small_sum)
     norm_value = jnp.sqrt(total)
     factor = jnp.minimum(1.0, 1.0 / (norm_value + 1e-06))
     small_grad = lax.dynamic_slice_in_dim(
@@ -515,11 +543,12 @@
             wide(attn_own[:, :, :wq]),
             wide(k_own),
             wide(v_own),
-            wide(attn_own[:, :, win:]),
+            wide(out_own),
         ]
         + [
-            wide(jnp.concatenate([m[:, :, i * half_ff : (i + 1) * half_ff] for m in mlp_own], axis=2))
+            wide(m[:, :, i * n : (i + 1) * n])
             for i in range(3)
+            for m, n in zip(own_parts, part_ff)
         ],
         axis=1,
     )

time: 572 us -> 562 us (0.983)
  other arithmetic: 62.4 us -> 52 us
  matrix products: 89 us -> 98.1 us
    ppermute x53, waiting for transfers between devices: 173 us -> 206 us  [shift(): lax.ppermute(value, axis, [(i, i ^ offset) for i in range(lax.axis_size(a...]
    all_gather x1, waiting for transfers between devices: 23.3 us -> 0.01 us  [local(): mlp_w.append(lax.all_gather(mlp_rows[1], 'dp', axis=0, tiled=True))]
    reduce_scatter x3 -> x2, waiting for transfers between devices: 28 us -> 15 us  [sum_rows(): return lax.psum_scatter(part, 'dp', scatter_dimension=0, tiled=True)]
    concatenate x5 -> x2, other arithmetic: 9.62 us -> 0.95 us  [unit_blocks(): jnp.concatenate([blocks(start_mlp + k * FF + start, part_ff[i] * groups)...]
    dynamic_update_slice x0 -> x2, other arithmetic: none -> 8.1 us  [side_by_side(): full = lax.dynamic_update_slice_in_dim(full, term.astype(bf16), start, 1)]
    all_gather x1, waiting for transfers between devices: 0.01 us -> 7.66 us  [local(): mlp_w = [lax.all_gather(mlp_rows[0], 'dp', axis=0, tiled=True)]]
    all_to_all x6 -> x5, waiting for transfers between devices: 18.6 us -> 12.1 us  [exchange(): return lax.all_to_all(part, 'cp', 0, 0, tiled=True)]
    dot_general x7, matrix products: 21.5 us -> 27.4 us  [dot_tn(): return lax.dot_general(a, b, contract_rows, preferred_element_type=f32)]
  transfers between devices with their start and end apart: 65 -> 63, of which waited for: 32 -> 35; matrix products, arithmetic and copies ran while one was open for 31% -> 30% of each run, Pallas kernels for 3% -> 3%
where the time goes in v5:
time: 562 us; the launch traced here: 554 us
  waiting for transfers between devices  241 us (43%)
  matrix products  98.1 us (17%)
  starting transfers between devices  76.9 us (14%)
  other arithmetic  52 us (9%)
  local copies, waits for them, and re-layouts  47.4 us (8%)
  Pallas kernels  20 us (4%)
  between operations  18.7 us (3%)
    ppermute x53, waiting for transfers between devices, shift(): lax.ppermute(value, axis, [(i, i ^ offset) for i in range(lax.axis_size(a...  206 us
    ppermute x53, starting transfers between devices, shift(): lax.ppermute(value, axis, [(i, i ^ offset) for i in range(lax.axis_size(a...  54.9 us
    dot_general x12, matrix products, dot_nt(): return lax.dot_general(a, b, contract_cols, preferred_element_type=f32)  40.2 us
    dot_general x7, matrix products, dot(): return jnp.dot(a, b, preferred_element_type=f32)  30.5 us
    dot_general x7, matrix products, dot_tn(): return lax.dot_general(a, b, contract_rows, preferred_element_type=f32)  27.4 us
    unnamed x166, local copies, waits for them, and re-layouts  22.3 us
    all_to_all x5, starting transfers between devices, exchange(): return lax.all_to_all(part, 'cp', 0, 0, tiled=True)  21.1 us
    pallas_call x2, Pallas kernels, call_kernel(): pl.pallas_call(kernel, out_shape=[jax.ShapeDtypeStruct(shape, dtype) for...  18.5 us
  transfers between devices with their start and end apart: 63, of which 35 were waited for; matrix products, arithmetic and copies ran while one was open for 30% of the time, Pallas kernels for 3%

profile of v5, /device:TPU:0, one launch (start us, length us, event | category | flops | bytes accessed | tf_op | source)
XLA Modules:
  0.0 554.4 jit_solution(8932271940176188680)
XLA Ops:
  12.3 5.2 all-to-all-start
  18.1 12.1 %all-to-all-done = bf16[8,64,768]{2,1,0:T(8,128)(2,1)} async-done(((bf16[8,64,768]{2,1,0:T(8,128)(2,1)}), bf16[8,64,768]{2,1,0:T(8,128)(2,1)}, u32[]{:S(2)}, u32[]{:S(2)}) %all-to-all-start) | async-done | bytes 786464 | tf_op jit(solution)/shard_map/all_to_all | solution.py:361
  41.6 19.9 %collective-permute-done.3 = bf16[18,512]{1,0:T(8,128)(2,1)S(1)} collective-permute-done((bf16[18,512]{1,0:T(8,128)(2,1)S(1)}, bf16[18,512]{1,0:T(8,128)(2,1)S(1)}, u32[]{:S(2)}, u32[]{:S(2)}) %collective-permute-start.3) | collective-permute-done | bytes 18464 | tf_op jit(solution)/shard_map/ppermute | solution.py:248
  67.6 9.4 %collective-permute-done.4 = bf16[128,2048]{1,0:T(8,128)(2,1)S(1)} collective-permute-done((bf16[128,2048]{1,0:T(8,128)(2,1)S(1)}, bf16[128,2048]{1,0:T(8,128)(2,1)S(1)}, u32[]{:S(2)}, u32[]{:S(2)}) %collective-permute-start.4) | collective-permute-done | bytes 524320 | tf_op jit(solution)/shard_map/ppermute | solution.py:248
  77.0 10.9 %collective-permute-done.5 = bf16[128,2048]{1,0:T(8,128)(2,1)S(1)} collective-permute-done((bf16[128,2048]{1,0:T(8,128)(2,1)S(1)}, bf16[128,2048]{1,0:T(8,128)(2,1)S(1)}, u32[]{:S(2)}, u32[]{:S(2)}) %collective-permute-start.5) | collective-permute-done | bytes 524320 | tf_op jit(solution)/shard_map/ppermute | solution.py:248
  121.7 5.3 fusion.90.proj
  127.0 7.5 %shard_map.252 = (bf16[1024,256]{1,0:T(8,128)(2,1)S(1)}, f32[1024,256]{1,0:T(8,128)S(1)}, f32[1024,2]{1,0:T(8,128)S(1)}, bf16[1024,256]{1,0:T(8,128)(2,1)S(1)}, ...) custom-call(f32[1024,512]{1,0:T(8,128)S(1)} %fusion.90.proj, f32[1024,2]{1,0:T(8,128)S(1)} %copy-done.2, ...), custom_call_target="tpu_custom_call" | custom-call | flops 10000000 | bytes 100000 | tf_op jit(solution)/shard_map/pallas_call | solution.py:195
  138.6 6.7 %collective-permute-done.12 = bf16[128,2048]{1,0:T(8,128)(2,1)} collective-permute-done((bf16[128,2048]{1,0:T(8,128)(2,1)}, bf16[128,2048]{1,0:T(8,128)(2,1)}, u32[]{:S(2)}, u32[]{:S(2)}) %collective-permute-start.12) | collective-permute-done | bytes 524320 | tf_op jit(solution)/shard_map/ppermute | solution.py:248
  145.3 12.7 %convolution_convert_fusion.3 = bf16[512,2048]{1,0:T(8,128)(2,1)S(1)} fusion(bf16[2048,768]{1,0:T(8,128)(2,1)} %all-gather.4.cloned.1.call-done, bf16[1024,256]{1,0:T(8,128)(2,1)} %copy-done.10), kind=kOutput, calls=%fused_computation.30 | convolution fusion | flops 537919488 | bytes 3407872 | tf_op jit(solution)/shard_map/dot_general | solution.py:37
  169.9 8.6 %collective-permute-done.17 = bf16[128,2048]{1,0:T(8,128)(2,1)S(1)} collective-permute-done((bf16[128,2048]{1,0:T(8,128)(2,1)S(1)}, bf16[128,2048]{1,0:T(8,128)(2,1)S(1)}, u32[]{:S(2)}, u32[]{:S(2)}) %collective-permute-start.17) | collective-permute-done | bytes 524320 | tf_op jit(solution)/shard_map/ppermute | solution.py:248
  180.8 10.1 %collective-permute-done.15 = bf16[128,2048]{1,0:T(8,128)(2,1)S(1)} collective-permute-done((bf16[128,2048]{1,0:T(8,128)(2,1)S(1)}, bf16[128,2048]{1,0:T(8,128)(2,1)S(1)}, u32[]{:S(2)}, u32[]{:S(2)}) %collective-permute-start.15) | collective-permute-done | bytes 524320 | tf_op jit(solution)/shard_map/ppermute | solution.py:248
  196.9 11.4 %collective-permute-done.18 = bf16[128,2048]{1,0:T(8,128)(2,1)S(1)} collective-permute-done((bf16[128,2048]{1,0:T(8,128)(2,1)S(1)}, bf16[128,2048]{1,0:T(8,128)(2,1)S(1)}, u32[]{:S(2)}, u32[]{:S(2)}) %collective-permute-start.18) | collective-permute-done | bytes 524320 | tf_op jit(solution)/shard_map/ppermute | solution.py:248
  208.2 8.6 %collective-permute-done.19 = bf16[128,2048]{1,0:T(8,128)(2,1)S(1)} collective-permute-done((bf16[128,2048]{1,0:T(8,128)(2,1)S(1)}, bf16[128,2048]{1,0:T(8,128)(2,1)S(1)}, u32[]{:S(2)}, u32[]{:S(2)}) %collective-permute-start.19) | collective-permute-done | bytes 524320 | tf_op jit(solution)/shard_map/ppermute | solution.py:248
  228.0 7.7 %all-gather.6.cloned.1.call-done = bf16[2048,1920]{1,0:T(8,128)(2,1)} async-done(((bf16[512,1920]{1,0:T(8,128)(2,1)}), bf16[2048,1920]{1,0:T(8,128)(2,1)}) %all-gather.6.cloned.1.call-update) | async-done | bytes 7864336 | tf_op jit(solution)/shard_map/all_gather | solution.py:399
  235.7 9.0 %fusion.8 = f32[1024,1280]{0,1:T(8,128)S(1)} fusion(bf16[1024,2048]{1,0:T(8,128)(2,1)} %constant_dynamic-update-slice_fusion.10, bf16[2048,1920]{1,0:T(8,128)(2,1)} %all-gather.6.cloned.1.call-done), kind=kOutput, calls=%fused_computation.22 | convolution fusion | flops 5368709120 | bytes 14680064 | tf_op jit(solution)/shard_map/dot_general | solution.py:33
  244.8 5.8 %multiply_convert_fusion.2 = (bf16[1024,640]{0,1:T(8,128)(2,1)S(1)}, bf16[1024,640]{0,1:T(8,128)(2,1)S(1)}, bf16[1024,640]{0,1:T(8,128)(2,1)S(1)}) fusion(f32[1024,1280]{0,1:T(8,128)S(1)} %fusion.8, bf16[1024,2048]{1,0:T(8,128)(2,1)S(1)} %copy-done.52, bf16[2048,1920]{1,0:T(8,128)(2,1)} %all-gather.6.cloned.1.call-done), kind=kOutput, calls=%fused_computation.36 | convolution fusion | flops 2694840320 | bytes 15990784 | tf_op jit(solution)/shard_map/dot_general | solution.py:33
  256.7 10.5 %convolution_convert_fusion = bf16[2048,1280]{0,1:T(8,128)(2,1)} fusion(bf16[1024,2048]{1,0:T(8,128)(2,1)} %constant_dynamic-update-slice_fusion.10, bf16[1024,640]{0,1:T(8,128)(2,1)S(1)} %get-tuple-element.139, bf16[1024,640]{0,1:T(8,128)(2,1)S(1)} %get-tuple-element.138), kind=kOutput, calls=%fused_computation.8 | convolution fusion | flops 5376573440 | bytes 12058624 | tf_op jit(solution)/shard_map/dot_general | solution.py:41
  267.3 7.9 %pad_maximum_fusion = bf16[2048,1920]{0,1:T(8,128)(2,1)} fusion(bf16[2048,640]{0,1:T(8,128)(2,1)} %convolution_convert_fusion.1, bf16[2048,1280]{0,1:T(8,128)(2,1)} %convolution_convert_fusion), kind=kLoop, calls=%fused_computation.7 | loop fusion | flops 15728640 | bytes 15728640 | tf_op jit(solution)/shard_map/dynamic_update_slice | solution.py:454
  275.7 7.8 %fusion.4 = f32[512,2048]{1,0:T(8,128)} fusion(bf16[2048,1920]{1,0:T(8,128)(2,1)} %all-gather.6.cloned.1.call-done, bf16[1024,1280]{0,1:T(8,128)(2,1)} %pad_maximum_fusion.1), kind=kOutput, calls=%fused_computation.18 | convolution fusion | flops 2684354560 | bytes 10747904 | tf_op jit(solution)/shard_map/dot_general | solution.py:37
  315.7 10.4 %collective-permute-done.24 = bf16[128,2048]{1,0:T(8,128)(2,1)S(1)} collective-permute-done((bf16[128,2048]{1,0:T(8,128)(2,1)S(1)}, bf16[128,2048]{1,0:T(8,128)(2,1)S(1)}, u32[]{:S(2)}, u32[]{:S(2)}) %collective-permute-start.24) | collective-permute-done | bytes 524320 | tf_op jit(solution)/shard_map/ppermute | solution.py:248
  334.1 11.4 %collective-permute-done.28 = bf16[128,2048]{1,0:T(8,128)(2,1)S(1)} collective-permute-done((bf16[128,2048]{1,0:T(8,128)(2,1)S(1)}, bf16[128,2048]{1,0:T(8,128)(2,1)S(1)}, u32[]{:S(2)}, u32[]{:S(2)}) %collective-permute-start.28) | collective-permute-done | bytes 524320 | tf_op jit(solution)/shard_map/ppermute | solution.py:248
  345.5 10.7 %collective-permute-done.29 = bf16[128,2048]{1,0:T(8,128)(2,1)S(1)} collective-permute-done((bf16[128,2048]{1,0:T(8,128)(2,1)S(1)}, bf16[128,2048]{1,0:T(8,128)(2,1)S(1)}, u32[]{:S(2)}, u32[]{:S(2)}) %collective-permute-start.29) | collective-permute-done | bytes 524320 | tf_op jit(solution)/shard_map/ppermute | solution.py:248
  363.7 11.0 %shard_map.253 = (bf16[1024,512]{1,0:T(8,128)(2,1)S(1)}, f32[1024,2]{1,0:T(8,128)S(1)}, f32[2,128]{1,0:T(2,128)S(1)}) custom-call(f32[1024,512]{1,0:T(8,128)S(1)} %fusion.90.proj, f32[1024,2]{1,0:T(8,128)S(1)} %copy-done.3, f32[1024,128]{1,0:T(8,128)S(1)} %get-tuple-element.186.cosine, f32[1024,128]{1,0:T(8,128)S(1)} %get-tuple-element.187.sine, ...), custom_call_target="tpu_custom_call" | custom-call | flops 10000000 | bytes 100000 | tf_op jit(solution)/shard_map/pallas_call | solution.py:195
  389.0 4.4 collective-permute-done.35
  402.5 9.3 %collective-permute-done.38 = bf16[128,2048]{1,0:T(8,128)(2,1)S(1)} collective-permute-done((bf16[128,2048]{1,0:T(8,128)(2,1)S(1)}, bf16[128,2048]{1,0:T(8,128)(2,1)S(1)}, u32[]{:S(2)}, u32[]{:S(2)}) %collective-permute-start.38) | collective-permute-done | bytes 524320 | tf_op jit(solution)/shard_map/ppermute | solution.py:248
  414.1 10.1 %collective-permute-done.36 = bf16[128,2048]{1,0:T(8,128)(2,1)S(1)} collective-permute-done((bf16[128,2048]{1,0:T(8,128)(2,1)S(1)}, bf16[128,2048]{1,0:T(8,128)(2,1)S(1)}, u32[]{:S(2)}, u32[]{:S(2)}) %collective-permute-start.36) | collective-permute-done | bytes 524320 | tf_op jit(solution)/shard_map/ppermute | solution.py:248
  440.3 4.3 all-to-all-start.3
  449.8 9.5 %collective-permute-done.32 = bf16[128,2048]{1,0:T(8,128)(2,1)} collective-permute-done((bf16[128,2048]{1,0:T(8,128)(2,1)}, bf16[128,2048]{1,0:T(8,128)(2,1)}, u32[]{:S(2)}, u32[]{:S(2)}) %collective-permute-start.32) | collective-permute-done | bytes 524320 | tf_op jit(solution)/shard_map/ppermute | solution.py:248
  463.6 18.4 %collective-permute-done.45 = f32[290,128]{1,0:T(8,128)S(1)} collective-permute-done((f32[290,128]{1,0:T(8,128)S(1)}, f32[290,128]{1,0:T(8,128)S(1)}, u32[]{:S(2)}, u32[]{:S(2)}) %collective-permute-start.45) | collective-permute-done | bytes 148512 | tf_op jit(solution)/shard_map/ppermute | solution.py:248
  485.9 15.0 %reduce-scatter.3.cloned.1.call-done.part = bf16[512,1152]{1,0:T(8,128)(2,1)} async-done(((bf16[2048,1152]{1,0:T(8,128)(2,1)}), bf16[512,1152]{1,0:T(8,128)(2,1)}) %reduce-scatter.3.cloned.1.call-update) | async-done | bytes 1179664 | tf_op jit(solution)/shard_map/reduce_scatter | solution.py:364
  518.3 9.2 %collective-permute-done.52 = f32[1,128]{1,0:T(1,128)S(1)} collective-permute-done((f32[1,128]{1,0:T(1,128)S(1)}, f32[1,128]{1,0:T(1,128)S(1)}, u32[]{:S(2)}, u32[]{:S(2)}) %collective-permute-start.52) | collective-permute-done | bytes 544 | tf_op jit(solution)/shard_map/ppermute | solution.py:248
  532.8 13.7 %fusion.102 = (bf16[64,24576]{1,0:T(8,128)(2,1)}, f32[64,24576]{1,0:T(8,128)}, f32[64,24576]{1,0:T(8,128)}, f32[64,24576]{1,0:T(8,128)}) fusion(f32[64,24576]{1,0:T(8,128)} %param.16, f32[]{:T(128)S(6)} %min.3, bf16[64,24576]{1,0:T(8,128)(2,1)S(1)} %bitcast_dynamic-update-slice_fusion, f32[64,24576]{1,0:T(8,128)} %param.18, f32[64,24576]{1,0:T(8,128)} %param.17), kind=kLoop, calls=%fused_computation.280 | loop fusion | flops 26738688 | bytes 44040196 | tf_op jit(solution)/shard_map/convert_element_type | solution.py:103
  (399 shorter events, 221.1 us)
Async XLA Ops:
  17.5 100.6 %all-gather.4.cloned.1.call-start = ((), (), s32[]{:S(2)}) async-start(), calls=%async_computation.7 | async-start | bytes 3932160 | tf_op jit(solution)/shard_map/all_gather | solution.py:391
  31.9 30.2 %all-to-all-start.1 = ((bf16[8,64,1920]{2,1,0:T(8,128)(2,1)}), bf16[8,64,1920]{2,1,0:T(8,128)(2,1)S(1)}, u32[]{:S(2)}, u32[]{:S(2)}) async-start(bf16[8,64,1920]{2,1,0:T(8,128)(2,1)} %copy.140), calls=%async_computation.1 | async-start | bytes 3932160 | tf_op jit(solution)/shard_map/all_to_all | solution.py:361
  35.5 200.1 %all-gather.6.cloned.1.call-start = ((), (), s32[]{:S(2)}) async-start(), calls=%async_computation.8 | async-start | bytes 9830400 | tf_op jit(solution)/shard_map/all_gather | solution.py:399
  37.9 23.5 %collective-permute-start.3 = (bf16[18,512]{1,0:T(8,128)(2,1)S(1)}, bf16[18,512]{1,0:T(8,128)(2,1)S(1)}, u32[]{:S(2)}, u32[]{:S(2)}) collective-permute-start(bf16[18,512]{1,0:T(8,128)(2,1)S(1)} %add.406), channel_id=1, source_target_pairs={{0,6},{1,7},{2,4},{3,5},{4,2},{5,3},{6,0},{7,1},{8,14},{9,15},{10,... | collective-permute-start | bytes 55304 | tf_op jit(solution)/shard_map/ppermute | solution.py:248
  40.5 20.9 %collective-permute-start.2 = (bf16[18,512]{1,0:T(8,128)(2,1)S(1)}, bf16[18,512]{1,0:T(8,128)(2,1)S(1)}, u32[]{:S(2)}, u32[]{:S(2)}) collective-permute-start(bf16[18,512]{1,0:T(8,128)(2,1)S(1)} %add.406), channel_id=1, source_target_pairs={{0,4},{1,5},{2,6},{3,7},{4,0},{5,1},{6,2},{7,3},{8,12},{9,13},{10,... | collective-permute-start | bytes 55304 | tf_op jit(solution)/shard_map/ppermute | solution.py:248
  41.1 20.3 %collective-permute-start.1 = (bf16[18,512]{1,0:T(8,128)(2,1)S(1)}, bf16[18,512]{1,0:T(8,128)(2,1)S(1)}, u32[]{:S(2)}, u32[]{:S(2)}) collective-permute-start(bf16[18,512]{1,0:T(8,128)(2,1)S(1)} %add.406), channel_id=1, source_target_pairs={{0,2},{1,3},{2,0},{3,1},{4,6},{5,7},{6,4},{7,5},{8,10},{9,11},{10,... | collective-permute-start | bytes 55304 | tf_op jit(solution)/shard_map/ppermute | solution.py:248
  62.9 25.0 %collective-permute-start.5 = (bf16[128,2048]{1,0:T(8,128)(2,1)S(1)}, bf16[128,2048]{1,0:T(8,128)(2,1)S(1)}, u32[]{:S(2)}, u32[]{:S(2)}) collective-permute-start(bf16[128,2048]{1,0:T(8,128)(2,1)S(1)} %bitcast.192), channel_id=1, source_target_pairs={{0,4},{1,5},{2,6},{3,7},{4,0},{5,1},{6,2},{7,3},{8,12},{9,13},{10,... | collective-permute-start | bytes 1572872 | tf_op jit(solution)/shard_map/ppermute | solution.py:248
  63.5 24.3 %collective-permute-start.6 = (bf16[128,2048]{1,0:T(8,128)(2,1)S(1)}, bf16[128,2048]{1,0:T(8,128)(2,1)S(1)}, u32[]{:S(2)}, u32[]{:S(2)}) collective-permute-start(bf16[128,2048]{1,0:T(8,128)(2,1)S(1)} %bitcast.193), channel_id=1, source_target_pairs={{0,6},{1,7},{2,4},{3,5},{4,2},{5,3},{6,0},{7,1},{8,14},{9,15},{10,... | collective-permute-start | bytes 1572872 | tf_op jit(solution)/shard_map/ppermute | solution.py:248
  89.5 22.6 %collective-permute-start.7 = (bf16[512,2048]{1,0:T(8,128)(2,1)}, bf16[512,2048]{1,0:T(8,128)(2,1)}, u32[]{:S(2)}, u32[]{:S(2)}) collective-permute-start(bf16[512,2048]{1,0:T(8,128)(2,1)} %pad_maximum_fusion.3), channel_id=1, source_target_pairs={{0,1},{1,0},{2,3},{3,2},{4,5},{5,4},{6,7},{7,6},{8,9},{9,8},{10,11... | collective-permute-start | bytes 6291464 | tf_op jit(solution)/shard_map/ppermute | solution.py:248
  106.3 32.3 %all-to-all-start.2 = ((bf16[8,64,384]{2,1,0:T(8,128)(2,1)}), bf16[8,64,384]{2,1,0:T(8,128)(2,1)}, u32[]{:S(2)}, u32[]{:S(2)}) async-start(bf16[8,64,384]{2,1,0:T(8,128)(2,1)} %copy.149), calls=%async_computation.2 | async-start | bytes 786432 | tf_op jit(solution)/shard_map/all_to_all | solution.py:361
  110.4 173.1 %all-gather.8.cloned.1.call-start = ((), (), s32[]{:S(2)}) async-start(), calls=%async_computation.9 | async-start | bytes 1966080 | tf_op jit(solution)/shard_map/all_gather | solution.py:432
  118.1 20.5 %collective-permute-start.11 = (bf16[128,2048]{1,0:T(8,128)(2,1)}, bf16[128,2048]{1,0:T(8,128)(2,1)}, u32[]{:S(2)}, u32[]{:S(2)}) collective-permute-start(bf16[128,2048]{1,0:T(8,128)(2,1)} %bitcast.4), channel_id=1, source_target_pairs={{0,2},{1,3},{2,0},{3,1},{4,6},{5,7},{6,4},{7,5},{8,10},{9,11},{10,... | collective-permute-start | bytes 1572872 | tf_op jit(solution)/shard_map/ppermute | solution.py:248
  120.0 25.3 %collective-permute-start.12 = (bf16[128,2048]{1,0:T(8,128)(2,1)}, bf16[128,2048]{1,0:T(8,128)(2,1)}, u32[]{:S(2)}, u32[]{:S(2)}) collective-permute-start(bf16[128,2048]{1,0:T(8,128)(2,1)} %bitcast.4), channel_id=1, source_target_pairs={{0,4},{1,5},{2,6},{3,7},{4,0},{5,1},{6,2},{7,3},{8,12},{9,13},{10,... | collective-permute-start | bytes 1572872 | tf_op jit(solution)/shard_map/ppermute | solution.py:248
  121.5 23.8 %collective-permute-start.13 = (bf16[128,2048]{1,0:T(8,128)(2,1)}, bf16[128,2048]{1,0:T(8,128)(2,1)}, u32[]{:S(2)}, u32[]{:S(2)}) collective-permute-start(bf16[128,2048]{1,0:T(8,128)(2,1)} %bitcast.4), channel_id=1, source_target_pairs={{0,6},{1,7},{2,4},{3,5},{4,2},{5,3},{6,0},{7,1},{8,14},{9,15},{10,... | collective-permute-start | bytes 1572872 | tf_op jit(solution)/shard_map/ppermute | solution.py:248
  166.6 24.4 %collective-permute-start.15 = (bf16[128,2048]{1,0:T(8,128)(2,1)S(1)}, bf16[128,2048]{1,0:T(8,128)(2,1)S(1)}, u32[]{:S(2)}, u32[]{:S(2)}) collective-permute-start(bf16[128,2048]{1,0:T(8,128)(2,1)S(1)} %get-tuple-element.154), channel_id=1, source_target_pairs={{0,6},{1,7},{2,4},{3,5},{4,2},{5,3},{6,0},{7,1},{8,14},{9,15},{10,... | collective-permute-start | bytes 1572872 | tf_op jit(solution)/shard_map/ppermute | solution.py:248
  169.8 53.3 %collective-permute-start.22 = (bf16[512,2048]{1,0:T(8,128)(2,1)S(1)}, bf16[512,2048]{1,0:T(8,128)(2,1)S(1)}, u32[]{:S(2)}, u32[]{:S(2)}) collective-permute-start(bf16[512,2048]{1,0:T(8,128)(2,1)S(1)} %pad_maximum_fusion.4), channel_id=1, source_target_pairs={{0,1},{1,0},{2,3},{3,2},{4,5},{5,4},{6,7},{7,6},{8,9},{9,8},{10,11... | collective-permute-start | bytes 6291464 | tf_op jit(solution)/shard_map/ppermute | solution.py:248
  194.6 22.3 %collective-permute-start.19 = (bf16[128,2048]{1,0:T(8,128)(2,1)S(1)}, bf16[128,2048]{1,0:T(8,128)(2,1)S(1)}, u32[]{:S(2)}, u32[]{:S(2)}) collective-permute-start(bf16[128,2048]{1,0:T(8,128)(2,1)S(1)} %get-tuple-element.135), channel_id=1, source_target_pairs={{0,4},{1,5},{2,6},{3,7},{4,0},{5,1},{6,2},{7,3},{8,12},{9,13},{10,... | collective-permute-start | bytes 1572872 | tf_op jit(solution)/shard_map/ppermute | solution.py:248
  195.4 23.0 %collective-permute-start.20 = (bf16[128,2048]{1,0:T(8,128)(2,1)S(1)}, bf16[128,2048]{1,0:T(8,128)(2,1)S(1)}, u32[]{:S(2)}, u32[]{:S(2)}) collective-permute-start(bf16[128,2048]{1,0:T(8,128)(2,1)S(1)} %get-tuple-element.135), channel_id=1, source_target_pairs={{0,6},{1,7},{2,4},{3,5},{4,2},{5,3},{6,0},{7,1},{8,14},{9,15},{10,... | collective-permute-start | bytes 1572872 | tf_op jit(solution)/shard_map/ppermute | solution.py:248
  235.7 200.5 %reduce-scatter.5.cloned.1.call-start = ((), (), s32[]{:S(2)}) async-start(), calls=%async_computation.11 | async-start | bytes 9830400 | tf_op jit(solution)/shard_map/reduce_scatter | solution.py:364
  275.2 225.7 %reduce-scatter.3.cloned.1.call-start = ((), (), s32[]{:S(2)}) async-start(), calls=%async_computation.10 | async-start | bytes 5898240 | tf_op jit(solution)/shard_map/reduce_scatter | solution.py:364
  299.0 27.5 %collective-permute-start.27 = (bf16[512,2048]{1,0:T(8,128)(2,1)S(1)}, bf16[512,2048]{1,0:T(8,128)(2,1)S(1)}, u32[]{:S(2)}, u32[]{:S(2)}) collective-permute-start(bf16[512,2048]{1,0:T(8,128)(2,1)S(1)} %add_convert_fusion), channel_id=1, source_target_pairs={{0,1},{1,0},{2,3},{3,2},{4,5},{5,4},{6,7},{7,6},{8,9},{9,8},{10,11... | collective-permute-start | bytes 6291464 | tf_op jit(solution)/shard_map/ppermute | solution.py:248
  302.4 23.7 %collective-permute-start.24 = (bf16[128,2048]{1,0:T(8,128)(2,1)S(1)}, bf16[128,2048]{1,0:T(8,128)(2,1)S(1)}, u32[]{:S(2)}, u32[]{:S(2)}) collective-permute-start(bf16[128,2048]{1,0:T(8,128)(2,1)S(1)} %get-tuple-element.163), channel_id=1, source_target_pairs={{0,6},{1,7},{2,4},{3,5},{4,2},{5,3},{6,0},{7,1},{8,14},{9,15},{10,... | collective-permute-start | bytes 1572872 | tf_op jit(solution)/shard_map/ppermute | solution.py:248
  332.1 24.1 %collective-permute-start.29 = (bf16[128,2048]{1,0:T(8,128)(2,1)S(1)}, bf16[128,2048]{1,0:T(8,128)(2,1)S(1)}, u32[]{:S(2)}, u32[]{:S(2)}) collective-permute-start(bf16[128,2048]{1,0:T(8,128)(2,1)S(1)} %get-tuple-element.133), channel_id=1, source_target_pairs={{0,4},{1,5},{2,6},{3,7},{4,0},{5,1},{6,2},{7,3},{8,12},{9,13},{10,... | collective-permute-start | bytes 1572872 | tf_op jit(solution)/shard_map/ppermute | solution.py:248
  333.6 22.6 %collective-permute-start.30 = (bf16[128,2048]{1,0:T(8,128)(2,1)S(1)}, bf16[128,2048]{1,0:T(8,128)(2,1)S(1)}, u32[]{:S(2)}, u32[]{:S(2)}) collective-permute-start(bf16[128,2048]{1,0:T(8,128)(2,1)S(1)} %get-tuple-element.133), channel_id=1, source_target_pairs={{0,6},{1,7},{2,4},{3,5},{4,2},{5,3},{6,0},{7,1},{8,14},{9,15},{10,... | collective-permute-start | bytes 1572872 | tf_op jit(solution)/shard_map/ppermute | solution.py:248
  399.8 24.4 %collective-permute-start.36 = (bf16[128,2048]{1,0:T(8,128)(2,1)S(1)}, bf16[128,2048]{1,0:T(8,128)(2,1)S(1)}, u32[]{:S(2)}, u32[]{:S(2)}) collective-permute-start(bf16[128,2048]{1,0:T(8,128)(2,1)S(1)} %get-tuple-element.151), channel_id=1, source_target_pairs={{0,6},{1,7},{2,4},{3,5},{4,2},{5,3},{6,0},{7,1},{8,14},{9,15},{10,... | collective-permute-start | bytes 1572872 | tf_op jit(solution)/shard_map/ppermute | solution.py:248
  431.3 18.3 %collective-permute-start.34 = (bf16[128,2048]{1,0:T(8,128)(2,1)}, bf16[128,2048]{1,0:T(8,128)(2,1)S(1)}, u32[]{:S(2)}, u32[]{:S(2)}) collective-permute-start(bf16[128,2048]{1,0:T(8,128)(2,1)} %get-tuple-element.161), channel_id=1, source_target_pairs={{0,4},{1,5},{2,6},{3,7},{4,0},{5,1},{6,2},{7,3},{8,12},{9,13},{10,... | collective-permute-start | bytes 1572872 | tf_op jit(solution)/shard_map/ppermute | solution.py:248
  433.3 26.0 %collective-permute-start.32 = (bf16[128,2048]{1,0:T(8,128)(2,1)}, bf16[128,2048]{1,0:T(8,128)(2,1)}, u32[]{:S(2)}, u32[]{:S(2)}) collective-permute-start(bf16[128,2048]{1,0:T(8,128)(2,1)} %get-tuple-element.160), channel_id=1, source_target_pairs={{0,6},{1,7},{2,4},{3,5},{4,2},{5,3},{6,0},{7,1},{8,14},{9,15},{10,... | collective-permute-start | bytes 1572872 | tf_op jit(solution)/shard_map/ppermute | solution.py:248
  440.3 45.6 %all-to-all-start.3 = ((bf16[8,64,1920]{2,1,0:T(8,128)(2,1)}), bf16[8,64,1920]{2,1,0:T(8,128)(2,1)}, u32[]{:S(2)}, u32[]{:S(2)}) async-start(bf16[8,64,1920]{2,1,0:T(8,128)(2,1)} %bitcast.197), calls=%async_computation.5 | async-start | bytes 3932160 | tf_op jit(solution)/shard_map/all_to_all | solution.py:361
  446.2 35.8 %collective-permute-start.45 = (f32[290,128]{1,0:T(8,128)S(1)}, f32[290,128]{1,0:T(8,128)S(1)}, u32[]{:S(2)}, u32[]{:S(2)}) collective-permute-start(f32[290,128]{1,0:T(8,128)S(1)} %fusion.89), channel_id=1, source_target_pairs={{0,6},{1,7},{2,4},{3,5},{4,2},{5,3},{6,0},{7,1},{8,14},{9,15},{10,... | collective-permute-start | bytes 445448 | tf_op jit(solution)/shard_map/ppermute | solution.py:248
  449.0 34.4 %collective-permute-start.44 = (f32[290,128]{1,0:T(8,128)S(1)}, f32[290,128]{1,0:T(8,128)S(1)}, u32[]{:S(2)}, u32[]{:S(2)}) collective-permute-start(f32[290,128]{1,0:T(8,128)S(1)} %fusion.89), channel_id=1, source_target_pairs={{0,4},{1,5},{2,6},{3,7},{4,0},{5,1},{6,2},{7,3},{8,12},{9,13},{10,... | collective-permute-start | bytes 445448 | tf_op jit(solution)/shard_map/ppermute | solution.py:248
  449.6 34.0 %collective-permute-start.43 = (f32[290,128]{1,0:T(8,128)S(1)}, f32[290,128]{1,0:T(8,128)S(1)}, u32[]{:S(2)}, u32[]{:S(2)}) collective-permute-start(f32[290,128]{1,0:T(8,128)S(1)} %fusion.89), channel_id=1, source_target_pairs={{0,2},{1,3},{2,0},{3,1},{4,6},{5,7},{6,4},{7,5},{8,10},{9,11},{10,... | collective-permute-start | bytes 445448 | tf_op jit(solution)/shard_map/ppermute | solution.py:248
  506.9 25.3 %all-to-all-start.4 = ((bf16[8,64,1152]{2,1,0:T(8,128)(2,1)}), bf16[8,64,1152]{2,1,0:T(8,128)(2,1)S(1)}, u32[]{:S(2)}, u32[]{:S(2)}) async-start(bf16[8,64,1152]{2,1,0:T(8,128)(2,1)} %bitcast.30), calls=%async_computation.6 | async-start | bytes 2359296 | tf_op jit(solution)/shard_map/all_to_all | solution.py:361
  (95 other events, 861.8 us)
Sparse Core Ops, SparseCore 0:
  30.4 63.2 all-gather.3
  95.8 139.7 all-gather.5
  237.2 35.3 all-gather.7
  275.4 134.6 reduce-scatter.4
  412.7 88.1 reduce-scatter.2

commit v6 on v5

--- a/solution.py
+++ b/solution.py
@@ -220,6 +220,31 @@
     return call_kernel(kernel, shapes, scratch, *args)
 
 
+def pack_kernel(spans, first, used, weights, out, held, arrived):
+    copy = pltpu.make_async_copy(weights.at[:, pl.ds(first, used)], held, arrived)
+    copy.start()
+    copy.wait()
+    for c, sources in enumerate(spans):
+        start = 0
+        for source, width in sources:
+            part = held[:, source : source + width]
+            out[c, :, start : start + width] = part.astype(bf16)
+            start += width
+
+
+def pack(weights, first, used, spans):
+    rows = weights.shape[0]
+    shape = (len(spans), rows, sum(width for _, width in spans[0]))
+    return pl.pallas_call(
+        functools.partial(pack_kernel, spans, first, used),
+        out_shape=jax.ShapeDtypeStruct(shape, bf16),
+        in_specs=[pl.BlockSpec(memory_space=pl.ANY)],
+        out_specs=pl.BlockSpec(memory_space=pltpu.VMEM),
+        scratch_shapes=[pltpu.VMEM((rows, used), f32), pltpu.SemaphoreType.DMA],
+        compiler_params=pltpu.CompilerParams(vmem_limit_bytes=56 * 2**20),
+    )(weights)
+
+
 def squares_kernel(part, out):
     total = jnp.zeros((1, 128), f32)
     for start in range(0, part.shape[1], 128):
@@ -352,11 +377,6 @@
     win = wq + 2 * wkv
     wff = FF // groups
 
-    def blocks(start, width, repeat=1):
-        part = big_weight[:, start : start + width].astype(bf16)
-        part = part.reshape(wr, groups // repeat, -1).transpose(1, 0, 2)
-        return jnp.repeat(part, repeat, axis=0) if repeat > 1 else part
-
     def exchange(part):
         return lax.all_to_all(part, "cp", 0, 0, tiled=True)
 
@@ -369,25 +389,27 @@
     def to_columns(part):
         return exchange(part).reshape(groups * wr, -1)
 
-    attn_blocks = jnp.concatenate(
-        [
-            blocks(0, width_attn),
-            blocks(width_attn, width_kv, copies),
-            blocks(width_attn + width_kv, width_kv, copies),
-            blocks(width_qkv, width_attn),
-        ],
-        axis=2,
-    )
-    attn_rows = to_columns(attn_blocks)
+    spans = [
+        (
+            (c * wq, wq),
+            (width_attn + c // copies * wkv, wkv),
+            (width_attn + width_kv + c // copies * wkv, wkv),
+            (width_qkv + c * wq, wq),
+        )
+        for c in range(groups)
+    ]
+    attn_blocks = pack(big_weight, 0, start_mlp, spans)
     part_ff = (5 * wff // 6, wff // 6)
 
-    def unit_blocks(i):
-        start = sum(part_ff[:i]) * groups
-        return jnp.concatenate(
-            [blocks(start_mlp + k * FF + start, part_ff[i] * groups) for k in range(3)], axis=2
-        )
-
-    first_blocks, attn_rows = tie(unit_blocks(0), attn_rows)
+    def unit_blocks(weights, i):
+        start, width = sum(part_ff[:i]) * groups, part_ff[i]
+        spans = [
+            tuple((k * FF + start + c * width, width) for k in range(3)) for c in range(groups)
+        ]
+        return pack(weights, start_mlp, 3 * FF, spans)
+
+    attn_blocks, later_weight = tie(attn_blocks, big_weight)
+    first_blocks, attn_rows = tie(unit_blocks(later_weight, 0), to_columns(attn_blocks))
     attn_w = lax.all_gather(attn_rows, "dp", axis=0, tiled=True)
     mlp_rows = [to_columns(first_blocks)]
 
@@ -414,7 +436,7 @@
     info = (cosine, sine, spots, place[None, :], qk_gain)
 
     second_blocks, own_branch, *tokens_all = tie(
-        unit_blocks(1), cotangent[0], *gather_chips(own_tokens)
+        unit_blocks(later_weight, 1), cotangent[0], *gather_chips(own_tokens)
     )
     mlp_rows.append(to_columns(second_blocks))
     tokens_all = gather_cores(tokens_all)

time: 562 us -> 557 us (level)
  matrix products: 98.1 us -> 87.2 us
  starting transfers between devices: 76.9 us -> 86.9 us
  Pallas kernels: 20 us -> 29.4 us
    dot_general x12, matrix products: 40.2 us -> 29.5 us  [dot_nt(): return lax.dot_general(a, b, contract_cols, preferred_element_type=f32)]
    ppermute x53, starting transfers between devices: 54.9 us -> 64.8 us  [shift(): lax.ppermute(value, axis, [(i, i ^ offset) for i in range(lax.axis_size(a...]
    pallas_call x0 -> x3, Pallas kernels: none -> 9.37 us  [pack(): pl.pallas_call(functools.partial(pack_kernel, spans, first, used), out_sh...]
    ppermute x53, waiting for transfers between devices: 206 us -> 200 us  [shift(): lax.ppermute(value, axis, [(i, i ^ offset) for i in range(lax.axis_size(a...]
    unnamed x166 -> x147, local copies, waits for them, and re-layouts: 22.3 us -> 22.2 us
  transfers between devices with their start and end apart: 63 -> 63, of which waited for: 35 -> 35; matrix products, arithmetic and copies ran while one was open for 30% -> 28% of each run, Pallas kernels for 3% -> 5%
where the time goes in v6:
time: 557 us; the launch traced here: 552 us
  waiting for transfers between devices  236 us (42%)
  matrix products  87.2 us (16%)
  starting transfers between devices  86.9 us (16%)
  other arithmetic  50.2 us (9%)
  local copies, waits for them, and re-layouts  43.5 us (8%)
  Pallas kernels  29.4 us (5%)
  between operations  18.5 us (3%)
    ppermute x53, waiting for transfers between devices, shift(): lax.ppermute(value, axis, [(i, i ^ offset) for i in range(lax.axis_size(a...  200 us
    ppermute x53, starting transfers between devices, shift(): lax.ppermute(value, axis, [(i, i ^ offset) for i in range(lax.axis_size(a...  64.8 us
    dot_general x7, matrix products, dot(): return jnp.dot(a, b, preferred_element_type=f32)  30.4 us
    dot_general x12, matrix products, dot_nt(): return lax.dot_general(a, b, contract_cols, preferred_element_type=f32)  29.5 us
    dot_general x7, matrix products, dot_tn(): return lax.dot_general(a, b, contract_rows, preferred_element_type=f32)  27.3 us
    unnamed x147, local copies, waits for them, and re-layouts  22.2 us
    all_to_all x5, starting transfers between devices, exchange(): return lax.all_to_all(part, 'cp', 0, 0, tiled=True)  21.1 us
    pallas_call x2, Pallas kernels, call_kernel(): pl.pallas_call(kernel, out_shape=[jax.ShapeDtypeStruct(shape, dtype) for...  18.5 us
  transfers between devices with their start and end apart: 63, of which 35 were waited for; matrix products, arithmetic and copies ran while one was open for 28% of the time, Pallas kernels for 5%

profile of v6, /device:TPU:0, one launch (start us, length us, event | category | flops | bytes accessed | tf_op | source)
XLA Modules:
  0.0 551.9 jit_solution(13846447667811509278)
XLA Ops:
  9.6 5.2 all-to-all-start
  18.7 8.7 %all-to-all-done = bf16[8,64,768]{2,1,0:T(8,128)(2,1)S(1)} async-done(((bf16[8,64,768]{2,1,0:T(8,128)(2,1)}), bf16[8,64,768]{2,1,0:T(8,128)(2,1)S(1)}, u32[]{:S(2)}, u32[]{:S(2)}) %all-to-all-start) | async-done | bytes 786464 | tf_op jit(solution)/shard_map/all_to_all | solution.py:381
  42.9 15.4 %collective-permute-done.3 = bf16[18,512]{1,0:T(8,128)(2,1)S(1)} collective-permute-done((bf16[18,512]{1,0:T(8,128)(2,1)S(1)}, bf16[18,512]{1,0:T(8,128)(2,1)S(1)}, u32[]{:S(2)}, u32[]{:S(2)}) %collective-permute-start.3) | collective-permute-done | bytes 18464 | tf_op jit(solution)/shard_map/ppermute | solution.py:273
  64.5 9.4 %collective-permute-done.4 = bf16[128,2048]{1,0:T(8,128)(2,1)S(1)} collective-permute-done((bf16[128,2048]{1,0:T(8,128)(2,1)S(1)}, bf16[128,2048]{1,0:T(8,128)(2,1)S(1)}, u32[]{:S(2)}, u32[]{:S(2)}) %collective-permute-start.4) | collective-permute-done | bytes 524320 | tf_op jit(solution)/shard_map/ppermute | solution.py:273
  73.9 10.9 %collective-permute-done.5 = bf16[128,2048]{1,0:T(8,128)(2,1)S(1)} collective-permute-done((bf16[128,2048]{1,0:T(8,128)(2,1)S(1)}, bf16[128,2048]{1,0:T(8,128)(2,1)S(1)}, u32[]{:S(2)}, u32[]{:S(2)}) %collective-permute-start.5) | collective-permute-done | bytes 524320 | tf_op jit(solution)/shard_map/ppermute | solution.py:273
  114.9 5.2 fusion.92.proj
  120.1 7.5 %shard_map.255 = (bf16[1024,256]{1,0:T(8,128)(2,1)S(1)}, f32[1024,256]{1,0:T(8,128)S(1)}, f32[1024,2]{1,0:T(8,128)S(1)}, bf16[1024,256]{1,0:T(8,128)(2,1)S(1)}, ...) custom-call(f32[1024,512]{1,0:T(8,128)S(1)} %fusion.92.proj, f32[1024,2]{1,0:T(8,128)S(1)} %copy-done.2, ...), custom_call_target="tpu_custom_call" | custom-call | flops 10000000 | bytes 100000 | tf_op jit(solution)/shard_map/pallas_call | solution.py:195
  131.8 6.7 %collective-permute-done.12 = bf16[128,2048]{1,0:T(8,128)(2,1)} collective-permute-done((bf16[128,2048]{1,0:T(8,128)(2,1)}, bf16[128,2048]{1,0:T(8,128)(2,1)}, u32[]{:S(2)}, u32[]{:S(2)}) %collective-permute-start.12) | collective-permute-done | bytes 524320 | tf_op jit(solution)/shard_map/ppermute | solution.py:273
  140.6 10.7 %collective-permute-start.14 = (bf16[512,2048]{1,0:T(8,128)(2,1)S(1)}, bf16[512,2048]{1,0:T(8,128)(2,1)S(1)}, u32[]{:S(2)}, u32[]{:S(2)}) collective-permute-start(bf16[512,2048]{1,0:T(8,128)(2,1)S(1)} %convolution_convert_fusion.3), channel_id=1, source_target_pairs={{0,1},{1,0},{2,3},{3,2},{4,5},{5,4},{6,7},{7,6},{8,9},{9,8},{10,11... | collective-permute-start | bytes 6291464 | tf_op jit(solution)/shard_map/ppermute | solution.py:273
  163.0 8.6 %collective-permute-done.17 = bf16[128,2048]{1,0:T(8,128)(2,1)S(1)} collective-permute-done((bf16[128,2048]{1,0:T(8,128)(2,1)S(1)}, bf16[128,2048]{1,0:T(8,128)(2,1)S(1)}, u32[]{:S(2)}, u32[]{:S(2)}) %collective-permute-start.17) | collective-permute-done | bytes 524320 | tf_op jit(solution)/shard_map/ppermute | solution.py:273
  173.9 10.1 %collective-permute-done.15 = bf16[128,2048]{1,0:T(8,128)(2,1)S(1)} collective-permute-done((bf16[128,2048]{1,0:T(8,128)(2,1)S(1)}, bf16[128,2048]{1,0:T(8,128)(2,1)S(1)}, u32[]{:S(2)}, u32[]{:S(2)}) %collective-permute-start.15) | collective-permute-done | bytes 524320 | tf_op jit(solution)/shard_map/ppermute | solution.py:273
  190.5 11.4 %collective-permute-done.18 = bf16[128,2048]{1,0:T(8,128)(2,1)S(1)} collective-permute-done((bf16[128,2048]{1,0:T(8,128)(2,1)S(1)}, bf16[128,2048]{1,0:T(8,128)(2,1)S(1)}, u32[]{:S(2)}, u32[]{:S(2)}) %collective-permute-start.18) | collective-permute-done | bytes 524320 | tf_op jit(solution)/shard_map/ppermute | solution.py:273
  202.7 9.3 %collective-permute-done.20 = bf16[128,2048]{1,0:T(8,128)(2,1)S(1)} collective-permute-done((bf16[128,2048]{1,0:T(8,128)(2,1)S(1)}, bf16[128,2048]{1,0:T(8,128)(2,1)S(1)}, u32[]{:S(2)}, u32[]{:S(2)}) %collective-permute-start.20) | collective-permute-done | bytes 524320 | tf_op jit(solution)/shard_map/ppermute | solution.py:273
  221.6 11.7 %all-gather.6.cloned.1.call-done = bf16[2048,1920]{1,0:T(8,128)(2,1)} async-done(((bf16[512,1920]{1,0:T(8,128)(2,1)}), bf16[2048,1920]{1,0:T(8,128)(2,1)}) %all-gather.6.cloned.1.call-update) | async-done | bytes 7864336 | tf_op jit(solution)/shard_map/all_gather | solution.py:421
  233.3 9.0 %fusion.8 = f32[1024,1280]{0,1:T(8,128)S(1)} fusion(bf16[1024,2048]{1,0:T(8,128)(2,1)} %constant_dynamic-update-slice_fusion.10, bf16[2048,1920]{1,0:T(8,128)(2,1)} %all-gather.6.cloned.1.call-done), kind=kOutput, calls=%fused_computation.22 | convolution fusion | flops 5368709120 | bytes 14680064 | tf_op jit(solution)/shard_map/dot_general | solution.py:33
  242.4 5.8 %multiply_convert_fusion.2 = (bf16[1024,640]{0,1:T(8,128)(2,1)S(1)}, bf16[1024,640]{0,1:T(8,128)(2,1)S(1)}, bf16[1024,640]{0,1:T(8,128)(2,1)S(1)}) fusion(f32[1024,1280]{0,1:T(8,128)S(1)} %fusion.8, bf16[1024,2048]{1,0:T(8,128)(2,1)S(1)} %copy-done.47, bf16[2048,1920]{1,0:T(8,128)(2,1)} %all-gather.6.cloned.1.call-done), kind=kOutput, calls=%fused_computation.36 | convolution fusion | flops 2694840320 | bytes 15990784 | tf_op jit(solution)/shard_map/dot_general | solution.py:33
  254.2 10.5 %convolution_convert_fusion = bf16[2048,1280]{0,1:T(8,128)(2,1)} fusion(bf16[1024,2048]{1,0:T(8,128)(2,1)} %constant_dynamic-update-slice_fusion.10, bf16[1024,640]{0,1:T(8,128)(2,1)S(1)} %get-tuple-element.141, bf16[1024,640]{0,1:T(8,128)(2,1)S(1)} %get-tuple-element.140), kind=kOutput, calls=%fused_computation.8 | convolution fusion | flops 5376573440 | bytes 12058624 | tf_op jit(solution)/shard_map/dot_general | solution.py:41
  264.8 7.9 %pad_maximum_fusion = bf16[2048,1920]{0,1:T(8,128)(2,1)} fusion(bf16[2048,640]{0,1:T(8,128)(2,1)} %convolution_convert_fusion.1, bf16[2048,1280]{0,1:T(8,128)(2,1)} %convolution_convert_fusion), kind=kLoop, calls=%fused_computation.7 | loop fusion | flops 15728640 | bytes 15728640 | tf_op jit(solution)/shard_map/dynamic_update_slice | solution.py:476
  273.2 7.8 %fusion.4 = f32[512,2048]{1,0:T(8,128)} fusion(bf16[2048,1920]{1,0:T(8,128)(2,1)} %all-gather.6.cloned.1.call-done, bf16[1024,1280]{0,1:T(8,128)(2,1)} %pad_maximum_fusion.1), kind=kOutput, calls=%fused_computation.18 | convolution fusion | flops 2684354560 | bytes 10747904 | tf_op jit(solution)/shard_map/dot_general | solution.py:37
  313.2 10.4 %collective-permute-done.24 = bf16[128,2048]{1,0:T(8,128)(2,1)S(1)} collective-permute-done((bf16[128,2048]{1,0:T(8,128)(2,1)S(1)}, bf16[128,2048]{1,0:T(8,128)(2,1)S(1)}, u32[]{:S(2)}, u32[]{:S(2)}) %collective-permute-start.24) | collective-permute-done | bytes 524320 | tf_op jit(solution)/shard_map/ppermute | solution.py:273
  331.6 11.4 %collective-permute-done.28 = bf16[128,2048]{1,0:T(8,128)(2,1)S(1)} collective-permute-done((bf16[128,2048]{1,0:T(8,128)(2,1)S(1)}, bf16[128,2048]{1,0:T(8,128)(2,1)S(1)}, u32[]{:S(2)}, u32[]{:S(2)}) %collective-permute-start.28) | collective-permute-done | bytes 524320 | tf_op jit(solution)/shard_map/ppermute | solution.py:273
  343.0 10.7 %collective-permute-done.29 = bf16[128,2048]{1,0:T(8,128)(2,1)S(1)} collective-permute-done((bf16[128,2048]{1,0:T(8,128)(2,1)S(1)}, bf16[128,2048]{1,0:T(8,128)(2,1)S(1)}, u32[]{:S(2)}, u32[]{:S(2)}) %collective-permute-start.29) | collective-permute-done | bytes 524320 | tf_op jit(solution)/shard_map/ppermute | solution.py:273
  361.2 11.0 %shard_map.256 = (bf16[1024,512]{1,0:T(8,128)(2,1)S(1)}, f32[1024,2]{1,0:T(8,128)S(1)}, f32[2,128]{1,0:T(2,128)S(1)}) custom-call(f32[1024,512]{1,0:T(8,128)S(1)} %fusion.92.proj, f32[1024,2]{1,0:T(8,128)S(1)} %copy-done.3, f32[1024,128]{1,0:T(8,128)S(1)} %get-tuple-element.180.cosine, f32[1024,128]{1,0:T(8,128)S(1)} %get-tuple-element.181.sine, ...), custom_call_target="tpu_custom_call" | custom-call | flops 10000000 | bytes 100000 | tf_op jit(solution)/shard_map/pallas_call | solution.py:195
  385.7 4.4 collective-permute-done.35
  399.1 9.3 %collective-permute-done.38 = bf16[128,2048]{1,0:T(8,128)(2,1)S(1)} collective-permute-done((bf16[128,2048]{1,0:T(8,128)(2,1)S(1)}, bf16[128,2048]{1,0:T(8,128)(2,1)S(1)}, u32[]{:S(2)}, u32[]{:S(2)}) %collective-permute-start.38) | collective-permute-done | bytes 524320 | tf_op jit(solution)/shard_map/ppermute | solution.py:273
  410.7 10.1 %collective-permute-done.36 = bf16[128,2048]{1,0:T(8,128)(2,1)S(1)} collective-permute-done((bf16[128,2048]{1,0:T(8,128)(2,1)S(1)}, bf16[128,2048]{1,0:T(8,128)(2,1)S(1)}, u32[]{:S(2)}, u32[]{:S(2)}) %collective-permute-start.36) | collective-permute-done | bytes 524320 | tf_op jit(solution)/shard_map/ppermute | solution.py:273
  437.2 4.3 all-to-all-start.3
  446.7 9.2 %collective-permute-done.32 = bf16[128,2048]{1,0:T(8,128)(2,1)} collective-permute-done((bf16[128,2048]{1,0:T(8,128)(2,1)}, bf16[128,2048]{1,0:T(8,128)(2,1)}, u32[]{:S(2)}, u32[]{:S(2)}) %collective-permute-start.32) | collective-permute-done | bytes 524320 | tf_op jit(solution)/shard_map/ppermute | solution.py:273
  460.1 18.5 %collective-permute-done.45 = f32[290,128]{1,0:T(8,128)S(1)} collective-permute-done((f32[290,128]{1,0:T(8,128)S(1)}, f32[290,128]{1,0:T(8,128)S(1)}, u32[]{:S(2)}, u32[]{:S(2)}) %collective-permute-start.45) | collective-permute-done | bytes 148512 | tf_op jit(solution)/shard_map/ppermute | solution.py:273
  482.5 15.9 %reduce-scatter.3.cloned.1.call-done.part = bf16[512,1152]{1,0:T(8,128)(2,1)} async-done(((bf16[2048,1152]{1,0:T(8,128)(2,1)}), bf16[512,1152]{1,0:T(8,128)(2,1)}) %reduce-scatter.3.cloned.1.call-update) | async-done | bytes 1179664 | tf_op jit(solution)/shard_map/reduce_scatter | solution.py:384
  515.9 9.2 %collective-permute-done.52 = f32[1,128]{1,0:T(1,128)S(1)} collective-permute-done((f32[1,128]{1,0:T(1,128)S(1)}, f32[1,128]{1,0:T(1,128)S(1)}, u32[]{:S(2)}, u32[]{:S(2)}) %collective-permute-start.52) | collective-permute-done | bytes 544 | tf_op jit(solution)/shard_map/ppermute | solution.py:273
  530.3 13.7 %fusion.104 = (bf16[64,24576]{1,0:T(8,128)(2,1)}, f32[64,24576]{1,0:T(8,128)}, f32[64,24576]{1,0:T(8,128)}, f32[64,24576]{1,0:T(8,128)}) fusion(f32[64,24576]{1,0:T(8,128)} %weights.3, f32[]{:T(128)S(6)} %min.3, bf16[64,24576]{1,0:T(8,128)(2,1)S(1)} %bitcast_dynamic-update-slice_fusion, f32[64,24576]{1,0:T(8,128)} %param.18, f32[64,24576]{1,0:T(8,128)} %param.17), kind=kLoop, calls=%fused_computation.274 | loop fusion | flops 26738688 | bytes 44040196 | tf_op jit(solution)/shard_map/convert_element_type | solution.py:103
  (371 shorter events, 223.4 us)
Async XLA Ops:
  9.6 17.8 %all-to-all-start = ((bf16[8,64,768]{2,1,0:T(8,128)(2,1)}), bf16[8,64,768]{2,1,0:T(8,128)(2,1)S(1)}, u32[]{:S(2)}, u32[]{:S(2)}) async-start(bf16[8,64,768]{2,1,0:T(8,128)(2,1)} %shard_map.252), calls=%async_computation | async-start | bytes 1572864 | tf_op jit(solution)/shard_map/all_to_all | solution.py:381
  14.8 96.5 %all-gather.4.cloned.1.call-start = ((), (), s32[]{:S(2)}) async-start(), calls=%async_computation.7 | async-start | bytes 3932160 | tf_op jit(solution)/shard_map/all_gather | solution.py:413
  28.8 30.2 %all-to-all-start.1 = ((bf16[8,64,1920]{2,1,0:T(8,128)(2,1)}), bf16[8,64,1920]{2,1,0:T(8,128)(2,1)S(1)}, u32[]{:S(2)}, u32[]{:S(2)}) async-start(bf16[8,64,1920]{2,1,0:T(8,128)(2,1)} %shard_map.254), calls=%async_computation.1 | async-start | bytes 3932160 | tf_op jit(solution)/shard_map/all_to_all | solution.py:381
  32.4 200.9 %all-gather.6.cloned.1.call-start = ((), (), s32[]{:S(2)}) async-start(), calls=%async_computation.8 | async-start | bytes 9830400 | tf_op jit(solution)/shard_map/all_gather | solution.py:421
  33.1 25.3 %collective-permute-start.3 = (bf16[18,512]{1,0:T(8,128)(2,1)S(1)}, bf16[18,512]{1,0:T(8,128)(2,1)S(1)}, u32[]{:S(2)}, u32[]{:S(2)}) collective-permute-start(bf16[18,512]{1,0:T(8,128)(2,1)S(1)} %add.406), channel_id=1, source_target_pairs={{0,6},{1,7},{2,4},{3,5},{4,2},{5,3},{6,0},{7,1},{8,14},{9,15},{10,... | collective-permute-start | bytes 55304 | tf_op jit(solution)/shard_map/ppermute | solution.py:273
  35.9 22.4 %collective-permute-start.2 = (bf16[18,512]{1,0:T(8,128)(2,1)S(1)}, bf16[18,512]{1,0:T(8,128)(2,1)S(1)}, u32[]{:S(2)}, u32[]{:S(2)}) collective-permute-start(bf16[18,512]{1,0:T(8,128)(2,1)S(1)} %add.406), channel_id=1, source_target_pairs={{0,4},{1,5},{2,6},{3,7},{4,0},{5,1},{6,2},{7,3},{8,12},{9,13},{10,... | collective-permute-start | bytes 55304 | tf_op jit(solution)/shard_map/ppermute | solution.py:273
  36.5 21.9 %collective-permute-start.1 = (bf16[18,512]{1,0:T(8,128)(2,1)S(1)}, bf16[18,512]{1,0:T(8,128)(2,1)S(1)}, u32[]{:S(2)}, u32[]{:S(2)}) collective-permute-start(bf16[18,512]{1,0:T(8,128)(2,1)S(1)} %add.406), channel_id=1, source_target_pairs={{0,2},{1,3},{2,0},{3,1},{4,6},{5,7},{6,4},{7,5},{8,10},{9,11},{10,... | collective-permute-start | bytes 55304 | tf_op jit(solution)/shard_map/ppermute | solution.py:273
  59.8 25.0 %collective-permute-start.5 = (bf16[128,2048]{1,0:T(8,128)(2,1)S(1)}, bf16[128,2048]{1,0:T(8,128)(2,1)S(1)}, u32[]{:S(2)}, u32[]{:S(2)}) collective-permute-start(bf16[128,2048]{1,0:T(8,128)(2,1)S(1)} %bitcast.149), channel_id=1, source_target_pairs={{0,4},{1,5},{2,6},{3,7},{4,0},{5,1},{6,2},{7,3},{8,12},{9,13},{10,... | collective-permute-start | bytes 1572872 | tf_op jit(solution)/shard_map/ppermute | solution.py:273
  60.5 24.3 %collective-permute-start.6 = (bf16[128,2048]{1,0:T(8,128)(2,1)S(1)}, bf16[128,2048]{1,0:T(8,128)(2,1)S(1)}, u32[]{:S(2)}, u32[]{:S(2)}) collective-permute-start(bf16[128,2048]{1,0:T(8,128)(2,1)S(1)} %bitcast.150), channel_id=1, source_target_pairs={{0,6},{1,7},{2,4},{3,5},{4,2},{5,3},{6,0},{7,1},{8,14},{9,15},{10,... | collective-permute-start | bytes 1572872 | tf_op jit(solution)/shard_map/ppermute | solution.py:273
  86.4 19.0 %collective-permute-start.7 = (bf16[512,2048]{1,0:T(8,128)(2,1)}, bf16[512,2048]{1,0:T(8,128)(2,1)}, u32[]{:S(2)}, u32[]{:S(2)}) collective-permute-start(bf16[512,2048]{1,0:T(8,128)(2,1)} %pad_maximum_fusion.3), channel_id=1, source_target_pairs={{0,1},{1,0},{2,3},{3,2},{4,5},{5,4},{6,7},{7,6},{8,9},{9,8},{10,11... | collective-permute-start | bytes 6291464 | tf_op jit(solution)/shard_map/ppermute | solution.py:273
  98.5 33.3 %all-to-all-start.2 = ((bf16[8,64,384]{2,1,0:T(8,128)(2,1)}), bf16[8,64,384]{2,1,0:T(8,128)(2,1)}, u32[]{:S(2)}, u32[]{:S(2)}) async-start(bf16[8,64,384]{2,1,0:T(8,128)(2,1)} %shard_map.253), calls=%async_computation.2 | async-start | bytes 786432 | tf_op jit(solution)/shard_map/all_to_all | solution.py:381
  102.6 178.4 %all-gather.8.cloned.1.call-start = ((), (), s32[]{:S(2)}) async-start(), calls=%async_computation.9 | async-start | bytes 1966080 | tf_op jit(solution)/shard_map/all_gather | solution.py:454
  111.3 20.5 %collective-permute-start.11 = (bf16[128,2048]{1,0:T(8,128)(2,1)}, bf16[128,2048]{1,0:T(8,128)(2,1)}, u32[]{:S(2)}, u32[]{:S(2)}) collective-permute-start(bf16[128,2048]{1,0:T(8,128)(2,1)} %bitcast.1), channel_id=1, source_target_pairs={{0,2},{1,3},{2,0},{3,1},{4,6},{5,7},{6,4},{7,5},{8,10},{9,11},{10,... | collective-permute-start | bytes 1572872 | tf_op jit(solution)/shard_map/ppermute | solution.py:273
  113.2 25.2 %collective-permute-start.12 = (bf16[128,2048]{1,0:T(8,128)(2,1)}, bf16[128,2048]{1,0:T(8,128)(2,1)}, u32[]{:S(2)}, u32[]{:S(2)}) collective-permute-start(bf16[128,2048]{1,0:T(8,128)(2,1)} %bitcast.1), channel_id=1, source_target_pairs={{0,4},{1,5},{2,6},{3,7},{4,0},{5,1},{6,2},{7,3},{8,12},{9,13},{10,... | collective-permute-start | bytes 1572872 | tf_op jit(solution)/shard_map/ppermute | solution.py:273
  114.7 23.8 %collective-permute-start.13 = (bf16[128,2048]{1,0:T(8,128)(2,1)}, bf16[128,2048]{1,0:T(8,128)(2,1)}, u32[]{:S(2)}, u32[]{:S(2)}) collective-permute-start(bf16[128,2048]{1,0:T(8,128)(2,1)} %bitcast.1), channel_id=1, source_target_pairs={{0,6},{1,7},{2,4},{3,5},{4,2},{5,3},{6,0},{7,1},{8,14},{9,15},{10,... | collective-permute-start | bytes 1572872 | tf_op jit(solution)/shard_map/ppermute | solution.py:273
  159.7 24.3 %collective-permute-start.15 = (bf16[128,2048]{1,0:T(8,128)(2,1)S(1)}, bf16[128,2048]{1,0:T(8,128)(2,1)S(1)}, u32[]{:S(2)}, u32[]{:S(2)}) collective-permute-start(bf16[128,2048]{1,0:T(8,128)(2,1)S(1)} %get-tuple-element.146), channel_id=1, source_target_pairs={{0,6},{1,7},{2,4},{3,5},{4,2},{5,3},{6,0},{7,1},{8,14},{9,15},{10,... | collective-permute-start | bytes 1572872 | tf_op jit(solution)/shard_map/ppermute | solution.py:273
  162.9 53.8 %collective-permute-start.22 = (bf16[512,2048]{1,0:T(8,128)(2,1)S(1)}, bf16[512,2048]{1,0:T(8,128)(2,1)S(1)}, u32[]{:S(2)}, u32[]{:S(2)}) collective-permute-start(bf16[512,2048]{1,0:T(8,128)(2,1)S(1)} %pad_maximum_fusion.4), channel_id=1, source_target_pairs={{0,1},{1,0},{2,3},{3,2},{4,5},{5,4},{6,7},{7,6},{8,9},{9,8},{10,11... | collective-permute-start | bytes 6291464 | tf_op jit(solution)/shard_map/ppermute | solution.py:273
  189.0 23.1 %collective-permute-start.20 = (bf16[128,2048]{1,0:T(8,128)(2,1)S(1)}, bf16[128,2048]{1,0:T(8,128)(2,1)S(1)}, u32[]{:S(2)}, u32[]{:S(2)}) collective-permute-start(bf16[128,2048]{1,0:T(8,128)(2,1)S(1)} %get-tuple-element.137), channel_id=1, source_target_pairs={{0,6},{1,7},{2,4},{3,5},{4,2},{5,3},{6,0},{7,1},{8,14},{9,15},{10,... | collective-permute-start | bytes 1572872 | tf_op jit(solution)/shard_map/ppermute | solution.py:273
  233.3 199.8 %reduce-scatter.5.cloned.1.call-start = ((), (), s32[]{:S(2)}) async-start(), calls=%async_computation.11 | async-start | bytes 9830400 | tf_op jit(solution)/shard_map/reduce_scatter | solution.py:384
  272.8 225.7 %reduce-scatter.3.cloned.1.call-start = ((), (), s32[]{:S(2)}) async-start(), calls=%async_computation.10 | async-start | bytes 5898240 | tf_op jit(solution)/shard_map/reduce_scatter | solution.py:384
  296.5 27.5 %collective-permute-start.27 = (bf16[512,2048]{1,0:T(8,128)(2,1)S(1)}, bf16[512,2048]{1,0:T(8,128)(2,1)S(1)}, u32[]{:S(2)}, u32[]{:S(2)}) collective-permute-start(bf16[512,2048]{1,0:T(8,128)(2,1)S(1)} %add_convert_fusion), channel_id=1, source_target_pairs={{0,1},{1,0},{2,3},{3,2},{4,5},{5,4},{6,7},{7,6},{8,9},{9,8},{10,11... | collective-permute-start | bytes 6291464 | tf_op jit(solution)/shard_map/ppermute | solution.py:273
  299.9 23.7 %collective-permute-start.24 = (bf16[128,2048]{1,0:T(8,128)(2,1)S(1)}, bf16[128,2048]{1,0:T(8,128)(2,1)S(1)}, u32[]{:S(2)}, u32[]{:S(2)}) collective-permute-start(bf16[128,2048]{1,0:T(8,128)(2,1)S(1)} %get-tuple-element.155), channel_id=1, source_target_pairs={{0,6},{1,7},{2,4},{3,5},{4,2},{5,3},{6,0},{7,1},{8,14},{9,15},{10,... | collective-permute-start | bytes 1572872 | tf_op jit(solution)/shard_map/ppermute | solution.py:273
  329.6 24.1 %collective-permute-start.29 = (bf16[128,2048]{1,0:T(8,128)(2,1)S(1)}, bf16[128,2048]{1,0:T(8,128)(2,1)S(1)}, u32[]{:S(2)}, u32[]{:S(2)}) collective-permute-start(bf16[128,2048]{1,0:T(8,128)(2,1)S(1)} %get-tuple-element.135), channel_id=1, source_target_pairs={{0,4},{1,5},{2,6},{3,7},{4,0},{5,1},{6,2},{7,3},{8,12},{9,13},{10,... | collective-permute-start | bytes 1572872 | tf_op jit(solution)/shard_map/ppermute | solution.py:273
  331.1 22.6 %collective-permute-start.30 = (bf16[128,2048]{1,0:T(8,128)(2,1)S(1)}, bf16[128,2048]{1,0:T(8,128)(2,1)S(1)}, u32[]{:S(2)}, u32[]{:S(2)}) collective-permute-start(bf16[128,2048]{1,0:T(8,128)(2,1)S(1)} %get-tuple-element.135), channel_id=1, source_target_pairs={{0,6},{1,7},{2,4},{3,5},{4,2},{5,3},{6,0},{7,1},{8,14},{9,15},{10,... | collective-permute-start | bytes 1572872 | tf_op jit(solution)/shard_map/ppermute | solution.py:273
  396.5 24.4 %collective-permute-start.36 = (bf16[128,2048]{1,0:T(8,128)(2,1)S(1)}, bf16[128,2048]{1,0:T(8,128)(2,1)S(1)}, u32[]{:S(2)}, u32[]{:S(2)}) collective-permute-start(bf16[128,2048]{1,0:T(8,128)(2,1)S(1)} %get-tuple-element.143), channel_id=1, source_target_pairs={{0,6},{1,7},{2,4},{3,5},{4,2},{5,3},{6,0},{7,1},{8,14},{9,15},{10,... | collective-permute-start | bytes 1572872 | tf_op jit(solution)/shard_map/ppermute | solution.py:273
  427.9 18.6 %collective-permute-start.34 = (bf16[128,2048]{1,0:T(8,128)(2,1)}, bf16[128,2048]{1,0:T(8,128)(2,1)S(1)}, u32[]{:S(2)}, u32[]{:S(2)}) collective-permute-start(bf16[128,2048]{1,0:T(8,128)(2,1)} %get-tuple-element.153), channel_id=1, source_target_pairs={{0,4},{1,5},{2,6},{3,7},{4,0},{5,1},{6,2},{7,3},{8,12},{9,13},{10,... | collective-permute-start | bytes 1572872 | tf_op jit(solution)/shard_map/ppermute | solution.py:273
  429.9 25.9 %collective-permute-start.32 = (bf16[128,2048]{1,0:T(8,128)(2,1)}, bf16[128,2048]{1,0:T(8,128)(2,1)}, u32[]{:S(2)}, u32[]{:S(2)}) collective-permute-start(bf16[128,2048]{1,0:T(8,128)(2,1)} %get-tuple-element.152), channel_id=1, source_target_pairs={{0,6},{1,7},{2,4},{3,5},{4,2},{5,3},{6,0},{7,1},{8,14},{9,15},{10,... | collective-permute-start | bytes 1572872 | tf_op jit(solution)/shard_map/ppermute | solution.py:273
  437.2 45.3 %all-to-all-start.3 = ((bf16[8,64,1920]{2,1,0:T(8,128)(2,1)}), bf16[8,64,1920]{2,1,0:T(8,128)(2,1)}, u32[]{:S(2)}, u32[]{:S(2)}) async-start(bf16[8,64,1920]{2,1,0:T(8,128)(2,1)} %bitcast.154), calls=%async_computation.5 | async-start | bytes 3932160 | tf_op jit(solution)/shard_map/all_to_all | solution.py:381
  443.2 35.4 %collective-permute-start.45 = (f32[290,128]{1,0:T(8,128)S(1)}, f32[290,128]{1,0:T(8,128)S(1)}, u32[]{:S(2)}, u32[]{:S(2)}) collective-permute-start(f32[290,128]{1,0:T(8,128)S(1)} %fusion.91), channel_id=1, source_target_pairs={{0,6},{1,7},{2,4},{3,5},{4,2},{5,3},{6,0},{7,1},{8,14},{9,15},{10,... | collective-permute-start | bytes 445448 | tf_op jit(solution)/shard_map/ppermute | solution.py:273
  446.0 34.1 %collective-permute-start.44 = (f32[290,128]{1,0:T(8,128)S(1)}, f32[290,128]{1,0:T(8,128)S(1)}, u32[]{:S(2)}, u32[]{:S(2)}) collective-permute-start(f32[290,128]{1,0:T(8,128)S(1)} %fusion.91), channel_id=1, source_target_pairs={{0,4},{1,5},{2,6},{3,7},{4,0},{5,1},{6,2},{7,3},{8,12},{9,13},{10,... | collective-permute-start | bytes 445448 | tf_op jit(solution)/shard_map/ppermute | solution.py:273
  446.5 33.7 %collective-permute-start.43 = (f32[290,128]{1,0:T(8,128)S(1)}, f32[290,128]{1,0:T(8,128)S(1)}, u32[]{:S(2)}, u32[]{:S(2)}) collective-permute-start(f32[290,128]{1,0:T(8,128)S(1)} %fusion.91), channel_id=1, source_target_pairs={{0,2},{1,3},{2,0},{3,1},{4,6},{5,7},{6,4},{7,5},{8,10},{9,11},{10,... | collective-permute-start | bytes 445448 | tf_op jit(solution)/shard_map/ppermute | solution.py:273
  504.4 25.3 %all-to-all-start.4 = ((bf16[8,64,1152]{2,1,0:T(8,128)(2,1)}), bf16[8,64,1152]{2,1,0:T(8,128)(2,1)S(1)}, u32[]{:S(2)}, u32[]{:S(2)}) async-start(bf16[8,64,1152]{2,1,0:T(8,128)(2,1)} %bitcast.22), calls=%async_computation.6 | async-start | bytes 2359296 | tf_op jit(solution)/shard_map/all_to_all | solution.py:381
  (91 other events, 844.7 us)
Sparse Core Ops, SparseCore 0:
  28.4 62.9 all-gather.3
  93.5 139.6 all-gather.5
  234.8 35.3 all-gather.7
  272.9 134.6 reduce-scatter.4
  410.2 88.1 reduce-scatter.2

commit v7 on v6

--- a/solution.py
+++ b/solution.py
@@ -97,9 +97,10 @@
     second_new = beta_two * second + (1.0 - beta_two) * grad * grad
     fix_one = 1.0 - beta_one**STEP
     fix_two = 1.0 - beta_two**STEP
-    weight_new = weight - rate * (
-        first_new / fix_one / (jnp.sqrt(second_new / fix_two) + adam_eps) + decay * weight
-    )
+    scaled = second_new * (1.0 / fix_two)
+    root = scaled * lax.rsqrt(scaled)
+    step = (rate / fix_one) * first_new / (root + adam_eps)
+    weight_new = weight * (1.0 - rate * decay) - step
     return (first_new, second_new, weight_new, weight_new.astype(bf16))
 
 
@@ -245,6 +246,28 @@
     )(weights)
 
 
+def small_adam_kernel(factor, *refs):
+    small, gains, outs = refs[:4], refs[4:8], refs[8:]
+    for group, targets in ((small, outs[:4]), (gains, outs[4:8])):
+        weight, first, second, grad = (ref[:, :] for ref in group)
+        for out, value in zip(targets, adam(weight, first, second, grad * factor[0, 0])):
+            out[:, :] = value
+    outs[8][:, :] = small[3][:, HEADS:] * factor[0, 0]
+
+
+def small_adam(factor, *arrays):
+    shapes = [(arrays[i].shape, dtype) for i in (0, 4) for dtype in (f32, f32, f32, bf16)]
+    shapes.append(((arrays[0].shape[0], 2), f32))
+    spec = pl.BlockSpec(memory_space=pltpu.VMEM)
+    return pl.pallas_call(
+        small_adam_kernel,
+        out_shape=[jax.ShapeDtypeStruct(shape, dtype) for shape, dtype in shapes],
+        in_specs=[pl.BlockSpec(memory_space=pltpu.SMEM)] + [spec] * len(arrays),
+        out_specs=[spec] * len(shapes),
+        compiler_params=pltpu.CompilerParams(vmem_limit_bytes=4 * 2**20),
+    )(factor.reshape(1, 1), *arrays)
+
+
 def squares_kernel(part, out):
     total = jnp.zeros((1, 128), f32)
     for start in range(0, part.shape[1], 128):
@@ -575,9 +598,11 @@
         axis=1,
     )
     big_out = adam(big_weight, big_first, big_second, big_grad * factor)
-    small_out = adam(small_weight, small_first, small_second, small_grad * factor)
-    qk_out = adam(qk_gain, qk_first, qk_second, qk_grad * factor)
-    gain_grads = small_grad[:, HEADS:] * factor
+    *little, gain_grads = small_adam(
+        factor, small_weight, small_first, small_second, small_grad,
+        qk_gain, qk_first, qk_second, qk_grad,
+    )
+    small_out, qk_out = little[:4], little[4:]
     return (
         result.astype(bf16)[None],
         grad_input.astype(bf16)[None],

time: 557 us -> 554 us (level)
  starting transfers between devices: 86.9 us -> 76.2 us
    ppermute x53, starting transfers between devices: 64.8 us -> 54.4 us  [shift(): lax.ppermute(value, axis, [(i, i ^ offset) for i in range(lax.axis_size(a...]
    all_gather x1, waiting for transfers between devices: 11.7 us -> 21.8 us  [local(): mlp_w = [lax.all_gather(mlp_rows[0], 'dp', axis=0, tiled=True)]]
    ppermute x53, waiting for transfers between devices: 200 us -> 194 us  [shift(): lax.ppermute(value, axis, [(i, i ^ offset) for i in range(lax.axis_size(a...]
    unnamed x147 -> x160, local copies, waits for them, and re-layouts: 22.2 us -> 26.6 us
    convert_element_type x3 -> x1, other arithmetic: 15.8 us -> 13.2 us  [adam(): return (first_new, second_new, weight_new, weight_new.astype(bf16))]
  transfers between devices with their start and end apart: 63 -> 63, of which waited for: 35 -> 35; matrix products, arithmetic and copies ran while one was open for 28% -> 29% of each run, Pallas kernels for 5% -> 5%
where the time goes in v7:
time: 554 us; the launch traced here: 548 us
  waiting for transfers between devices  241 us (44%)
  matrix products  87.1 us (16%)
  starting transfers between devices  76.2 us (14%)
  local copies, waits for them, and re-layouts  48.5 us (9%)
  other arithmetic  47.1 us (9%)
  Pallas kernels  30.2 us (5%)
  between operations  18.6 us (3%)
    ppermute x53, waiting for transfers between devices, shift(): lax.ppermute(value, axis, [(i, i ^ offset) for i in range(lax.axis_size(a...  194 us
    ppermute x53, starting transfers between devices, shift(): lax.ppermute(value, axis, [(i, i ^ offset) for i in range(lax.axis_size(a...  54.4 us
    dot_general x7, matrix products, dot(): return jnp.dot(a, b, preferred_element_type=f32)  30.4 us
    dot_general x12, matrix products, dot_nt(): return lax.dot_general(a, b, contract_cols, preferred_element_type=f32)  29.3 us
    dot_general x7, matrix products, dot_tn(): return lax.dot_general(a, b, contract_rows, preferred_element_type=f32)  27.4 us
    unnamed x160, local copies, waits for them, and re-layouts  26.6 us
    all_gather x1, waiting for transfers between devices, local(): mlp_w = [lax.all_gather(mlp_rows[0], 'dp', axis=0, tiled=True)]  21.8 us
    all_to_all x5, starting transfers between devices, exchange(): return lax.all_to_all(part, 'cp', 0, 0, tiled=True)  21.2 us
  transfers between devices with their start and end apart: 63, of which 35 were waited for; matrix products, arithmetic and copies ran while one was open for 29% of the time, Pallas kernels for 5%

profile of v7, /device:TPU:0, one launch (start us, length us, event | category | flops | bytes accessed | tf_op | source)
XLA Modules:
  0.0 548.5 jit_solution(10181425152929412346)
XLA Ops:
  9.6 5.2 all-to-all-start
  18.7 8.7 %all-to-all-done = bf16[8,64,768]{2,1,0:T(8,128)(2,1)S(1)} async-done(((bf16[8,64,768]{2,1,0:T(8,128)(2,1)}), bf16[8,64,768]{2,1,0:T(8,128)(2,1)S(1)}, u32[]{:S(2)}, u32[]{:S(2)}) %all-to-all-start) | async-done | bytes 786464 | tf_op jit(solution)/shard_map/all_to_all | solution.py:404
  42.9 15.4 %collective-permute-done.3 = bf16[18,512]{1,0:T(8,128)(2,1)S(1)} collective-permute-done((bf16[18,512]{1,0:T(8,128)(2,1)S(1)}, bf16[18,512]{1,0:T(8,128)(2,1)S(1)}, u32[]{:S(2)}, u32[]{:S(2)}) %collective-permute-start.3) | collective-permute-done | bytes 18464 | tf_op jit(solution)/shard_map/ppermute | solution.py:296
  64.5 9.4 %collective-permute-done.4 = bf16[128,2048]{1,0:T(8,128)(2,1)S(1)} collective-permute-done((bf16[128,2048]{1,0:T(8,128)(2,1)S(1)}, bf16[128,2048]{1,0:T(8,128)(2,1)S(1)}, u32[]{:S(2)}, u32[]{:S(2)}) %collective-permute-start.4) | collective-permute-done | bytes 524320 | tf_op jit(solution)/shard_map/ppermute | solution.py:296
  73.9 10.9 %collective-permute-done.5 = bf16[128,2048]{1,0:T(8,128)(2,1)S(1)} collective-permute-done((bf16[128,2048]{1,0:T(8,128)(2,1)S(1)}, bf16[128,2048]{1,0:T(8,128)(2,1)S(1)}, u32[]{:S(2)}, u32[]{:S(2)}) %collective-permute-start.5) | collective-permute-done | bytes 524320 | tf_op jit(solution)/shard_map/ppermute | solution.py:296
  114.8 5.2 fusion.93.proj
  120.1 7.5 %shard_map.255 = (bf16[1024,256]{1,0:T(8,128)(2,1)S(1)}, f32[1024,256]{1,0:T(8,128)S(1)}, f32[1024,2]{1,0:T(8,128)S(1)}, bf16[1024,256]{1,0:T(8,128)(2,1)S(1)}, ...) custom-call(f32[1024,512]{1,0:T(8,128)S(1)} %fusion.93.proj, f32[1024,2]{1,0:T(8,128)S(1)} %copy-done.2, ...), custom_call_target="tpu_custom_call" | custom-call | flops 10000000 | bytes 100000 | tf_op jit(solution)/shard_map/pallas_call | solution.py:196
  131.7 6.7 %collective-permute-done.12 = bf16[128,2048]{1,0:T(8,128)(2,1)} collective-permute-done((bf16[128,2048]{1,0:T(8,128)(2,1)}, bf16[128,2048]{1,0:T(8,128)(2,1)}, u32[]{:S(2)}, u32[]{:S(2)}) %collective-permute-start.12) | collective-permute-done | bytes 524320 | tf_op jit(solution)/shard_map/ppermute | solution.py:296
  152.9 8.6 %collective-permute-done.17 = bf16[128,2048]{1,0:T(8,128)(2,1)S(1)} collective-permute-done((bf16[128,2048]{1,0:T(8,128)(2,1)S(1)}, bf16[128,2048]{1,0:T(8,128)(2,1)S(1)}, u32[]{:S(2)}, u32[]{:S(2)}) %collective-permute-start.17) | collective-permute-done | bytes 524320 | tf_op jit(solution)/shard_map/ppermute | solution.py:296
  163.8 10.1 %collective-permute-done.15 = bf16[128,2048]{1,0:T(8,128)(2,1)S(1)} collective-permute-done((bf16[128,2048]{1,0:T(8,128)(2,1)S(1)}, bf16[128,2048]{1,0:T(8,128)(2,1)S(1)}, u32[]{:S(2)}, u32[]{:S(2)}) %collective-permute-start.15) | collective-permute-done | bytes 524320 | tf_op jit(solution)/shard_map/ppermute | solution.py:296
  180.4 11.4 %collective-permute-done.18 = bf16[128,2048]{1,0:T(8,128)(2,1)S(1)} collective-permute-done((bf16[128,2048]{1,0:T(8,128)(2,1)S(1)}, bf16[128,2048]{1,0:T(8,128)(2,1)S(1)}, u32[]{:S(2)}, u32[]{:S(2)}) %collective-permute-start.18) | collective-permute-done | bytes 524320 | tf_op jit(solution)/shard_map/ppermute | solution.py:296
  191.7 8.6 %collective-permute-done.19 = bf16[128,2048]{1,0:T(8,128)(2,1)S(1)} collective-permute-done((bf16[128,2048]{1,0:T(8,128)(2,1)S(1)}, bf16[128,2048]{1,0:T(8,128)(2,1)S(1)}, u32[]{:S(2)}, u32[]{:S(2)}) %collective-permute-start.19) | collective-permute-done | bytes 524320 | tf_op jit(solution)/shard_map/ppermute | solution.py:296
  211.5 21.8 %all-gather.6.cloned.1.call-done = bf16[2048,1920]{1,0:T(8,128)(2,1)} async-done(((bf16[512,1920]{1,0:T(8,128)(2,1)}), bf16[2048,1920]{1,0:T(8,128)(2,1)}) %all-gather.6.cloned.1.call-update) | async-done | bytes 7864336 | tf_op jit(solution)/shard_map/all_gather | solution.py:444
  233.3 9.0 %fusion.11 = f32[1024,1280]{0,1:T(8,128)S(1)} fusion(bf16[1024,2048]{1,0:T(8,128)(2,1)} %constant_dynamic-update-slice_fusion.10, bf16[2048,1920]{1,0:T(8,128)(2,1)} %all-gather.6.cloned.1.call-done), kind=kOutput, calls=%fused_computation.25 | convolution fusion | flops 5368709120 | bytes 14680064 | tf_op jit(solution)/shard_map/dot_general | solution.py:33
  242.4 5.8 %multiply_convert_fusion.2 = (bf16[1024,640]{0,1:T(8,128)(2,1)S(1)}, bf16[1024,640]{0,1:T(8,128)(2,1)S(1)}, bf16[1024,640]{0,1:T(8,128)(2,1)S(1)}) fusion(f32[1024,1280]{0,1:T(8,128)S(1)} %fusion.11, bf16[1024,2048]{1,0:T(8,128)(2,1)S(1)} %copy-done.51, bf16[2048,1920]{1,0:T(8,128)(2,1)} %all-gather.6.cloned.1.call-done), kind=kOutput, calls=%fused_computation.39 | convolution fusion | flops 2694840320 | bytes 15990784 | tf_op jit(solution)/shard_map/dot_general | solution.py:33
  250.1 4.3 convolution_convert_fusion.1
  254.3 10.5 %convolution_convert_fusion = bf16[2048,1280]{0,1:T(8,128)(2,1)} fusion(bf16[1024,2048]{1,0:T(8,128)(2,1)} %constant_dynamic-update-slice_fusion.10, bf16[1024,640]{0,1:T(8,128)(2,1)S(1)} %get-tuple-element.246, bf16[1024,640]{0,1:T(8,128)(2,1)S(1)} %get-tuple-element.245), kind=kOutput, calls=%fused_computation.9 | convolution fusion | flops 5376573440 | bytes 12058624 | tf_op jit(solution)/shard_map/dot_general | solution.py:41
  264.9 7.9 %pad_maximum_fusion = bf16[2048,1920]{0,1:T(8,128)(2,1)} fusion(bf16[2048,640]{0,1:T(8,128)(2,1)} %convolution_convert_fusion.1, bf16[2048,1280]{0,1:T(8,128)(2,1)} %convolution_convert_fusion), kind=kLoop, calls=%fused_computation.8 | loop fusion | flops 15728640 | bytes 15728640 | tf_op jit(solution)/shard_map/dynamic_update_slice | solution.py:499
  273.1 7.8 %fusion.7 = f32[512,2048]{1,0:T(8,128)} fusion(bf16[2048,1920]{1,0:T(8,128)(2,1)} %all-gather.6.cloned.1.call-done, bf16[1024,1280]{0,1:T(8,128)(2,1)} %pad_maximum_fusion.1), kind=kOutput, calls=%fused_computation.21 | convolution fusion | flops 2684354560 | bytes 10747904 | tf_op jit(solution)/shard_map/dot_general | solution.py:37
  313.1 10.4 %collective-permute-done.24 = bf16[128,2048]{1,0:T(8,128)(2,1)S(1)} collective-permute-done((bf16[128,2048]{1,0:T(8,128)(2,1)S(1)}, bf16[128,2048]{1,0:T(8,128)(2,1)S(1)}, u32[]{:S(2)}, u32[]{:S(2)}) %collective-permute-start.24) | collective-permute-done | bytes 524320 | tf_op jit(solution)/shard_map/ppermute | solution.py:296
  331.5 11.4 %collective-permute-done.28 = bf16[128,2048]{1,0:T(8,128)(2,1)S(1)} collective-permute-done((bf16[128,2048]{1,0:T(8,128)(2,1)S(1)}, bf16[128,2048]{1,0:T(8,128)(2,1)S(1)}, u32[]{:S(2)}, u32[]{:S(2)}) %collective-permute-start.28) | collective-permute-done | bytes 524320 | tf_op jit(solution)/shard_map/ppermute | solution.py:296
  342.9 10.7 %collective-permute-done.29 = bf16[128,2048]{1,0:T(8,128)(2,1)S(1)} collective-permute-done((bf16[128,2048]{1,0:T(8,128)(2,1)S(1)}, bf16[128,2048]{1,0:T(8,128)(2,1)S(1)}, u32[]{:S(2)}, u32[]{:S(2)}) %collective-permute-start.29) | collective-permute-done | bytes 524320 | tf_op jit(solution)/shard_map/ppermute | solution.py:296
  361.1 11.2 %shard_map.256 = (bf16[1024,512]{1,0:T(8,128)(2,1)S(1)}, f32[1024,2]{1,0:T(8,128)S(1)}, f32[2,128]{1,0:T(2,128)S(1)}) custom-call(f32[1024,512]{1,0:T(8,128)S(1)} %fusion.93.proj, f32[1024,2]{1,0:T(8,128)S(1)} %copy-done.3, f32[1024,128]{1,0:T(8,128)S(1)} %get-tuple-element.285.cosine, f32[1024,128]{1,0:T(8,128)S(1)} %get-tuple-element.286.sine, ...), custom_call_target="tpu_custom_call" | custom-call | flops 10000000 | bytes 100000 | tf_op jit(solution)/shard_map/pallas_call | solution.py:196
  390.0 4.3 fusion.111
  399.1 9.3 %collective-permute-done.38 = bf16[128,2048]{1,0:T(8,128)(2,1)S(1)} collective-permute-done((bf16[128,2048]{1,0:T(8,128)(2,1)S(1)}, bf16[128,2048]{1,0:T(8,128)(2,1)S(1)}, u32[]{:S(2)}, u32[]{:S(2)}) %collective-permute-start.38) | collective-permute-done | bytes 524320 | tf_op jit(solution)/shard_map/ppermute | solution.py:296
  410.7 10.1 %collective-permute-done.36 = bf16[128,2048]{1,0:T(8,128)(2,1)S(1)} collective-permute-done((bf16[128,2048]{1,0:T(8,128)(2,1)S(1)}, bf16[128,2048]{1,0:T(8,128)(2,1)S(1)}, u32[]{:S(2)}, u32[]{:S(2)}) %collective-permute-start.36) | collective-permute-done | bytes 524320 | tf_op jit(solution)/shard_map/ppermute | solution.py:296
  437.3 4.3 all-to-all-start.3
  446.8 9.1 %collective-permute-done.32 = bf16[128,2048]{1,0:T(8,128)(2,1)} collective-permute-done((bf16[128,2048]{1,0:T(8,128)(2,1)}, bf16[128,2048]{1,0:T(8,128)(2,1)}, u32[]{:S(2)}, u32[]{:S(2)}) %collective-permute-start.32) | collective-permute-done | bytes 524320 | tf_op jit(solution)/shard_map/ppermute | solution.py:296
  455.9 4.2 fusion.33
  460.2 18.5 %collective-permute-done.45 = f32[290,128]{1,0:T(8,128)S(1)} collective-permute-done((f32[290,128]{1,0:T(8,128)S(1)}, f32[290,128]{1,0:T(8,128)S(1)}, u32[]{:S(2)}, u32[]{:S(2)}) %collective-permute-start.45) | collective-permute-done | bytes 148512 | tf_op jit(solution)/shard_map/ppermute | solution.py:296
  482.5 16.0 %reduce-scatter.3.cloned.1.call-done.part = bf16[512,1152]{1,0:T(8,128)(2,1)} async-done(((bf16[2048,1152]{1,0:T(8,128)(2,1)}), bf16[512,1152]{1,0:T(8,128)(2,1)}) %reduce-scatter.3.cloned.1.call-update) | async-done | bytes 1179664 | tf_op jit(solution)/shard_map/reduce_scatter | solution.py:407
  527.4 13.2 %fusion.101 = (bf16[64,24576]{1,0:T(8,128)(2,1)}, f32[64,24576]{1,0:T(8,128)}, f32[64,24576]{1,0:T(8,128)}, f32[64,24576]{1,0:T(8,128)}) fusion(f32[64,24576]{1,0:T(8,128)} %weights.3, f32[]{:T(128)} %min.3, bf16[64,24576]{1,0:T(8,128)(2,1)S(1)} %bitcast_dynamic-update-slice_fusion, f32[64,24576]{1,0:T(8,128)} %param.18, f32[64,24576]{1,0:T(8,128)} %param.17), kind=kLoop, calls=%fused_computation.265 | loop fusion | flops 25165824 | bytes 44040196 | tf_op jit(solution)/shard_map/convert_element_type | solution.py:104
  (384 shorter events, 222.4 us)
Async XLA Ops:
  14.8 96.4 %all-gather.4.cloned.1.call-start = ((), (), s32[]{:S(2)}) async-start(), calls=%async_computation.7 | async-start | bytes 3932160 | tf_op jit(solution)/shard_map/all_gather | solution.py:436
  28.8 30.2 %all-to-all-start.1 = ((bf16[8,64,1920]{2,1,0:T(8,128)(2,1)}), bf16[8,64,1920]{2,1,0:T(8,128)(2,1)S(1)}, u32[]{:S(2)}, u32[]{:S(2)}) async-start(bf16[8,64,1920]{2,1,0:T(8,128)(2,1)} %shard_map.254), calls=%async_computation.1 | async-start | bytes 3932160 | tf_op jit(solution)/shard_map/all_to_all | solution.py:404
  32.4 200.9 %all-gather.6.cloned.1.call-start = ((), (), s32[]{:S(2)}) async-start(), calls=%async_computation.8 | async-start | bytes 9830400 | tf_op jit(solution)/shard_map/all_gather | solution.py:444
  33.1 25.3 %collective-permute-start.3 = (bf16[18,512]{1,0:T(8,128)(2,1)S(1)}, bf16[18,512]{1,0:T(8,128)(2,1)S(1)}, u32[]{:S(2)}, u32[]{:S(2)}) collective-permute-start(bf16[18,512]{1,0:T(8,128)(2,1)S(1)} %add.373), channel_id=1, source_target_pairs={{0,6},{1,7},{2,4},{3,5},{4,2},{5,3},{6,0},{7,1},{8,14},{9,15},{10,... | collective-permute-start | bytes 55304 | tf_op jit(solution)/shard_map/ppermute | solution.py:296
  35.9 22.4 %collective-permute-start.2 = (bf16[18,512]{1,0:T(8,128)(2,1)S(1)}, bf16[18,512]{1,0:T(8,128)(2,1)S(1)}, u32[]{:S(2)}, u32[]{:S(2)}) collective-permute-start(bf16[18,512]{1,0:T(8,128)(2,1)S(1)} %add.373), channel_id=1, source_target_pairs={{0,4},{1,5},{2,6},{3,7},{4,0},{5,1},{6,2},{7,3},{8,12},{9,13},{10,... | collective-permute-start | bytes 55304 | tf_op jit(solution)/shard_map/ppermute | solution.py:296
  36.5 21.9 %collective-permute-start.1 = (bf16[18,512]{1,0:T(8,128)(2,1)S(1)}, bf16[18,512]{1,0:T(8,128)(2,1)S(1)}, u32[]{:S(2)}, u32[]{:S(2)}) collective-permute-start(bf16[18,512]{1,0:T(8,128)(2,1)S(1)} %add.373), channel_id=1, source_target_pairs={{0,2},{1,3},{2,0},{3,1},{4,6},{5,7},{6,4},{7,5},{8,10},{9,11},{10,... | collective-permute-start | bytes 55304 | tf_op jit(solution)/shard_map/ppermute | solution.py:296
  59.8 25.0 %collective-permute-start.5 = (bf16[128,2048]{1,0:T(8,128)(2,1)S(1)}, bf16[128,2048]{1,0:T(8,128)(2,1)S(1)}, u32[]{:S(2)}, u32[]{:S(2)}) collective-permute-start(bf16[128,2048]{1,0:T(8,128)(2,1)S(1)} %bitcast.149), channel_id=1, source_target_pairs={{0,4},{1,5},{2,6},{3,7},{4,0},{5,1},{6,2},{7,3},{8,12},{9,13},{10,... | collective-permute-start | bytes 1572872 | tf_op jit(solution)/shard_map/ppermute | solution.py:296
  60.5 24.3 %collective-permute-start.6 = (bf16[128,2048]{1,0:T(8,128)(2,1)S(1)}, bf16[128,2048]{1,0:T(8,128)(2,1)S(1)}, u32[]{:S(2)}, u32[]{:S(2)}) collective-permute-start(bf16[128,2048]{1,0:T(8,128)(2,1)S(1)} %bitcast.150), channel_id=1, source_target_pairs={{0,6},{1,7},{2,4},{3,5},{4,2},{5,3},{6,0},{7,1},{8,14},{9,15},{10,... | collective-permute-start | bytes 1572872 | tf_op jit(solution)/shard_map/ppermute | solution.py:296
  86.4 18.9 %collective-permute-start.7 = (bf16[512,2048]{1,0:T(8,128)(2,1)}, bf16[512,2048]{1,0:T(8,128)(2,1)}, u32[]{:S(2)}, u32[]{:S(2)}) collective-permute-start(bf16[512,2048]{1,0:T(8,128)(2,1)} %pad_maximum_fusion.3), channel_id=1, source_target_pairs={{0,1},{1,0},{2,3},{3,2},{4,5},{5,4},{6,7},{7,6},{8,9},{9,8},{10,11... | collective-permute-start | bytes 6291464 | tf_op jit(solution)/shard_map/ppermute | solution.py:296
  98.5 33.2 %all-to-all-start.2 = ((bf16[8,64,384]{2,1,0:T(8,128)(2,1)}), bf16[8,64,384]{2,1,0:T(8,128)(2,1)}, u32[]{:S(2)}, u32[]{:S(2)}) async-start(bf16[8,64,384]{2,1,0:T(8,128)(2,1)} %shard_map.253), calls=%async_computation.2 | async-start | bytes 786432 | tf_op jit(solution)/shard_map/all_to_all | solution.py:404
  102.6 178.3 %all-gather.8.cloned.1.call-start = ((), (), s32[]{:S(2)}) async-start(), calls=%async_computation.9 | async-start | bytes 1966080 | tf_op jit(solution)/shard_map/all_gather | solution.py:477
  111.2 20.4 %collective-permute-start.11 = (bf16[128,2048]{1,0:T(8,128)(2,1)}, bf16[128,2048]{1,0:T(8,128)(2,1)}, u32[]{:S(2)}, u32[]{:S(2)}) collective-permute-start(bf16[128,2048]{1,0:T(8,128)(2,1)} %bitcast.1), channel_id=1, source_target_pairs={{0,2},{1,3},{2,0},{3,1},{4,6},{5,7},{6,4},{7,5},{8,10},{9,11},{10,... | collective-permute-start | bytes 1572872 | tf_op jit(solution)/shard_map/ppermute | solution.py:296
  113.2 25.2 %collective-permute-start.12 = (bf16[128,2048]{1,0:T(8,128)(2,1)}, bf16[128,2048]{1,0:T(8,128)(2,1)}, u32[]{:S(2)}, u32[]{:S(2)}) collective-permute-start(bf16[128,2048]{1,0:T(8,128)(2,1)} %bitcast.1), channel_id=1, source_target_pairs={{0,4},{1,5},{2,6},{3,7},{4,0},{5,1},{6,2},{7,3},{8,12},{9,13},{10,... | collective-permute-start | bytes 1572872 | tf_op jit(solution)/shard_map/ppermute | solution.py:296
  114.6 23.8 %collective-permute-start.13 = (bf16[128,2048]{1,0:T(8,128)(2,1)}, bf16[128,2048]{1,0:T(8,128)(2,1)}, u32[]{:S(2)}, u32[]{:S(2)}) collective-permute-start(bf16[128,2048]{1,0:T(8,128)(2,1)} %bitcast.1), channel_id=1, source_target_pairs={{0,6},{1,7},{2,4},{3,5},{4,2},{5,3},{6,0},{7,1},{8,14},{9,15},{10,... | collective-permute-start | bytes 1572872 | tf_op jit(solution)/shard_map/ppermute | solution.py:296
  149.6 24.3 %collective-permute-start.15 = (bf16[128,2048]{1,0:T(8,128)(2,1)S(1)}, bf16[128,2048]{1,0:T(8,128)(2,1)S(1)}, u32[]{:S(2)}, u32[]{:S(2)}) collective-permute-start(bf16[128,2048]{1,0:T(8,128)(2,1)S(1)} %get-tuple-element.251), channel_id=1, source_target_pairs={{0,6},{1,7},{2,4},{3,5},{4,2},{5,3},{6,0},{7,1},{8,14},{9,15},{10,... | collective-permute-start | bytes 1572872 | tf_op jit(solution)/shard_map/ppermute | solution.py:296
  152.8 53.8 %collective-permute-start.22 = (bf16[512,2048]{1,0:T(8,128)(2,1)S(1)}, bf16[512,2048]{1,0:T(8,128)(2,1)S(1)}, u32[]{:S(2)}, u32[]{:S(2)}) collective-permute-start(bf16[512,2048]{1,0:T(8,128)(2,1)S(1)} %pad_maximum_fusion.4), channel_id=1, source_target_pairs={{0,1},{1,0},{2,3},{3,2},{4,5},{5,4},{6,7},{7,6},{8,9},{9,8},{10,11... | collective-permute-start | bytes 6291464 | tf_op jit(solution)/shard_map/ppermute | solution.py:296
  178.1 22.3 %collective-permute-start.19 = (bf16[128,2048]{1,0:T(8,128)(2,1)S(1)}, bf16[128,2048]{1,0:T(8,128)(2,1)S(1)}, u32[]{:S(2)}, u32[]{:S(2)}) collective-permute-start(bf16[128,2048]{1,0:T(8,128)(2,1)S(1)} %get-tuple-element.242), channel_id=1, source_target_pairs={{0,4},{1,5},{2,6},{3,7},{4,0},{5,1},{6,2},{7,3},{8,12},{9,13},{10,... | collective-permute-start | bytes 1572872 | tf_op jit(solution)/shard_map/ppermute | solution.py:296
  178.9 23.0 %collective-permute-start.20 = (bf16[128,2048]{1,0:T(8,128)(2,1)S(1)}, bf16[128,2048]{1,0:T(8,128)(2,1)S(1)}, u32[]{:S(2)}, u32[]{:S(2)}) collective-permute-start(bf16[128,2048]{1,0:T(8,128)(2,1)S(1)} %get-tuple-element.242), channel_id=1, source_target_pairs={{0,6},{1,7},{2,4},{3,5},{4,2},{5,3},{6,0},{7,1},{8,14},{9,15},{10,... | collective-permute-start | bytes 1572872 | tf_op jit(solution)/shard_map/ppermute | solution.py:296
  233.3 199.9 %reduce-scatter.5.cloned.1.call-start = ((), (), s32[]{:S(2)}) async-start(), calls=%async_computation.11 | async-start | bytes 9830400 | tf_op jit(solution)/shard_map/reduce_scatter | solution.py:407
  272.8 225.7 %reduce-scatter.3.cloned.1.call-start = ((), (), s32[]{:S(2)}) async-start(), calls=%async_computation.10 | async-start | bytes 5898240 | tf_op jit(solution)/shard_map/reduce_scatter | solution.py:407
  296.3 27.5 %collective-permute-start.27 = (bf16[512,2048]{1,0:T(8,128)(2,1)S(1)}, bf16[512,2048]{1,0:T(8,128)(2,1)S(1)}, u32[]{:S(2)}, u32[]{:S(2)}) collective-permute-start(bf16[512,2048]{1,0:T(8,128)(2,1)S(1)} %add_convert_fusion), channel_id=1, source_target_pairs={{0,1},{1,0},{2,3},{3,2},{4,5},{5,4},{6,7},{7,6},{8,9},{9,8},{10,11... | collective-permute-start | bytes 6291464 | tf_op jit(solution)/shard_map/ppermute | solution.py:296
  299.8 23.7 %collective-permute-start.24 = (bf16[128,2048]{1,0:T(8,128)(2,1)S(1)}, bf16[128,2048]{1,0:T(8,128)(2,1)S(1)}, u32[]{:S(2)}, u32[]{:S(2)}) collective-permute-start(bf16[128,2048]{1,0:T(8,128)(2,1)S(1)} %get-tuple-element.260), channel_id=1, source_target_pairs={{0,6},{1,7},{2,4},{3,5},{4,2},{5,3},{6,0},{7,1},{8,14},{9,15},{10,... | collective-permute-start | bytes 1572872 | tf_op jit(solution)/shard_map/ppermute | solution.py:296
  329.5 24.1 %collective-permute-start.29 = (bf16[128,2048]{1,0:T(8,128)(2,1)S(1)}, bf16[128,2048]{1,0:T(8,128)(2,1)S(1)}, u32[]{:S(2)}, u32[]{:S(2)}) collective-permute-start(bf16[128,2048]{1,0:T(8,128)(2,1)S(1)} %get-tuple-element.240), channel_id=1, source_target_pairs={{0,4},{1,5},{2,6},{3,7},{4,0},{5,1},{6,2},{7,3},{8,12},{9,13},{10,... | collective-permute-start | bytes 1572872 | tf_op jit(solution)/shard_map/ppermute | solution.py:296
  331.0 22.7 %collective-permute-start.30 = (bf16[128,2048]{1,0:T(8,128)(2,1)S(1)}, bf16[128,2048]{1,0:T(8,128)(2,1)S(1)}, u32[]{:S(2)}, u32[]{:S(2)}) collective-permute-start(bf16[128,2048]{1,0:T(8,128)(2,1)S(1)} %get-tuple-element.240), channel_id=1, source_target_pairs={{0,6},{1,7},{2,4},{3,5},{4,2},{5,3},{6,0},{7,1},{8,14},{9,15},{10,... | collective-permute-start | bytes 1572872 | tf_op jit(solution)/shard_map/ppermute | solution.py:296
  396.5 24.4 %collective-permute-start.36 = (bf16[128,2048]{1,0:T(8,128)(2,1)S(1)}, bf16[128,2048]{1,0:T(8,128)(2,1)S(1)}, u32[]{:S(2)}, u32[]{:S(2)}) collective-permute-start(bf16[128,2048]{1,0:T(8,128)(2,1)S(1)} %get-tuple-element.248), channel_id=1, source_target_pairs={{0,6},{1,7},{2,4},{3,5},{4,2},{5,3},{6,0},{7,1},{8,14},{9,15},{10,... | collective-permute-start | bytes 1572872 | tf_op jit(solution)/shard_map/ppermute | solution.py:296
  428.0 18.7 %collective-permute-start.34 = (bf16[128,2048]{1,0:T(8,128)(2,1)}, bf16[128,2048]{1,0:T(8,128)(2,1)S(1)}, u32[]{:S(2)}, u32[]{:S(2)}) collective-permute-start(bf16[128,2048]{1,0:T(8,128)(2,1)} %get-tuple-element.258), channel_id=1, source_target_pairs={{0,4},{1,5},{2,6},{3,7},{4,0},{5,1},{6,2},{7,3},{8,12},{9,13},{10,... | collective-permute-start | bytes 1572872 | tf_op jit(solution)/shard_map/ppermute | solution.py:296
  430.0 25.9 %collective-permute-start.32 = (bf16[128,2048]{1,0:T(8,128)(2,1)}, bf16[128,2048]{1,0:T(8,128)(2,1)}, u32[]{:S(2)}, u32[]{:S(2)}) collective-permute-start(bf16[128,2048]{1,0:T(8,128)(2,1)} %get-tuple-element.257), channel_id=1, source_target_pairs={{0,6},{1,7},{2,4},{3,5},{4,2},{5,3},{6,0},{7,1},{8,14},{9,15},{10,... | collective-permute-start | bytes 1572872 | tf_op jit(solution)/shard_map/ppermute | solution.py:296
  437.3 45.2 %all-to-all-start.3 = ((bf16[8,64,1920]{2,1,0:T(8,128)(2,1)}), bf16[8,64,1920]{2,1,0:T(8,128)(2,1)}, u32[]{:S(2)}, u32[]{:S(2)}) async-start(bf16[8,64,1920]{2,1,0:T(8,128)(2,1)} %bitcast.154), calls=%async_computation.5 | async-start | bytes 3932160 | tf_op jit(solution)/shard_map/all_to_all | solution.py:404
  443.3 35.4 %collective-permute-start.45 = (f32[290,128]{1,0:T(8,128)S(1)}, f32[290,128]{1,0:T(8,128)S(1)}, u32[]{:S(2)}, u32[]{:S(2)}) collective-permute-start(f32[290,128]{1,0:T(8,128)S(1)} %fusion.92), channel_id=1, source_target_pairs={{0,6},{1,7},{2,4},{3,5},{4,2},{5,3},{6,0},{7,1},{8,14},{9,15},{10,... | collective-permute-start | bytes 445448 | tf_op jit(solution)/shard_map/ppermute | solution.py:296
  446.1 34.0 %collective-permute-start.44 = (f32[290,128]{1,0:T(8,128)S(1)}, f32[290,128]{1,0:T(8,128)S(1)}, u32[]{:S(2)}, u32[]{:S(2)}) collective-permute-start(f32[290,128]{1,0:T(8,128)S(1)} %fusion.92), channel_id=1, source_target_pairs={{0,4},{1,5},{2,6},{3,7},{4,0},{5,1},{6,2},{7,3},{8,12},{9,13},{10,... | collective-permute-start | bytes 445448 | tf_op jit(solution)/shard_map/ppermute | solution.py:296
  446.6 33.6 %collective-permute-start.43 = (f32[290,128]{1,0:T(8,128)S(1)}, f32[290,128]{1,0:T(8,128)S(1)}, u32[]{:S(2)}, u32[]{:S(2)}) collective-permute-start(f32[290,128]{1,0:T(8,128)S(1)} %fusion.92), channel_id=1, source_target_pairs={{0,2},{1,3},{2,0},{3,1},{4,6},{5,7},{6,4},{7,5},{8,10},{9,11},{10,... | collective-permute-start | bytes 445448 | tf_op jit(solution)/shard_map/ppermute | solution.py:296
  500.0 26.8 %all-to-all-start.4 = ((bf16[8,64,1152]{2,1,0:T(8,128)(2,1)}), bf16[8,64,1152]{2,1,0:T(8,128)(2,1)S(1)}, u32[]{:S(2)}, u32[]{:S(2)}) async-start(bf16[8,64,1152]{2,1,0:T(8,128)(2,1)} %bitcast.22), calls=%async_computation.6 | async-start | bytes 2359296 | tf_op jit(solution)/shard_map/all_to_all | solution.py:404
  (93 other events, 778.1 us)
Sparse Core Ops, SparseCore 0:
  28.4 62.9 all-gather.3
  93.5 139.6 all-gather.5
  234.8 35.3 all-gather.7
  273.0 134.6 reduce-scatter.4
  410.3 88.1 reduce-scatter.2
